TPU v7x, 32 devices: a whole 2x2x4 slice. The times are simulated.
32 devices in a mesh: dp: 8 (over z, y), head: 4 (over x, core).
Axes of the slice: x: 2, y: 2, z: 4, core: 2. Of those that a mesh axis runs over, the one named last changes fastest.
Arguments:
- patches: bfloat16 [18432, 768], P('dp'), may hold values from -6 to 6
- cotangent: bfloat16 [18432, 768], P('dp'), may hold values from -6 to 6
- expert_ids: int32 [18432, 2], P('dp'), may hold values from 0 to 7, as said below
- slot_pos: int32 [18432, 2], P('dp'), may hold values from 0 to 288, as said below
- owners: int32 [4, 96], P('head'), may hold values from 0 to 7, as said below
- tile_master: float32 [768, 8, 768], P(('dp', 'head'))
- tile_first: float32 [768, 8, 768], P(('dp', 'head'))
- tile_second: float32 [768, 8, 768], P(('dp', 'head'))
- expert_up: float32 [8, 768, 3072], P('dp', None, 'head'), may hold values from -0.21875 to 0.21875
- up_first: float32 [8, 768, 3072], P('dp', None, 'head')
- up_second: float32 [8, 768, 3072], P('dp', None, 'head')
- expert_down: float32 [8, 3072, 768], P('dp', 'head'), may hold values from -0.875 to 0.875
- down_first: float32 [8, 3072, 768], P('dp', 'head')
- down_second: float32 [8, 3072, 768], P('dp', 'head')
- router: float32 [8, 768], replicated, may hold values from -0.15625 to 0.15625
- router_first: float32 [8, 768], replicated
- router_second: float32 [8, 768], replicated
- norm_params: float32 [4, 768], replicated
- norm_first: float32 [4, 768], replicated
- norm_second: float32 [4, 768], replicated
Outputs:
- block_out: bfloat16 [18432, 768], P('dp')
- input_grad: float32 [18432, 768], P('dp')
- tile_new: float32 [768, 8, 768], P(('dp', 'head'))
- tile_first_new: float32 [768, 8, 768], P(('dp', 'head'))
- tile_second_new: float32 [768, 8, 768], P(('dp', 'head'))
- tile_copy: bfloat16 [768, 8, 768], P(('dp', 'head'))
- up_new: float32 [8, 768, 3072], P('dp', None, 'head')
- up_first_new: float32 [8, 768, 3072], P('dp', None, 'head')
- up_second_new: float32 [8, 768, 3072], P('dp', None, 'head')
- up_copy: bfloat16 [8, 768, 3072], P('dp', None, 'head')
- down_new: float32 [8, 3072, 768], P('dp', 'head')
- down_first_new: float32 [8, 3072, 768], P('dp', 'head')
- down_second_new: float32 [8, 3072, 768], P('dp', 'head')
- down_copy: bfloat16 [8, 3072, 768], P('dp', 'head')
- router_new: float32 [8, 768], replicated
- router_first_new: float32 [8, 768], replicated
- router_second_new: float32 [8, 768], replicated
- norm_new: float32 [4, 768], replicated
- norm_first_new: float32 [4, 768], replicated
- norm_second_new: float32 [2, 768], replicated
- later_second_new: float32 [2, 768], replicated
Inputs may be any that keep to these rules, and one draw needn't show every extreme that they name: `expert_ids`: A token's two experts differ. `slot_pos`: the value 288 marks a dropped pair. Among the tokens of one dp index (rows s * 2304 to s * 2304 + 2303), the kept pairs that name one expert hold the distinct slots 0 to n - 1 for some n; in each such block some expert has all 288 slots taken. `owners`: row h names, for each of the 96 tiles of head group h, the dp index that owns it; no dp index owns more than 24 tiles of one group, and in every group one dp index owns exactly 24.
All inputs are finite; a program needn't handle non-finite values.
Results may differ from a plain program's by a relative error of at most 0.025.
Values may be sent and summed in bfloat16 or wider, within the bound.
A program may use at most 256 MiB of HBM per device.

v0:
```python
import jax
import jax.numpy as jnp
from jax import lax
from jax.sharding import PartitionSpec as P

HD = 64
PATCH = 576
TILE = 8
STEP = 10


eps_norm = 1e-06
beta_one = 0.9
beta_two = 0.999
adam_eps = 1e-08
rate_attention = 0.12
rate_up = 0.08
rate_down = 0.3
rate_router = 0.05
rate_norm = 0.4
decay_factor = 0.1


def layer_norm(values, gain_row, shift_row):
    average = jnp.mean(values, axis=-1, keepdims=True)
    centred = values - average
    variance = jnp.mean(centred * centred, axis=-1, keepdims=True)
    return centred * lax.rsqrt(variance + eps_norm) * gain_row + shift_row


def smooth_gelu(values):
    return jax.nn.gelu(values, approximate=True)


def adam_update(weight, moment_one, moment_two, gradient, step_rate, weight_decay):
    moment_one = beta_one * moment_one + (1.0 - beta_one) * gradient
    moment_two = beta_two * moment_two + (1.0 - beta_two) * gradient * gradient
    fixed_one = moment_one / (1.0 - beta_one**STEP)
    fixed_two = moment_two / (1.0 - beta_two**STEP)
    weight = weight - step_rate * (
        fixed_one / (jnp.sqrt(fixed_two) + adam_eps) + weight_decay * weight
    )
    return (weight, moment_one, moment_two)


def times_transposed(left_side, right_side):
    return lax.dot_general(
        left_side, right_side, (((1,), (1,)), ((), ())), preferred_element_type=jnp.float32
    )


def transposed_times(left_side, right_side):
    return lax.dot_general(
        left_side, right_side, (((0,), (0,)), ((), ())), preferred_element_type=jnp.float32
    )


def matmul_float(left_side, right_side):
    return jnp.dot(left_side, right_side, preferred_element_type=jnp.float32)


def attention_scores(queries, key_rows):
    return jnp.einsum(
        "iqhd,ikhd->ihqk", queries, key_rows, preferred_element_type=jnp.float32
    ) * HD ** (-0.5)


def expert_front(rows, up_weight):
    activated, gelu_back = jax.vjp(smooth_gelu, matmul_float(rows, up_weight))
    return (activated.astype(jnp.bfloat16), gelu_back)


def body(
    patches,
    cotangent,
    expert_ids,
    slot_pos,
    owners,
    tile_master,
    tile_first,
    tile_second,
    expert_up,
    up_first,
    up_second,
    expert_down,
    down_first,
    down_second,
    router,
    router_first,
    router_second,
    norm_params,
    norm_first,
    norm_second,
):
    tok_rows, model_width = patches.shape
    experts = router.shape[0]
    capacity = tok_rows // experts
    rows_total = experts * capacity
    dp_count = lax.axis_size("dp")
    slot_count = tile_master.shape[0]
    owner_row = owners[0]
    tile_count = owner_row.shape[0]
    head_rows = tile_count * TILE // 4
    local_heads = head_rows // HD
    images = tok_rows // PATCH
    head_shape = (images, PATCH, local_heads, HD)
    order_index = jnp.arange(tile_count, dtype=jnp.int32)
    same_owner = owner_row[:, None] == owner_row[None, :]
    earlier = order_index[None, :] < order_index[:, None]
    tile_rank = jnp.sum(jnp.where(same_owner & earlier, 1, 0), axis=1).astype(jnp.int32)
    tile_place = owner_row * slot_count + tile_rank
    gathered = lax.all_gather(tile_master.astype(jnp.bfloat16), "dp", axis=0, tiled=True)
    tile_rows = jnp.take(gathered, tile_place, axis=0).reshape(4 * head_rows, model_width)
    w_qkv = tile_rows[: 3 * head_rows]
    w_proj = tile_rows[3 * head_rows :]
    inputs = patches.astype(jnp.float32)
    normed_one, norm_one_back = jax.vjp(layer_norm, inputs, norm_params[0], norm_params[1])
    normed_low = normed_one.astype(jnp.bfloat16)
    qkv_low = times_transposed(normed_low, w_qkv).astype(jnp.bfloat16)
    queries = qkv_low[:, :head_rows].reshape(head_shape)
    key_rows = qkv_low[:, head_rows : 2 * head_rows].reshape(head_shape)
    value_rows = qkv_low[:, 2 * head_rows :].reshape(head_shape)
    scores = attention_scores(queries, key_rows)
    top_score = jnp.max(scores, axis=-1, keepdims=True)
    log_total = top_score + jnp.log(jnp.sum(jnp.exp(scores - top_score), axis=-1, keepdims=True))
    weights_low = jnp.exp(scores - log_total).astype(jnp.bfloat16)
    attended = jnp.einsum(
        "ihqk,ikhd->iqhd", weights_low, value_rows, preferred_element_type=jnp.float32
    )
    mixed_low = attended.reshape(tok_rows, head_rows).astype(jnp.bfloat16)
    attn_total = lax.psum(matmul_float(mixed_low, w_proj), "head")
    residual_one = inputs + attn_total
    normed_two, norm_two_back = jax.vjp(layer_norm, residual_one, norm_params[2], norm_params[3])
    normed_two_low = normed_two.astype(jnp.bfloat16)
    router_low = router.astype(jnp.bfloat16)
    gate_probs = jax.nn.softmax(times_transposed(normed_two_low, router_low), axis=-1)
    gate_pair = jnp.take_along_axis(gate_probs, expert_ids, axis=1)
    kept_pair = slot_pos < capacity
    flat_slot = jnp.where(kept_pair, expert_ids * capacity + slot_pos, rows_total).reshape(-1)
    token_index = jnp.repeat(jnp.arange(tok_rows, dtype=jnp.int32), 2)
    token_of = jnp.zeros((rows_total,), jnp.int32).at[flat_slot].set(token_index, mode="drop")
    slot_used = jnp.zeros((rows_total,), jnp.int32).at[flat_slot].set(1, mode="drop") > 0
    gate_of = (
        jnp.zeros((rows_total,), jnp.float32).at[flat_slot].set(gate_pair.reshape(-1), mode="drop")
    )
    send_rows = jnp.where(
        slot_used[:, None], jnp.take(normed_two_low, token_of, axis=0), jnp.zeros((), jnp.bfloat16)
    )
    send_rows = send_rows.reshape(experts, capacity, model_width)
    up_low = expert_up[0].astype(jnp.bfloat16)
    down_low = expert_down[0].astype(jnp.bfloat16)
    up_use, down_use = (up_low, down_low)
    received = lax.all_to_all(send_rows, "dp", split_axis=0, concat_axis=0, tiled=True)
    part_slots = received.shape[1]
    expert_rows = received.reshape(dp_count * part_slots, model_width)
    act_low, gelu_back = expert_front(expert_rows, up_use)
    out_partial = matmul_float(act_low, down_use)
    expert_total = lax.psum(out_partial.astype(jnp.bfloat16), "head")
    returned = lax.all_to_all(
        expert_total.reshape(dp_count, part_slots, model_width),
        "dp",
        split_axis=0,
        concat_axis=0,
        tiled=True,
    )
    gather_slot = jnp.minimum(flat_slot, rows_total - 1).reshape(tok_rows, 2)
    picked = jnp.take(returned.reshape(rows_total, model_width), gather_slot, axis=0).astype(
        jnp.float32
    )
    picked = jnp.where(kept_pair[:, :, None], picked, 0.0)
    expert_mix = jnp.sum(gate_pair[:, :, None] * picked, axis=1)
    block_out = (residual_one + expert_mix).astype(jnp.bfloat16)
    upstream = cotangent.astype(jnp.float32)
    gate_grad = jnp.sum(upstream[:, None, :] * picked, axis=-1)
    slot_grad = jnp.where(
        slot_used[:, None], jnp.take(upstream, token_of, axis=0) * gate_of[:, None], 0.0
    )
    slot_grad = slot_grad.astype(jnp.bfloat16).reshape(experts, capacity, model_width)
    back_rows = lax.all_to_all(slot_grad, "dp", split_axis=0, concat_axis=0, tiled=True)
    back_rows = back_rows.reshape(dp_count * part_slots, model_width)
    rows_again, up_again, back_rows = lax.optimization_barrier((expert_rows, up_use, back_rows))
    kept_act, kept_back = expert_front(rows_again, up_again)
    down_grad = transposed_times(kept_act, back_rows)
    hidden_grad = kept_back(times_transposed(back_rows, down_use))[0].astype(jnp.bfloat16)
    up_grad = transposed_times(expert_rows, hidden_grad)
    row_partial = times_transposed(hidden_grad, up_use)
    row_grad = lax.psum(row_partial.astype(jnp.bfloat16), "head")
    sent_grad = lax.all_to_all(
        row_grad.reshape(dp_count, part_slots, model_width),
        "dp",
        split_axis=0,
        concat_axis=0,
        tiled=True,
    )
    pair_grad = jnp.take(sent_grad.reshape(rows_total, model_width), gather_slot, axis=0).astype(
        jnp.float32
    )
    dispatch_grad = jnp.sum(jnp.where(kept_pair[:, :, None], pair_grad, 0.0), axis=1)
    expert_match = expert_ids[:, :, None] == jnp.arange(experts, dtype=jnp.int32)[None, None, :]
    prob_grad = jnp.sum(jnp.where(expert_match, gate_grad[:, :, None], 0.0), axis=1)
    logit_grad = (
        gate_probs * (prob_grad - jnp.sum(gate_probs * prob_grad, axis=-1, keepdims=True))
    ).astype(jnp.bfloat16)
    router_grad = transposed_times(logit_grad, normed_two_low)
    normed_two_grad = dispatch_grad + matmul_float(logit_grad, router_low)
    residual_back, gain_two_grad, shift_two_grad = norm_two_back(normed_two_grad)
    residual_grad = upstream + residual_back
    residual_low = residual_grad.astype(jnp.bfloat16)
    proj_grad = transposed_times(mixed_low, residual_low)
    mixed_grad = times_transposed(residual_low, w_proj).astype(jnp.bfloat16).reshape(head_shape)
    weights_full = jnp.exp(attention_scores(queries, key_rows) - log_total)
    weights_again = weights_full.astype(jnp.bfloat16)
    prob_back = jnp.einsum(
        "iqhd,ikhd->ihqk", mixed_grad, value_rows, preferred_element_type=jnp.float32
    )
    score_grad = (
        weights_full * (prob_back - jnp.sum(weights_full * prob_back, axis=-1, keepdims=True))
    ).astype(jnp.bfloat16)
    query_grad = jnp.einsum(
        "ihqk,ikhd->iqhd", score_grad, key_rows, preferred_element_type=jnp.float32
    ) * HD ** (-0.5)
    key_grad = jnp.einsum(
        "ihqk,iqhd->ikhd", score_grad, queries, preferred_element_type=jnp.float32
    ) * HD ** (-0.5)
    value_grad = jnp.einsum(
        "ihqk,iqhd->ikhd", weights_again, mixed_grad, preferred_element_type=jnp.float32
    )
    qkv_grad = jnp.concatenate(
        [
            query_grad.reshape(tok_rows, head_rows),
            key_grad.reshape(tok_rows, head_rows),
            value_grad.reshape(tok_rows, head_rows),
        ],
        axis=1,
    ).astype(jnp.bfloat16)
    qkv_weight_grad = transposed_times(qkv_grad, normed_low)
    normed_one_grad = lax.psum(matmul_float(qkv_grad, w_qkv).astype(jnp.bfloat16), "head").astype(
        jnp.float32
    )
    input_back, gain_one_grad, shift_one_grad = norm_one_back(normed_one_grad)
    input_grad = residual_grad + input_back
    tile_grad = jnp.concatenate([qkv_weight_grad, proj_grad], axis=0).reshape(
        tile_count, TILE, model_width
    )
    padded = (
        jnp.zeros((dp_count * slot_count, TILE, model_width), jnp.float32)
        .at[tile_place]
        .set(tile_grad)
    )
    owned_grad = lax.psum_scatter(
        padded.astype(jnp.bfloat16), "dp", scatter_dimension=0, tiled=True
    ).astype(jnp.float32)
    norm_grad = jnp.stack([gain_one_grad, shift_one_grad, gain_two_grad, shift_two_grad])
    router_total, norm_total = (
        lax.psum(router_grad.astype(jnp.bfloat16), "dp").astype(jnp.float32),
        lax.psum(norm_grad.astype(jnp.bfloat16), "dp").astype(jnp.float32),
    )
    tile_new, tile_first_new, tile_second_new = adam_update(
        tile_master, tile_first, tile_second, owned_grad, rate_attention, decay_factor
    )
    up_new, up_first_new, up_second_new = adam_update(
        expert_up, up_first, up_second, up_grad[None], rate_up, decay_factor
    )
    down_new, down_first_new, down_second_new = adam_update(
        expert_down, down_first, down_second, down_grad[None], rate_down, decay_factor
    )
    router_new, router_first_new, router_second_new = adam_update(
        router, router_first, router_second, router_total, rate_router, decay_factor
    )
    norm_new, norm_first_new, norm_second_all = adam_update(
        norm_params, norm_first, norm_second, norm_total, rate_norm, 0.0
    )
    return (
        block_out,
        input_grad,
        tile_new,
        tile_first_new,
        tile_second_new,
        tile_new.astype(jnp.bfloat16),
        up_new,
        up_first_new,
        up_second_new,
        up_new.astype(jnp.bfloat16),
        down_new,
        down_first_new,
        down_second_new,
        down_new.astype(jnp.bfloat16),
        router_new,
        router_first_new,
        router_second_new,
        norm_new,
        norm_first_new,
        norm_second_all[:2],
        norm_second_all[2:],
    )


def solution(mesh):
    in_specs = (
        P("dp", None),
        P("dp", None),
        P("dp", None),
        P("dp", None),
        P("head", None),
        P(("dp", "head"), None, None),
        P(("dp", "head"), None, None),
        P(("dp", "head"), None, None),
        P("dp", None, "head"),
        P("dp", None, "head"),
        P("dp", None, "head"),
        P("dp", "head", None),
        P("dp", "head", None),
        P("dp", "head", None),
        P(),
        P(),
        P(),
        P(),
        P(),
        P(),
    )
    out_specs = (
        P("dp", None),
        P("dp", None),
        P(("dp", "head"), None, None),
        P(("dp", "head"), None, None),
        P(("dp", "head"), None, None),
        P(("dp", "head"), None, None),
        P("dp", None, "head"),
        P("dp", None, "head"),
        P("dp", None, "head"),
        P("dp", None, "head"),
        P("dp", "head", None),
        P("dp", "head", None),
        P("dp", "head", None),
        P("dp", "head", None),
        P(),
        P(),
        P(),
        P(),
        P(),
        P(),
        P(),
    )
    return jax.shard_map(body, mesh=mesh, in_specs=in_specs, out_specs=out_specs, check_vma=False)
```

profile of v0, /device:TPU:0, one launch (start us, length us, event | category | flops | bytes accessed | tf_op | source)
XLA Modules:
  0.0 1132.4 jit_solution(13690719689477783034)
XLA Ops:
  19.1 46.5 %all-gather.2.cloned.1.call-done = bf16[192,8,768]{2,1,0:T(8,128)(2,1)} async-done(((bf16[24,8,768]{2,1,0:T(8,128)(2,1)}), bf16[192,8,768]{2,1,0:T(8,128)(2,1)}) %all-gather.2.cloned.1.call-update) | async-done | bytes 2359312 | tf_op jit(solution)/shard_map/all_gather | solution.py:112
  80.2 8.0 multiply_reduce_fusion.1
  88.2 9.1 exponential_reduce_fusion
  98.5 9.6 fusion.43
  124.7 17.4 %scatter_custom_fusion.1 = s32[2304]{0:T(1024)S(1)} fusion(s32[4608]{0:T(1024)S(1)} %fusion.72, s32[4608]{0:T(1024)S(1)} %reshape.393, s32[]{:T(128)} %constant.52.clone.1), kind=kCustom, calls=%fused_computation.176 | custom fusion | bytes 9220 | tf_op jit(solution)/shard_map/scatter | solution.py:141
  142.8 17.4 %scatter_custom_fusion = s32[2304]{0:T(1024)S(1)} fusion(s32[4608]{0:T(1024)S(1)} %fusion.72, s32[4608]{0:T(1024)S(1)} %broadcast.272, s32[]{:T(128)} %constant.52.clone.1), kind=kCustom, calls=%fused_computation.179 | custom fusion | bytes 9220 | tf_op jit(solution)/shard_map/scatter | solution.py:142
  160.9 12.5 %gather_fusion.2 = f32[2304,768]{1,0:T(8,128)} fusion(f32[2304,768]{1,0:T(8,128)} %convert_element_type.139, s32[3072]{0:T(1024)S(1)} %pad_clamp_fusion.1), kind=kCustom, calls=%fused_computation.4 | custom fusion | bytes 14164992 | tf_op jit(solution)/shard_map/jit(_take)/gather | solution.py:176
  173.5 72.5 %all-reduce.6.cloned.1.call-done = f32[2304,768]{1,0:T(8,128)} async-done(((f32[2304,768]{1,0:T(8,128)}), f32[2304,768]{1,0:T(8,128)}) %all-reduce.6.cloned.1.call-update) | async-done | bytes 7077904 | tf_op jit(solution)/shard_map/psum | solution.py:131
  256.4 27.0 %gather_fusion.3 = f32[4608]{0:T(1024)S(1)} fusion(f32[2304,8]{0,1:T(8,128)S(1)} %fusion.67, s32[4608]{0:T(1024)S(1)} %reshape.375), kind=kCustom, calls=%fused_computation.5 | custom fusion | bytes 73728 | tf_op jit(solution)/shard_map/jit(take_along_axis)/gather | solution.py:137
  286.0 17.5 %scatter_custom_fusion.2 = f32[2304]{0:T(1024)S(1)} fusion(s32[4608]{0:T(1024)} %copy-done.66, f32[4608]{0:T(1024)S(1)} %reshape.401, f32[]{:T(128)} %constant.47.clone.1), kind=kCustom, calls=%fused_computation.174 | custom fusion | bytes 9728 | tf_op jit(solution)/shard_map/scatter | solution.py:144
  316.5 7.8 gather_fusion.1
  328.1 67.3 %all-to-all-done.2 = bf16[8,288,768]{2,1,0:T(8,128)(2,1)} async-done(((bf16[8,288,768]{2,1,0:T(8,128)(2,1)}), bf16[8,288,768]{2,1,0:T(8,128)(2,1)}, u32[]{:S(2)}, u32[]{:S(2)}) %all-to-all-start.2) | async-done | bytes 3538976 | tf_op jit(solution)/shard_map/all_to_all | solution.py:179
  402.0 76.4 %all-to-all-done = bf16[8,288,768]{2,1,0:T(8,128)(2,1)S(1)} async-done(((bf16[8,288,768]{2,1,0:T(8,128)(2,1)}), bf16[8,288,768]{2,1,0:T(8,128)(2,1)S(1)}, u32[]{:S(2)}, u32[]{:S(2)}) %all-to-all-start) | async-done | bytes 3538976 | tf_op jit(solution)/shard_map/all_to_all | solution.py:153
  478.4 11.2 convolution_convert_fusion.1
  494.1 9.5 fusion.16
  508.2 131.5 %all-reduce.10.cloned.1.call-done = (bf16[8,288,768]{2,1,0:T(8,128)(2,1)}, bf16[8,288,768]{2,1,0:T(8,128)(2,1)}) async-done(((bf16[8,288,768]{2,1,0:T(8,128)(2,1)}, bf16[8,288,768]{2,1,0:T(8,128)(2,1)}), (bf16[8,288,768]{2,1,0:T(8,128)(2,1)}, bf16[8,288,768]{2,1,0:T(8,128)(2,1)})) %all-reduce.10.cloned.1.call-update) | async-done | bytes 7077904 | tf_op jit(solution)/shard_map/psum | solution.py:158
  639.7 85.0 %all_to_all.20 = bf16[8,288,768]{2,1,0:T(8,128)(2,1)} all-to-all(bf16[8,288,768]{2,1,0:T(8,128)(2,1)} %get-tuple-element.43), channel_id=1, replica_groups=mesh['dp'=8,'head'=4] {'dp'}, dimensions={0} | all-to-all | bytes 7077888 | tf_op jit(solution)/shard_map/all_to_all | solution.py:188
  737.7 20.1 %gather_fusion.5 = bf16[4608,768]{1,0:T(8,128)(2,1)} fusion(bf16[2304,768]{1,0:T(8,128)(2,1)} %bitcast.102, s32[5120]{0:T(1024)} %pad_clamp_fusion), kind=kCustom, calls=%fused_computation.1.clone | custom fusion | bytes 14174208 | tf_op jit(solution)/shard_map/jit(_take)/gather | solution.py:195
  757.8 14.7 %reshape.431 = bf16[2304,2,768]{2,1,0:T(2,128)(2,1)} reshape(bf16[4608,768]{1,0:T(8,128)(2,1)} %gather_fusion.5) | data formatting | bytes 14155776 | tf_op jit(solution)/shard_map/jit(_take)/gather | solution.py:195
  772.5 34.2 %all-to-all-done.1 = bf16[8,288,768]{2,1,0:T(8,128)(2,1)S(1)} async-done(((bf16[8,288,768]{2,1,0:T(8,128)(2,1)}), bf16[8,288,768]{2,1,0:T(8,128)(2,1)S(1)}, u32[]{:S(2)}, u32[]{:S(2)}) %all-to-all-start.1) | async-done | bytes 3538976 | tf_op jit(solution)/shard_map/all_to_all | solution.py:159
  806.7 14.5 %gather_fusion.4 = bf16[4608,768]{1,0:T(8,128)(2,1)} fusion(bf16[2304,768]{1,0:T(8,128)(2,1)S(1)} %bitcast.101, s32[5120]{0:T(1024)} %pad_clamp_fusion), kind=kCustom, calls=%fused_computation.clone | custom fusion | bytes 14174208 | tf_op jit(solution)/shard_map/jit(_take)/gather | solution.py:167
  821.2 14.8 %reshape.427 = bf16[2304,2,768]{2,1,0:T(2,128)(2,1)} reshape(bf16[4608,768]{1,0:T(8,128)(2,1)} %gather_fusion.4) | data formatting | bytes 14155776 | tf_op jit(solution)/shard_map/jit(_take)/gather | solution.py:167
  836.1 63.7 %multiply_reduce_fusion.2 = (f32[2304,2]{1,0:T(8,128)S(1)}, f32[2304,768]{1,0:T(8,128)}, f32[2304,768]{1,0:T(8,128)}) fusion(pred[2304,2]{1,0:T(8,128)(4,1)S(1)} %copy-done.27, f32[2304,768]{1,0:T(8,128)} %convert_element_type.139, bf16[2304,2,768]{2,1,0:T(2,128)(2,1)} %reshape.427, pred[2304,2]{1,0:T(8,128)(4,1)S(1)} %copy-done.28, ...), kind=kLoop, calls=%fused_computation.15 | loop fusion | flops 35384832 | bytes 35435520 | tf_op jit(solution)/shard_map/reduce_sum | solution.py:174
  922.4 9.3 fusion.44
  931.7 11.7 %multiply_reduce_fusion = (f32[4,3,576]{2,1,0:T(4,128)S(1)}, f32[4,3,576,576]{2,3,1,0:T(8,128)}) fusion(f32[4,3,576,576]{2,3,1,0:T(8,128)} %get-tuple-element.77, f32[4,3,576]{2,1,0:T(4,128)S(1)} %copy-done.26, bf16[4,576,3,64]{1,0,3,2:T(4,128)(2,1)S(1)} %copy-done.11, bf16[4,576,3,64]{1,0,3,2:T(4,128)(2,1)S(1)} %reshape.326), kind=kOutput, calls=%fused_computation.11 | convolution fusion | flops 525526272 | bytes 33675264 | tf_op jit(solution)/shard_map/iqhd,ikhd->ihqk/dot_general | solution.py:213
  943.3 12.7 %multiply_convert_fusion = bf16[4,3,576,576]{2,3,1,0:T(8,128)(2,1)S(1)} fusion(f32[4,3,576,576]{2,3,1,0:T(8,128)} %get-tuple-element.82, f32[4,3,576,576]{2,3,1,0:T(8,128)} %get-tuple-element.77, f32[4,3,576]{2,1,0:T(4,128)S(1)} %get-tuple-element.81, f32[4,3,576]{2,1,0:T(4,128)S(1)} %copy-done.26), kind=kLoop, calls=%fused_computation.10 | loop fusion | flops 19906560 | bytes 39868416 | tf_op jit(solution)/shard_map/convert_element_type | solution.py:218
  975.4 11.6 %fusion.104 = (bf16[1,768,768]{2,1,0:T(8,128)(2,1)}, f32[1,768,768]{2,1,0:T(8,128)}, f32[1,768,768]{2,1,0:T(8,128)}, f32[1,768,768]{2,1,0:T(8,128)}) fusion(f32[1,768,768]{2,1,0:T(8,128)S(1)} %copy-done.74, f32[1,768,768]{2,1,0:T(8,128)} %param.34, f32[1,768,768]{2,1,0:T(8,128)} %param.35, bf16[2304,768]{1,0:T(8,128)(2,1)} %bitcast.15, ...), kind=kOutput, calls=%fused_computation.207 | convolution fusion | flops 2743271424 | bytes 25952256 | tf_op jit(solution)/shard_map/dot_general | solution.py:53
  998.4 14.3 %scatter_fusion = f32[192,8,768]{2,1,0:T(8,128)} fusion(f32[192,8,768]{2,1,0:T(8,128)} %broadcast_in_dim.187, s32[96]{0:T(128)} %copy-done.72, f32[96,8,768]{2,1,0:T(8,128)} %maximum_bitcast_fusion), kind=kCustom, calls=%fused_computation.9 | custom fusion | bytes 7078272 | tf_op jit(solution)/shard_map/scatter | solution.py:248
  1016.8 14.0 %fusion.106 = (bf16[1,768,768]{2,1,0:T(8,128)(2,1)}, f32[1,768,768]{2,1,0:T(8,128)}, f32[1,768,768]{2,1,0:T(8,128)}, f32[1,768,768]{2,1,0:T(8,128)}) fusion(f32[1,768,768]{2,1,0:T(8,128)} %param.30, f32[1,768,768]{2,1,0:T(8,128)} %param.31, f32[1,768,768]{2,1,0:T(8,128)} %param.32, bf16[2304,768]{1,0:T(8,128)(2,1)} %bitcast.109, ...), kind=kOutput, calls=%fused_computation.208 | convolution fusion | flops 2727346176 | bytes 22413312 | tf_op jit(solution)/shard_map/dot_general | solution.py:53
  1033.1 16.2 %all-reduce.8.cloned.1.call-done = bf16[2304,768]{1,0:T(8,128)(2,1)} async-done(((bf16[2304,768]{1,0:T(8,128)(2,1)}), bf16[2304,768]{1,0:T(8,128)(2,1)}) %all-reduce.8.cloned.1.call-update) | async-done | bytes 3538960 | tf_op jit(solution)/shard_map/psum | solution.py:237
  1063.9 38.5 %all-reduce = (bf16[8,768]{1,0:T(8,128)(2,1)}, bf16[4,768]{1,0:T(4,128)(2,1)}) all-reduce(bf16[8,768]{1,0:T(8,128)(2,1)} %convolution_convert_fusion.7, bf16[4,768]{1,0:T(4,128)(2,1)} %pad_maximum_fusion), channel_id=1, replica_groups=mesh['dp'=8,'head'=4] {'dp'}, use_global_device_ids=true, to_apply=%region_28.30 | all-reduce | flops 9216 | bytes 36864 | tf_op jit(solution)/shard_map/psum | solution.py:255
  1106.6 10.3 add_add_fusion.2
  (277 shorter events, 189.8 us)
Async XLA Ops:
  7.2 58.4 %all-gather.2.cloned.1.call-start = ((), (), s32[]{:S(2)}) async-start(), calls=%async_computation.5 | async-start | bytes 2654208 | tf_op jit(solution)/shard_map/all_gather | solution.py:112
  9.2 236.8 %all-reduce.6.cloned.1.call-start = ((), (), s32[]{:S(2)}) async-start(), calls=%async_computation.6 | async-start | bytes 14155776 | tf_op jit(solution)/shard_map/psum | solution.py:131
  13.0 62.0 %copy-start.60 = (f32[768]{0:T(1024)}, f32[768]{0:T(1024)S(1)}, u32[]{:S(2)}) copy-start(f32[768]{0:T(1024)S(1)} %get-tuple-element.38) | copy-start | bytes 9220
  16.7 58.2 %copy-start.36 = (f32[2304]{0:T(1024)}, f32[2304]{0:T(1024)S(1)}, u32[]{:S(2)}) copy-start(f32[2304]{0:T(1024)S(1)} %broadcast_multiply_fusion.1) | copy-start | bytes 27652
  124.7 48.8 %copy-start.66 = (s32[4608]{0:T(1024)}, s32[4608]{0:T(1024)S(1)}, u32[]{:S(2)}) copy-start(s32[4608]{0:T(1024)S(1)} %fusion.72) | copy-start | bytes 55300
  160.9 12.6 %copy-start.51 = (s32[3072]{0:T(1024)}, s32[3072]{0:T(1024)S(1)}, u32[]{:S(2)}) copy-start(s32[3072]{0:T(1024)S(1)} %pad_clamp_fusion.1) | copy-start | bytes 36868
  256.4 28.6 %copy-start.41 = (s32[2304,2]{0,1:T(2,128)S(1)}, s32[2304,2]{0,1:T(2,128)}, u32[]{:S(2)}) copy-start(s32[2304,2]{0,1:T(2,128)} %param.24) | copy-start | bytes 55300
  256.4 47.8 %copy-start.65 = (pred[8,288]{1,0:T(8,128)(4,1)S(1)}, pred[8,288]{1,0:T(8,128)(4,1)}, u32[]{:S(2)}) copy-start(pred[8,288]{1,0:T(8,128)(4,1)} %broadcast_in_dim.172) | copy-start | bytes 6916
  285.4 18.8 %copy-start.14 = (f32[2304,2]{1,0:T(8,128)}, f32[2304,2]{1,0:T(8,128)S(1)}, u32[]{:S(2)}) copy-start(f32[2304,2]{1,0:T(8,128)S(1)} %copy.176) | copy-start | bytes 55300
  310.7 84.7 %all-to-all-start.2 = ((bf16[8,288,768]{2,1,0:T(8,128)(2,1)}), bf16[8,288,768]{2,1,0:T(8,128)(2,1)}, u32[]{:S(2)}, u32[]{:S(2)}) async-start(bf16[8,288,768]{2,1,0:T(8,128)(2,1)} %select_convert_fusion), calls=%async_computation.2 | async-start | bytes 7077888 | tf_op jit(solution)/shard_map/all_to_all | solution.py:179
  395.4 83.0 %all-to-all-start = ((bf16[8,288,768]{2,1,0:T(8,128)(2,1)}), bf16[8,288,768]{2,1,0:T(8,128)(2,1)S(1)}, u32[]{:S(2)}, u32[]{:S(2)}) async-start(bf16[8,288,768]{2,1,0:T(8,128)(2,1)} %select_select_fusion), calls=%async_computation | async-start | bytes 7077888 | tf_op jit(solution)/shard_map/all_to_all | solution.py:153
  399.1 240.6 %all-reduce.10.cloned.1.call-start = ((), (), s32[]{:S(2)}) async-start(), calls=%async_computation.9 | async-start | bytes 14155776 | tf_op jit(solution)/shard_map/psum | solution.py:158
  639.7 95.5 %copy-start.64 = (pred[2304,2]{0,1:T(4,128)(4,1)S(1)}, pred[2304,2]{0,1:T(4,128)(4,1)}, u32[]{:S(2)}) copy-start(pred[2304,2]{0,1:T(4,128)(4,1)} %get-tuple-element.64) | copy-start | bytes 13828
  724.7 82.0 %all-to-all-start.1 = ((bf16[8,288,768]{2,1,0:T(8,128)(2,1)}), bf16[8,288,768]{2,1,0:T(8,128)(2,1)S(1)}, u32[]{:S(2)}, u32[]{:S(2)}) async-start(bf16[8,288,768]{2,1,0:T(8,128)(2,1)} %get-tuple-element.42), calls=%async_computation.1 | async-start | bytes 7077888 | tf_op jit(solution)/shard_map/all_to_all | solution.py:159
  728.4 320.9 %all-reduce.8.cloned.1.call-start = ((), (), s32[]{:S(2)}) async-start(), calls=%async_computation.7 | async-start | bytes 7077888 | tf_op jit(solution)/shard_map/psum | solution.py:237
  821.2 14.8 %copy-start.15 = (f32[2304,2]{1,0:T(8,128)S(1)}, f32[2304,2]{1,0:T(8,128)}, u32[]{:S(2)}) copy-start(f32[2304,2]{1,0:T(8,128)} %copy-done.14) | copy-start | bytes 55300
  821.2 14.8 %copy-start.27 = (pred[2304,2]{1,0:T(8,128)(4,1)S(1)}, pred[2304,2]{1,0:T(8,128)(4,1)}, u32[]{:S(2)}) copy-start(pred[2304,2]{1,0:T(8,128)(4,1)} %copy.177) | copy-start | bytes 13828
  821.2 14.8 %copy-start.28 = (pred[2304,2]{1,0:T(8,128)(4,1)S(1)}, pred[2304,2]{1,0:T(8,128)(4,1)}, u32[]{:S(2)}) copy-start(pred[2304,2]{1,0:T(8,128)(4,1)} %copy.178) | copy-start | bytes 13828
  836.0 64.2 %copy-start.42 = (s32[2304,2]{0,1:T(2,128)S(1)}, s32[2304,2]{0,1:T(2,128)}, u32[]{:S(2)}) copy-start(s32[2304,2]{0,1:T(2,128)} %param.24) | copy-start | bytes 55300
  836.0 64.2 %copy-start.24 = (f32[2304,8]{0,1:T(8,128)S(1)}, f32[2304,8]{0,1:T(8,128)}, u32[]{:S(2)}) copy-start(f32[2304,8]{0,1:T(8,128)} %copy-done.23) | copy-start | bytes 221188
  836.1 64.2 %copy-start.35 = (f32[2304]{0:T(1024)S(1)}, f32[2304]{0:T(1024)}, u32[]{:S(2)}) copy-start(f32[2304]{0:T(1024)} %copy-done.34) | copy-start | bytes 27652
  836.1 64.2 %copy-start.50 = (f32[2304]{0:T(1024)S(1)}, f32[2304]{0:T(1024)}, u32[]{:S(2)}) copy-start(f32[2304]{0:T(1024)} %copy-done.49) | copy-start | bytes 27652
  836.1 64.3 %copy-start.33 = (f32[2304]{0:T(1024)S(1)}, f32[2304]{0:T(1024)}, u32[]{:S(2)}) copy-start(f32[2304]{0:T(1024)} %copy-done.32) | copy-start | bytes 27652
  836.1 64.3 %copy-start.44 = (f32[8,768]{1,0:T(8,128)S(1)}, f32[8,768]{1,0:T(8,128)}, u32[]{:S(2)}) copy-start(f32[8,768]{1,0:T(8,128)} %param.36) | copy-start | bytes 73732
  836.1 64.3 %copy-start.46 = (f32[2304]{0:T(1024)S(1)}, f32[2304]{0:T(1024)}, u32[]{:S(2)}) copy-start(f32[2304]{0:T(1024)} %copy-done.45) | copy-start | bytes 27652
  836.1 64.3 %copy-start.63 = (f32[768]{0:T(1024)S(1)}, f32[768]{0:T(1024)}, u32[]{:S(2)}) copy-start(f32[768]{0:T(1024)} %get-tuple-element.36) | copy-start | bytes 9220
  943.3 12.7 %copy-start.13 = (bf16[4,576,3,64]{1,0,3,2:T(4,128)(2,1)S(1)}, bf16[4,576,3,64]{1,0,3,2:T(4,128)(2,1)}, u32[]{:S(2)}) copy-start(bf16[4,576,3,64]{1,0,3,2:T(4,128)(2,1)} %copy-done.12) | copy-start | bytes 2654212
  975.3 147.0 %reduce-scatter.2.cloned.1.call-start = ((), (), s32[]{:S(2)}) async-start(), calls=%async_computation.8 | async-start | bytes 2654208 | tf_op jit(solution)/shard_map/reduce_scatter | solution.py:250
  1016.7 14.0 %copy-start.70 = (bf16[768]{0:T(1024)(128)(2,1)S(1)}, bf16[768]{0:T(1024)(128)(2,1)}, u32[]{:S(2)}) copy-start(bf16[768]{0:T(1024)(128)(2,1)} %get-tuple-element.28) | copy-start | bytes 4612
  1016.7 14.6 %copy-start.69 = (bf16[768]{0:T(1024)(128)(2,1)S(1)}, bf16[768]{0:T(1024)(128)(2,1)}, u32[]{:S(2)}) copy-start(bf16[768]{0:T(1024)(128)(2,1)} %get-tuple-element.34) | copy-start | bytes 4612
  1016.8 15.2 %copy-start.2 = (bf16[2304,768]{1,0:T(8,128)(2,1)S(1)}, bf16[2304,768]{1,0:T(8,128)(2,1)}, u32[]{:S(2)}) copy-start(bf16[2304,768]{1,0:T(8,128)(2,1)} %copy-done) | copy-start | bytes 10616836
  1016.8 15.1 %copy-start.31 = (bf16[2304,8]{0,1:T(8,128)(2,1)S(1)}, bf16[2304,8]{0,1:T(8,128)(2,1)}, u32[]{:S(2)}) copy-start(bf16[2304,8]{0,1:T(8,128)(2,1)} %copy-done.30) | copy-start | bytes 110596
  (55 other events, 293.4 us)
Sparse Core Ops, SparseCore 0:
  10.8 54.7 all-gather.1
  115.1 130.8 all-reduce.5
  508.3 131.3 all-reduce.9
  975.4 73.8 all-reduce.7
  1052.6 69.5 reduce-scatter.1
where the time goes:
time: 1140 us; the launch traced here: 1130 us
  waiting for transfers between devices  450 us (39%)
  local copies, waits for them, and re-layouts  228 us (20%)
  other arithmetic  169 us (15%)
  matrix products  133 us (12%)
  blocking collectives  124 us (11%)
  between operations  15.6 us (1%)
  starting transfers between devices  13.7 us (1%)
    psum x1, waiting for transfers between devices, body(): expert_total = lax.psum(out_partial.astype(jnp.bfloat16), 'head')  132 us
    all_to_all x1, blocking collectives, body(): lax.all_to_all(row_grad.reshape(dp_count, part_slots, model_width), 'dp',...  85 us
    all_to_all x1, waiting for transfers between devices, body(): lax.all_to_all(send_rows, 'dp', split_axis=0, concat_axis=0, tiled=True)  76.4 us
    psum x1, waiting for transfers between devices, body(): attn_total = lax.psum(matmul_float(mixed_low, w_proj), 'head')  72.5 us
    all_to_all x1, waiting for transfers between devices, body(): lax.all_to_all(slot_grad, 'dp', split_axis=0, concat_axis=0, tiled=True)  67.3 us
    reduce_sum x1, other arithmetic, body(): gate_grad = jnp.sum(upstream[:, None, :] * picked, axis=-1)  63.7 us
    all_gather x1, waiting for transfers between devices, body(): lax.all_gather(tile_master.astype(jnp.bfloat16), 'dp', axis=0, tiled=True)  46.5 us
    psum x1, blocking collectives, body(): lax.psum(router_grad.astype(jnp.bfloat16), 'dp').astype(jnp.float32)  38.5 us
  transfers between devices with their start and end apart: 8, of which 8 were waited for; matrix products, arithmetic and copies ran while one was open for 19% of the time, Pallas kernels for 0%

commit v1 on v0

v1 whole, which is shorter than its diff:
```python
import functools

import jax
import jax.numpy as jnp
from jax import lax
from jax.experimental import pallas as pl
from jax.experimental.pallas import tpu as pltpu
from jax.sharding import PartitionSpec as P

HD = 64
PATCH = 576
TILE = 8
STEP = 10

eps_norm = 1e-06
beta_one = 0.9
beta_two = 0.999
adam_eps = 1e-08
rate_attention = 0.12
rate_up = 0.08
rate_down = 0.3
rate_router = 0.05
rate_norm = 0.4
decay_factor = 0.1

LOW = jnp.bfloat16
FULL = jnp.float32
MESH = pl.DeviceIdType.MESH
VMEM_BYTES = 56 * 1024 * 1024


def adam_update(weight, moment_one, moment_two, gradient, step_rate, weight_decay):
    moment_one = beta_one * moment_one + (1.0 - beta_one) * gradient
    moment_two = beta_two * moment_two + (1.0 - beta_two) * gradient * gradient
    fixed_one = moment_one / (1.0 - beta_one**STEP)
    fixed_two = moment_two / (1.0 - beta_two**STEP)
    weight = weight - step_rate * (
        fixed_one / (jnp.sqrt(fixed_two) + adam_eps) + weight_decay * weight
    )
    return (weight, moment_one, moment_two)


def nn(left, right):
    return lax.dot_general(left, right, (((1,), (0,)), ((), ())), preferred_element_type=FULL)


def nt(left, right):
    return lax.dot_general(left, right, (((1,), (1,)), ((), ())), preferred_element_type=FULL)


def tn(left, right):
    return lax.dot_general(left, right, (((0,), (0,)), ((), ())), preferred_element_type=FULL)


def params(**more):
    return pltpu.CompilerParams(vmem_limit_bytes=VMEM_BYTES, **more)


def whole(shape):
    return pl.BlockSpec(shape, lambda *_: (0,) * len(shape))


def lead(shape):
    return pl.BlockSpec(shape, lambda i: (i,) + (0,) * (len(shape) - 1))


def normalise(values):
    average = jnp.mean(values, axis=-1, keepdims=True)
    centred = values - average
    variance = jnp.mean(centred * centred, axis=-1, keepdims=True)
    scale = lax.rsqrt(variance + eps_norm)
    return centred * scale, scale


def norm_back(normal, scale, gain, upstream):
    inner = upstream * gain
    mean_inner = jnp.mean(inner, axis=-1, keepdims=True)
    mean_cross = jnp.mean(inner * normal, axis=-1, keepdims=True)
    result = scale * (inner - mean_inner - normal * mean_cross)
    gain_sum = jnp.sum(upstream * normal, axis=0, keepdims=True)
    shift_sum = jnp.sum(upstream, axis=0, keepdims=True)
    return result, gain_sum, shift_sum


def one_hot(condition):
    return jnp.where(condition, 1.0, 0.0).astype(LOW)


def head_mask(shape, axis, head):
    return lax.broadcasted_iota(jnp.int32, shape, axis) // HD == head


def attention_front(
    x_ref, norm_ref, held_ref, src_ref,
    w_ref, xn_ref, q_ref, qt_ref, k_ref, kt_ref, v_ref, lse_ref, ot_ref, part_ref,
):
    rows = w_ref.shape[0] // 4
    heads = rows // HD

    @pl.when(pl.program_id(0) == 0)
    def _():
        total = held_ref.shape[0]
        for part in range(4):
            block = pl.ds(part * rows, rows)
            lanes = lax.broadcasted_iota(jnp.int32, (rows, total), 1)
            pick = one_hot(lanes == src_ref[block, :])
            w_ref[block, :] = nn(pick, held_ref[...]).astype(LOW)

    normal, _ = normalise(x_ref[...].astype(FULL))
    xn = (normal * norm_ref[0:1, :] + norm_ref[1:2, :]).astype(LOW)
    xn_ref[...] = xn
    wq, wk, wv = (w_ref[pl.ds(part * rows, rows), :] for part in range(3))
    shrink = HD ** (-0.5)
    q_ref[...] = (nt(xn, wq) * shrink).astype(LOW)
    qt = (nt(wq, xn) * shrink).astype(LOW)
    qt_ref[0] = qt
    k = nt(xn, wk).astype(LOW)
    k_ref[...] = k
    kt_ref[0] = nt(wk, xn).astype(LOW)
    v_ref[...] = nt(xn, wv).astype(LOW)
    vt = nt(wv, xn).astype(LOW)
    mixed = []
    for head in range(heads):
        span = slice(head * HD, (head + 1) * HD)
        only = jnp.where(head_mask(qt.shape, 0, head), qt, jnp.zeros_like(qt))
        scores = nn(k, only)
        top = jnp.max(scores, axis=0, keepdims=True)
        weights = jnp.exp(scores - top)
        total = jnp.sum(weights, axis=0, keepdims=True)
        mixed.append(nn(vt[span], weights.astype(LOW)) / total)
        lse_ref[0, head:head + 1, :] = top + jnp.log(total)
    ot = jnp.concatenate(mixed, axis=0).astype(LOW)
    ot_ref[0] = ot
    part_ref[...] = tn(ot, w_ref[pl.ds(3 * rows, rows), :]).astype(LOW)


def attention_forward(patches, norm_params, held, src_col):
    tokens, width = patches.shape
    images = tokens // PATCH
    all_rows = src_col.shape[0]
    rows = all_rows // 4
    flat = jax.ShapeDtypeStruct((tokens, rows), LOW)
    turned = jax.ShapeDtypeStruct((images, rows, PATCH), LOW)
    wide = jax.ShapeDtypeStruct((tokens, width), LOW)
    flat_spec, turned_spec, wide_spec = (
        lead((PATCH, rows)), lead((1, rows, PATCH)), lead((PATCH, width))
    )
    return pl.pallas_call(
        attention_front,
        grid=(images,),
        in_specs=[wide_spec, whole(norm_params.shape), whole(held.shape), whole(src_col.shape)],
        out_specs=[
            whole((all_rows, width)), wide_spec, flat_spec, turned_spec, flat_spec, turned_spec,
            flat_spec, lead((1, 8, PATCH)), turned_spec, wide_spec,
        ],
        out_shape=[
            jax.ShapeDtypeStruct((all_rows, width), LOW), wide, flat, turned, flat, turned,
            flat, jax.ShapeDtypeStruct((images, 8, PATCH), FULL), turned, wide,
        ],
        compiler_params=params(),
        name="attention_forward",
    )(patches, norm_params, held, src_col)


def attention_rear(
    x1g_ref, w_ref, xn_ref, q_ref, qt_ref, k_ref, kt_ref, v_ref, lse_ref, ot_ref, src_ref,
    part_ref, padded_ref, grad_ref,
):
    rows = w_ref.shape[0] // 4
    heads = rows // HD
    step = pl.program_id(0)
    wq, wk, wv, wo = (w_ref[pl.ds(part * rows, rows), :] for part in range(4))
    x1g, xn = x1g_ref[...], xn_ref[...]
    q, qt, k, kt, v, ot = q_ref[...], qt_ref[0], k_ref[...], kt_ref[0], v_ref[...], ot_ref[0]
    do = nt(x1g, wo).astype(LOW)
    dot = nt(wo, x1g).astype(LOW)
    product = dot.astype(FULL) * ot.astype(FULL)
    shrink = HD ** (-0.5)
    dqt, dk, dv = [], None, None
    for head in range(heads):
        span = slice(head * HD, (head + 1) * HD)
        zero_t = jnp.zeros_like(qt)
        mask_t = head_mask(qt.shape, 0, head)
        mask = head_mask(q.shape, 1, head)
        scores = nn(k, jnp.where(mask_t, qt, zero_t))
        weights = jnp.exp(scores - lse_ref[0, head:head + 1, :])
        back = nn(v, jnp.where(mask_t, dot, zero_t))
        delta = jnp.sum(product[span], axis=0, keepdims=True)
        score_grad = (weights * (back - delta)).astype(LOW)
        dqt.append(nn(kt[span], score_grad) * shrink)
        dk_one = nn(score_grad, jnp.where(mask, q, jnp.zeros_like(q)))
        dv_one = nn(weights.astype(LOW), jnp.where(mask, do, jnp.zeros_like(do)))
        dk = dk_one if dk is None else dk + dk_one
        dv = dv_one if dv is None else dv + dv_one
    dqt = jnp.concatenate(dqt, axis=0).astype(LOW)
    dk, dv = dk.astype(LOW), dv.astype(LOW)
    part_ref[...] = (tn(dqt, wq) + nn(dk, wk) + nn(dv, wv)).astype(LOW)
    pieces = (nn(dqt, xn), tn(dk, xn), tn(dv, xn), nn(ot, x1g))

    @pl.when(step == 0)
    def _():
        for part, piece in enumerate(pieces):
            grad_ref[pl.ds(part * rows, rows), :] = piece

    @pl.when(step > 0)
    def _():
        for part, piece in enumerate(pieces):
            grad_ref[pl.ds(part * rows, rows), :] += piece

    @pl.when(step == pl.num_programs(0) - 1)
    def _():
        low = grad_ref[...].astype(LOW)
        total = padded_ref.shape[0]
        cut = total // 4
        for part in range(4):
            row = lax.broadcasted_iota(jnp.int32, (cut, low.shape[0]), 0) + part * cut
            pick = one_hot(row == src_ref[...])
            padded_ref[pl.ds(part * cut, cut), :] = nn(pick, low).astype(LOW)


def attention_backward(x1_grad, saved, src_row, padded_rows):
    w, xn, q, qt, k, kt, v, lse, ot = saved
    tokens, width = x1_grad.shape
    images = tokens // PATCH
    rows = q.shape[1]
    flat_spec, turned_spec, wide_spec = (
        lead((PATCH, rows)), lead((1, rows, PATCH)), lead((PATCH, width))
    )
    return pl.pallas_call(
        attention_rear,
        grid=(images,),
        in_specs=[
            wide_spec, whole(w.shape), wide_spec, flat_spec, turned_spec, flat_spec, turned_spec,
            flat_spec, lead((1, 8, PATCH)), turned_spec, whole(src_row.shape),
        ],
        out_specs=[wide_spec, whole((padded_rows, width))],
        out_shape=[
            jax.ShapeDtypeStruct((tokens, width), LOW),
            jax.ShapeDtypeStruct((padded_rows, width), LOW),
        ],
        scratch_shapes=[pltpu.VMEM(w.shape, FULL)],
        compiler_params=params(),
        name="attention_backward",
    )(x1_grad, *saved, src_row)


def dispatch_plain(rows_ref, col_ref, out_ref, sum_ref):
    place_rows(rows_ref[...], col_ref, out_ref, sum_ref)


def dispatch_normed(rows_ref, norm_ref, col_ref, out_ref, sum_ref):
    normal, _ = normalise(rows_ref[...].astype(FULL))
    low = (normal * norm_ref[2:3, :] + norm_ref[3:4, :]).astype(LOW)
    place_rows(low, col_ref, out_ref, sum_ref)


def place_rows(rows, col_ref, out_ref, sum_ref):
    step = pl.program_id(0)
    shape = (out_ref.shape[0], rows.shape[0])
    slots = lax.broadcasted_iota(jnp.int32, shape, 0)
    col = col_ref[0]
    pick = one_hot((slots == col[0:1, :]) | (slots == col[1:2, :]))
    part = nn(pick, rows)

    @pl.when(step == 0)
    def _():
        sum_ref[...] = part

    @pl.when(step > 0)
    def _():
        sum_ref[...] += part

    @pl.when(step == pl.num_programs(0) - 1)
    def _():
        out_ref[...] = sum_ref[...].astype(LOW)


def dispatch(rows, norm_params, col_rows, slots):
    width = rows.shape[1]
    wide_spec = lead((PATCH, width))
    operands, specs, kernel = [rows], [wide_spec], dispatch_plain
    if norm_params is not None:
        operands, specs, kernel = (
            [rows, norm_params], [wide_spec, whole(norm_params.shape)], dispatch_normed
        )
    return pl.pallas_call(
        kernel,
        grid=(rows.shape[0] // PATCH,),
        in_specs=specs + [lead((1,) + col_rows.shape[1:])],
        out_specs=whole((slots, width)),
        out_shape=jax.ShapeDtypeStruct((slots, width), LOW),
        scratch_shapes=[pltpu.VMEM((slots, width), FULL)],
        compiler_params=params(),
        name="dispatch_rows",
    )(*operands, col_rows)


def picked_rows(col_ref, held_ref):
    tokens = col_ref.shape[0]
    slots, width = held_ref.shape
    cut = slots // 4
    total = jnp.zeros((tokens, width), FULL)
    for part in range(4):
        lanes = lax.broadcasted_iota(jnp.int32, (tokens, cut), 1) + part * cut
        pick = one_hot((lanes == col_ref[:, 0:1]) | (lanes == col_ref[:, 1:2]))
        total = total + nn(pick, held_ref[pl.ds(part * cut, cut), :])
    return total


def combine_front(col_ref, held_ref, x1_ref, out_ref):
    mix = picked_rows(col_ref, held_ref)
    out_ref[...] = (x1_ref[...].astype(FULL) + mix).astype(LOW)


def combine_rear(col_ref, held_ref, x1_ref, g_ref, norm_ref, out_ref, sums_ref):
    step = pl.program_id(0)
    upstream = picked_rows(col_ref, held_ref)
    normal, scale = normalise(x1_ref[...].astype(FULL))
    back, gain_sum, shift_sum = norm_back(normal, scale, norm_ref[2:3, :], upstream)
    out_ref[...] = (g_ref[...].astype(FULL) + back).astype(LOW)

    @pl.when(step == 0)
    def _():
        sums_ref[...] = jnp.zeros_like(sums_ref)

    sums_ref[0:1, :] += gain_sum
    sums_ref[1:2, :] += shift_sum


def combine_forward(col, held, x1):
    tokens, width = x1.shape
    wide_spec = lead((PATCH, width))
    return pl.pallas_call(
        combine_front,
        grid=(tokens // PATCH,),
        in_specs=[lead((PATCH, 2)), whole(held.shape), wide_spec],
        out_specs=wide_spec,
        out_shape=jax.ShapeDtypeStruct((tokens, width), LOW),
        compiler_params=params(),
        name="combine_forward",
    )(col, held, x1)


def combine_backward(col, held, x1, cotangent, norm_params):
    tokens, width = x1.shape
    wide_spec = lead((PATCH, width))
    return pl.pallas_call(
        combine_rear,
        grid=(tokens // PATCH,),
        in_specs=[
            lead((PATCH, 2)), whole(held.shape), wide_spec, wide_spec, whole(norm_params.shape)
        ],
        out_specs=[wide_spec, whole((8, width))],
        out_shape=[
            jax.ShapeDtypeStruct((tokens, width), LOW), jax.ShapeDtypeStruct((8, width), FULL)
        ],
        compiler_params=params(),
        name="combine_backward",
    )(col, held, x1, cotangent, norm_params)


def expert_kernel(
    rows_ref, g_ref, up_ref, down_ref, router_ref, own_ref, count_ref,
    back_ref, out_ref, upg_ref, downg_ref, router_grad_ref,
    out_sum, back_sum, og_ref, gate_ref, probs_ref,
):
    step = pl.program_id(0)
    rows = rows_ref[...]

    @pl.when(step == 0)
    def _():
        logits = nt(rows, router_ref[...]) + count_ref[...]
        top = jnp.max(logits, axis=-1, keepdims=True)
        weights = jnp.exp(logits - top)
        probs = weights / jnp.sum(weights, axis=-1, keepdims=True)
        gate = jnp.sum(probs * own_ref[...], axis=-1, keepdims=True)
        probs_ref[...] = probs
        gate_ref[...] = gate
        og_ref[...] = (gate * g_ref[...].astype(FULL)).astype(LOW)
        out_sum[...] = jnp.zeros_like(out_sum)
        back_sum[...] = jnp.zeros_like(back_sum)

    og = og_ref[...]
    up, down = up_ref[0], down_ref[0]
    hidden = nn(rows, up)
    slope = (2.0 / jnp.pi) ** 0.5
    square = hidden * hidden
    bend = jnp.tanh(slope * (hidden + 0.044715 * (square * hidden)))
    act = (0.5 * hidden * (1.0 + bend)).astype(LOW)
    out_sum[...] += nn(act, down)
    act_grad = nt(og, down)
    inner = slope * (1.0 + (3.0 * 0.044715) * square)
    curve = 0.5 * (1.0 + bend) + 0.5 * hidden * (1.0 - bend * bend) * inner
    hidden_grad = (curve * act_grad).astype(LOW)
    back_sum[...] += nt(hidden_grad, up)
    upg_ref[0] = tn(rows, hidden_grad).astype(LOW)
    downg_ref[0] = tn(act, og).astype(LOW)

    @pl.when(step == pl.num_programs(0) - 1)
    def _():
        out = out_sum[...].astype(LOW).astype(FULL)
        gate, probs = gate_ref[...], probs_ref[...]
        out_ref[...] = (gate * out).astype(LOW)
        gate_grad = jnp.sum(g_ref[...].astype(FULL) * out, axis=-1, keepdims=True)
        logit_grad = (gate_grad * (probs * (own_ref[...] - gate))).astype(LOW)
        back = back_sum[...].astype(LOW).astype(FULL) + nn(logit_grad, router_ref[...])
        back_ref[...] = back.astype(LOW)
        router_grad_ref[...] = tn(logit_grad, rows)


def experts_both_ways(rows, g_rows, up, down, router_low, own):
    slots, width = rows.shape
    parts, _, units = up.shape
    experts = router_low.shape[0]
    lanes = 128
    router_wide = jnp.zeros((lanes, width), LOW).at[:experts].set(router_low)
    lane = jnp.arange(lanes, dtype=jnp.int32)[None, :]
    own_row = jnp.where(lane == own, 1.0, 0.0).astype(FULL)
    closed = jnp.where(lane < experts, 0.0, -1e30).astype(FULL)
    wide_spec = whole((slots, width))
    return pl.pallas_call(
        expert_kernel,
        grid=(parts,),
        in_specs=[
            wide_spec, wide_spec, lead((1, width, units)), lead((1, units, width)),
            whole((lanes, width)), whole((1, lanes)), whole((1, lanes)),
        ],
        out_specs=[
            wide_spec, wide_spec, lead((1, width, units)), lead((1, units, width)),
            whole((lanes, width)),
        ],
        out_shape=[
            jax.ShapeDtypeStruct((slots, width), LOW),
            jax.ShapeDtypeStruct((slots, width), LOW),
            jax.ShapeDtypeStruct(up.shape, LOW),
            jax.ShapeDtypeStruct(down.shape, LOW),
            jax.ShapeDtypeStruct((lanes, width), FULL),
        ],
        scratch_shapes=[
            pltpu.VMEM((slots, width), FULL), pltpu.VMEM((slots, width), FULL),
            pltpu.VMEM((slots, width), LOW), pltpu.VMEM((slots, 1), FULL),
            pltpu.VMEM((slots, lanes), FULL),
        ],
        compiler_params=params(),
        name="experts_both_ways",
    )(rows, g_rows, up, down, router_wide, own_row, closed)


def partners():
    me = lax.axis_index("head")
    near = me + 1 - 2 * lax.rem(me, 2)
    far = lax.rem(me + 2, 4)
    corner = near + 2 - 4 * (near // 2)
    return me, near, far, corner


def greet(near, far):
    barrier = pltpu.get_barrier_semaphore()
    for other in (near, far):
        pl.semaphore_signal(barrier, inc=1, device_id={"head": other}, device_id_type=MESH)
    pl.semaphore_wait(barrier, 2)


def gather_kernel(cuts, x_ref, out_ref, local_sem, send_sem, recv_sem):
    me, near, far, corner = partners()
    greet(near, far)
    size = x_ref.shape[0] // cuts

    def remote(src, dst, lane, index, other):
        return pltpu.make_async_remote_copy(
            src_ref=src, dst_ref=dst, send_sem=send_sem.at[lane, index],
            recv_sem=recv_sem.at[lane, index], device_id={"head": other}, device_id_type=MESH,
        )

    local = pltpu.make_async_copy(x_ref, out_ref.at[me], local_sem)
    local.start()
    across, beside, onward = [], [], []
    for cut in range(cuts):
        span = pl.ds(cut * size, size)
        across.append(remote(x_ref.at[span], out_ref.at[me, span], 0, cut, far))
        across[-1].start()
    for cut in range(cuts):
        span = pl.ds(cut * size, size)
        beside.append(remote(x_ref.at[span], out_ref.at[me, span], 1, cut, near))
        beside[-1].start()
    for cut in range(cuts):
        span = pl.ds(cut * size, size)
        across[cut].wait_recv()
        onward.append(remote(out_ref.at[far, span], out_ref.at[far, span], 2, cut, near))
        onward[-1].start()
    for cut in range(cuts):
        across[cut].wait_send()
        beside[cut].wait()
        onward[cut].wait()
    local.wait()


def head_gather(x, collective_id, cuts=4):
    return pl.pallas_call(
        functools.partial(gather_kernel, cuts),
        in_specs=[pl.BlockSpec(memory_space=pl.ANY)],
        out_specs=pl.BlockSpec(memory_space=pl.ANY),
        out_shape=jax.ShapeDtypeStruct((4,) + x.shape, x.dtype),
        scratch_shapes=[
            pltpu.SemaphoreType.DMA, pltpu.SemaphoreType.DMA((3, cuts)),
            pltpu.SemaphoreType.DMA((3, cuts)),
        ],
        compiler_params=params(collective_id=collective_id, has_side_effects=True),
        name="head_gather",
    )(x)


def scatter_kernel(
    cuts, x_ref, out_ref, mine, passed, corner_in, near_in, far_in,
    local_sem, send_sem, recv_sem,
):
    me, near, far, corner = partners()
    greet(near, far)
    size = out_ref.shape[0] // cuts

    def remote(src, dst, lane, index, other):
        return pltpu.make_async_remote_copy(
            src_ref=src, dst_ref=dst, send_sem=send_sem.at[lane, index],
            recv_sem=recv_sem.at[lane, index], device_id={"head": other}, device_id_type=MESH,
        )

    locals_, first, second, third = [], [], [], []
    for cut in range(cuts):
        span = pl.ds(cut * size, size)
        first.append(remote(x_ref.at[corner, span], corner_in.at[span], 0, cut, near))
        first[-1].start()
        locals_.append(
            pltpu.make_async_copy(x_ref.at[far, span], passed.at[span], local_sem.at[0, cut])
        )
        locals_[-1].start()
    own = []
    for cut in range(cuts):
        span = pl.ds(cut * size, size)
        second.append(remote(x_ref.at[near, span], near_in.at[span], 1, cut, near))
        second[-1].start()
        own.append(pltpu.make_async_copy(x_ref.at[me, span], mine.at[span], local_sem.at[1, cut]))
        own[-1].start()
    for cut in range(cuts):
        span = pl.ds(cut * size, size)
        first[cut].wait_recv()
        locals_[cut].wait()
        both = passed[span, :].astype(FULL) + corner_in[span, :].astype(FULL)
        passed[span, :] = both.astype(LOW)
        third.append(remote(passed.at[span], far_in.at[span], 2, cut, far))
        third[-1].start()
    for cut in range(cuts):
        span = pl.ds(cut * size, size)
        second[cut].wait_recv()
        own[cut].wait()
        third[cut].wait_recv()
        total = mine[span, :].astype(FULL) + near_in[span, :].astype(FULL)
        out_ref[span, :] = (total + far_in[span, :].astype(FULL)).astype(LOW)
    for cut in range(cuts):
        first[cut].wait_send()
        second[cut].wait_send()
        third[cut].wait_send()


def head_scatter(x, collective_id, cuts=4):
    shape = x.shape[1:]
    return pl.pallas_call(
        functools.partial(scatter_kernel, cuts),
        in_specs=[pl.BlockSpec(memory_space=pl.ANY)],
        out_specs=pl.BlockSpec(memory_space=pltpu.VMEM),
        out_shape=jax.ShapeDtypeStruct(shape, LOW),
        scratch_shapes=[pltpu.VMEM(shape, LOW)] * 5
        + [
            pltpu.SemaphoreType.DMA((2, cuts)), pltpu.SemaphoreType.DMA((3, cuts)),
            pltpu.SemaphoreType.DMA((3, cuts)),
        ],
        compiler_params=params(collective_id=collective_id, has_side_effects=True),
        name="head_scatter",
    )(x)


def first_norm_kernel(x_ref, n1g_ref, x1g_ref, norm_ref, out_ref, sums_ref):
    normal, scale = normalise(x_ref[...].astype(FULL))
    upstream = n1g_ref[...].astype(FULL)
    back, gain_sum, shift_sum = norm_back(normal, scale, norm_ref[0:1, :], upstream)
    out_ref[...] = (x1g_ref[...].astype(FULL) + back).astype(LOW)
    sums_ref[...] = jnp.zeros_like(sums_ref)
    sums_ref[0:1, :] = gain_sum
    sums_ref[1:2, :] = shift_sum


def first_norm_backward(x, normed_grad, x1_grad, norm_params):
    rows, width = x.shape
    return pl.pallas_call(
        first_norm_kernel,
        out_shape=[
            jax.ShapeDtypeStruct((rows, width), LOW), jax.ShapeDtypeStruct((8, width), FULL)
        ],
        compiler_params=params(),
        name="first_norm_backward",
    )(x, normed_grad, x1_grad, norm_params)


def body(
    patches, cotangent, expert_ids, slot_pos, owners,
    tile_master, tile_first, tile_second,
    expert_up, up_first, up_second,
    expert_down, down_first, down_second,
    router, router_first, router_second,
    norm_params, norm_first, norm_second,
):
    tok_rows, width = patches.shape
    experts = router.shape[0]
    capacity = tok_rows // experts
    dp_count = lax.axis_size("dp")
    head_count = lax.axis_size("head")
    me_head = lax.axis_index("head")
    me_dp = lax.axis_index("dp")
    images = tok_rows // PATCH
    share = capacity // head_count
    own_slots = experts * share
    own_rows = tok_rows // head_count
    slot_count = tile_master.shape[0]

    gathered = lax.all_gather(tile_master.astype(LOW), "dp", axis=0, tiled=True)
    owner_row = owners[0]
    tile_count = owner_row.shape[0]
    order_index = jnp.arange(tile_count, dtype=jnp.int32)
    same_owner = owner_row[:, None] == owner_row[None, :]
    earlier = order_index[None, :] < order_index[:, None]
    tile_rank = jnp.sum(jnp.where(same_owner & earlier, 1, 0), axis=1).astype(jnp.int32)
    tile_place = owner_row * slot_count + tile_rank
    src = (tile_place[:, None] * TILE + jnp.arange(TILE, dtype=jnp.int32)[None, :]).reshape(-1)
    held = gathered.reshape(dp_count * slot_count * TILE, width)

    up_low = expert_up[0].astype(LOW)
    down_low = expert_down[0].astype(LOW)
    up_all = lax.all_gather(up_low, "head", axis=0)
    down_all = lax.all_gather(down_low, "head", axis=0)

    kept = slot_pos < capacity
    col = (slot_pos // share) * own_slots + expert_ids * share + lax.rem(slot_pos, share)
    col = jnp.where(kept, col, tok_rows)
    col_rows = (col - me_head * own_slots).reshape(images, PATCH, 2).transpose(0, 2, 1)

    def to_experts(rows):
        rows = rows.reshape(experts, share, width)
        return lax.all_to_all(rows, "dp", 0, 0, tiled=True).reshape(own_slots, width)

    g_rows = to_experts(dispatch(cotangent, None, col_rows, own_slots))

    *saved, partial = attention_forward(patches, norm_params, held, src[:, None])
    own_patches = lax.dynamic_slice_in_dim(patches, me_head * own_rows, own_rows, 0)
    attended = head_scatter(partial.reshape(head_count, own_rows, width), 0)
    x1_own = (own_patches.astype(FULL) + attended.astype(FULL)).astype(LOW)
    x1 = head_gather(x1_own, 1).reshape(tok_rows, width)

    rows = to_experts(dispatch(x1, norm_params, col_rows, own_slots))
    back, out, up_part, down_part, router_part = experts_both_ways(
        rows, g_rows, up_all, down_all, router.astype(LOW), me_dp
    )
    back_all = head_gather(to_experts(back), 2).reshape(tok_rows, width)
    x1_grad, second_sums = combine_backward(col, back_all, x1, cotangent, norm_params)

    partial_grad, padded = attention_backward(
        x1_grad, saved, src[None, :], dp_count * slot_count * TILE
    )
    normed_grad = head_scatter(partial_grad.reshape(head_count, own_rows, width), 3)
    own_grad = lax.dynamic_slice_in_dim(x1_grad, me_head * own_rows, own_rows, 0)
    input_own, first_sums = first_norm_backward(own_patches, normed_grad, own_grad, norm_params)
    input_grad = head_gather(input_own, 4).reshape(tok_rows, width).astype(FULL)

    out_all = lax.all_gather(to_experts(out), "head", axis=0, tiled=True)
    block_out = combine_forward(col, out_all, x1)

    up_grad = lax.psum_scatter(up_part, "head", scatter_dimension=0).astype(FULL)
    down_grad = lax.psum_scatter(down_part, "head", scatter_dimension=0).astype(FULL)
    owned_grad = lax.psum_scatter(
        padded.reshape(dp_count * slot_count, TILE, width), "dp", scatter_dimension=0, tiled=True
    ).astype(FULL)

    small = jnp.concatenate(
        [router_part[:experts], first_sums[:2], second_sums[:2] * (1.0 / head_count)], axis=0
    )
    small = lax.psum(small, ("dp", "head"))
    router_total, norm_total = small[:experts], small[experts:]

    tile_new, tile_first_new, tile_second_new = adam_update(
        tile_master, tile_first, tile_second, owned_grad, rate_attention, decay_factor
    )
    up_new, up_first_new, up_second_new = adam_update(
        expert_up, up_first, up_second, up_grad[None], rate_up, decay_factor
    )
    down_new, down_first_new, down_second_new = adam_update(
        expert_down, down_first, down_second, down_grad[None], rate_down, decay_factor
    )
    router_new, router_first_new, router_second_new = adam_update(
        router, router_first, router_second, router_total, rate_router, decay_factor
    )
    norm_new, norm_first_new, norm_second_all = adam_update(
        norm_params, norm_first, norm_second, norm_total, rate_norm, 0.0
    )
    return (
        block_out,
        input_grad,
        tile_new,
        tile_first_new,
        tile_second_new,
        tile_new.astype(LOW),
        up_new,
        up_first_new,
        up_second_new,
        up_new.astype(LOW),
        down_new,
        down_first_new,
        down_second_new,
        down_new.astype(LOW),
        router_new,
        router_first_new,
        router_second_new,
        norm_new,
        norm_first_new,
        norm_second_all[:2],
        norm_second_all[2:],
    )


def solution(mesh):
    row = P("dp", None)
    tiles = P(("dp", "head"), None, None)
    up = P("dp", None, "head")
    down = P("dp", "head", None)
    in_specs = (
        row, row, row, row, P("head", None), tiles, tiles, tiles,
        up, up, up, down, down, down, P(), P(), P(), P(), P(), P(),
    )
    out_specs = (
        row, row, tiles, tiles, tiles, tiles, up, up, up, up, down, down, down, down,
        P(), P(), P(), P(), P(), P(), P(),
    )
    return jax.shard_map(body, mesh=mesh, in_specs=in_specs, out_specs=out_specs, check_vma=False)
```

time: 1140 us -> 596 us (0.52)
  waiting for transfers between devices: 450 us -> 108 us
  Pallas kernels: 0 us -> 299 us
  local copies, waits for them, and re-layouts: 228 us -> 21.8 us
  matrix products: 133 us -> 0 us
  other arithmetic: 169 us -> 45.7 us
  blocking collectives: 124 us -> 83.7 us
    pallas_call x0 -> x13, Pallas kernels: none -> 299 us  [the longest x3 105 us: head_gather(): pl.pallas_call(functools.partial(gather_kernel, cuts), in_specs=[pl.Block...]
    psum x3 -> x0, waiting for transfers between devices: 220 us -> none  [the longest x1 132 us: body(): expert_total = lax.psum(out_partial.astype(jnp.bfloat16), 'head')]
    all_to_all x3, waiting for transfers between devices: 178 us -> 42.9 us  [to_experts(): lax.all_to_all(rows, 'dp', 0, 0, tiled=True).reshape(own_slots, width)]
    dot_general x21 -> x0, matrix products: 133 us -> none  [the longest x5 34.3 us: matmul_float(): return jnp.dot(left_side, right_side, preferred_element_type=jnp.float32)]
    gather x12 -> x0, local copies, waits for them, and re-layouts: 117 us -> none  [the longest x2 34.8 us: body(): jnp.take(sent_grad.reshape(rows_total, model_width), gather_slot, axis=0)]
    reduce_sum x13 -> x0, other arithmetic: 102 us -> none  [the longest x1 63.7 us: body(): gate_grad = jnp.sum(upstream[:, None, :] * picked, axis=-1)]
    scatter x4 -> x1, local copies, waits for them, and re-layouts: 66.6 us -> 0.69 us  [experts_both_ways(): router_wide = jnp.zeros((lanes, width), LOW).at[:experts].set(router_low)]
    all_to_all x1, blocking collectives: 85 us -> 44.6 us  [to_experts(): lax.all_to_all(rows, 'dp', 0, 0, tiled=True).reshape(own_slots, width)]
  transfers between devices with their start and end apart: 8 -> 10, of which waited for: 8 -> 4; matrix products, arithmetic and copies ran while one was open for 19% -> 9% of each run, Pallas kernels for 0% -> 33%
where the time goes in v1:
time: 596 us; the launch traced here: 590 us
  Pallas kernels  299 us (50%)
  waiting for transfers between devices  108 us (18%)
  blocking collectives  83.7 us (14%)
  other arithmetic  45.7 us (8%)
  local copies, waits for them, and re-layouts  21.8 us (4%)
  starting transfers between devices  17.9 us (3%)
  between operations  14.6 us (2%)
    pallas_call x3, Pallas kernels, head_gather(): pl.pallas_call(functools.partial(gather_kernel, cuts), in_specs=[pl.Block...  105 us
    pallas_call x2, Pallas kernels, head_scatter(): pl.pallas_call(functools.partial(scatter_kernel, cuts), in_specs=[pl.Bloc...  57.1 us
    all_to_all x1, blocking collectives, to_experts(): lax.all_to_all(rows, 'dp', 0, 0, tiled=True).reshape(own_slots, width)  44.6 us
    all_to_all x3, waiting for transfers between devices, to_experts(): lax.all_to_all(rows, 'dp', 0, 0, tiled=True).reshape(own_slots, width)  42.9 us
    psum x1, blocking collectives, body(): small = lax.psum(small, ('dp', 'head'))  39.2 us
    reduce_scatter x1, waiting for transfers between devices, body(): lax.psum_scatter(up_part, 'head', scatter_dimension=0).astype(FULL)  35.3 us
    pallas_call x1, Pallas kernels, attention_backward(): pl.pallas_call(attention_rear, grid=(images,), in_specs=[wide_spec, whole...  31 us
    all_gather x1, waiting for transfers between devices, body(): gathered = lax.all_gather(tile_master.astype(LOW), 'dp', axis=0, tiled=True)  28.7 us
  transfers between devices with their start and end apart: 10, of which 4 were waited for; matrix products, arithmetic and copies ran while one was open for 9% of the time, Pallas kernels for 33%

profile of v1, /device:TPU:0, one launch (start us, length us, event | category | flops | bytes accessed | tf_op | source)
XLA Modules:
  0.0 590.5 jit_solution(15565416100075797459)
XLA Ops:
  9.1 2.9 convert_element_type.55
  22.0 3.3 fusion.5
  25.3 2.2 copy.101
  31.0 3.3 broadcast_subtract_fusion
  34.3 2.3 copy.106
  36.6 6.5 %dispatch_rows.3 = bf16[576,768]{1,0:T(8,128)(2,1)} custom-call(bf16[2304,768]{1,0:T(8,128)(2,1)} %g_ref.1, s32[4,2,576]{2,1,0:T(2,128)} %bitcast.37), custom_call_target="tpu_custom_call" | custom-call | tf_op jit(solution)/shard_map/dispatch_rows/pallas_call | solution.py:286
  43.2 7.6 %all-to-all-start.1 = ((bf16[8,72,768]{2,1,0:T(8,128)(2,1)}), bf16[8,72,768]{2,1,0:T(8,128)(2,1)S(1)}, u32[]{:S(2)}, u32[]{:S(2)}) async-start(bf16[8,72,768]{2,1,0:T(8,128)(2,1)} %bitcast.28), calls=%async_computation.1 | async-start | bytes 1769472 | tf_op jit(solution)/shard_map/all_to_all | solution.py:647
  52.0 28.7 %all-gather.5.cloned.1.call-done = bf16[192,8,768]{2,1,0:T(8,128)(2,1)} async-done(((bf16[24,8,768]{2,1,0:T(8,128)(2,1)}), bf16[192,8,768]{2,1,0:T(8,128)(2,1)}) %all-gather.5.cloned.1.call-update) | async-done | bytes 2359312 | tf_op jit(solution)/shard_map/all_gather | solution.py:624
  80.7 23.6 %attention_forward.1 = (bf16[768,768]{1,0:T(8,128)(2,1)}, bf16[2304,768]{1,0:T(8,128)(2,1)}, bf16[2304,192]{1,0:T(8,128)(2,1)}, bf16[4,192,576]{2,1,0:T(8,128)(2...) custom-call(bf16[2304,768]{1,0:T(8,128)(2,1)} %x_ref.1, ...), custom_call_target="tpu_custom_call" | custom-call | tf_op jit(solution)/shard_map/attention_forward/pallas_call | solution.py:148
  104.3 32.4 %head_scatter.2 = bf16[576,768]{1,0:T(8,128)(2,1)} custom-call(bf16[4,576,768]{2,1,0:T(8,128)(2,1)} %bitcast.30), custom_call_target="tpu_custom_call" | custom-call | tf_op jit(solution)/shard_map/head_scatter/pallas_call | solution.py:566
  136.7 3.1 add_convert_fusion
  139.8 42.8 %head_gather.3 = bf16[4,576,768]{2,1,0:T(8,128)(2,1)} custom-call(bf16[576,768]{1,0:T(8,128)(2,1)} %get-tuple-element.95.x_ref), custom_call_target="tpu_custom_call" | custom-call | tf_op jit(solution)/shard_map/head_gather/pallas_call | solution.py:499
  182.6 8.7 %dispatch_rows.2 = bf16[576,768]{1,0:T(8,128)(2,1)} custom-call(bf16[2304,768]{1,0:T(8,128)(2,1)} %bitcast.21, f32[4,768]{1,0:T(4,128)} %norm_ref.7, s32[4,2,576]{2,1,0:T(2,128)} %bitcast.38), custom_call_target="tpu_custom_call" | custom-call | tf_op jit(solution)/shard_map/dispatch_rows/pallas_call | solution.py:286
  191.2 5.7 all-to-all-start
  198.2 21.6 %all-to-all-done = bf16[8,72,768]{2,1,0:T(8,128)(2,1)} async-done(((bf16[8,72,768]{2,1,0:T(8,128)(2,1)}), bf16[8,72,768]{2,1,0:T(8,128)(2,1)}, u32[]{:S(2)}, u32[]{:S(2)}) %all-to-all-start) | async-done | bytes 884768 | tf_op jit(solution)/shard_map/all_to_all | solution.py:647
  219.8 27.4 %experts_both_ways.1 = (bf16[576,768]{1,0:T(8,128)(2,1)}, bf16[576,768]{1,0:T(8,128)(2,1)}, bf16[4,768,768]{2,1,0:T(8,128)(2,1)}, bf16[4,768,768]{2,1,0:T(8,128)(2,1)}, f32[128,768]{1,0:T(8,128)}) custom-call(bf16[576,768]{1,0:T(8,128)(2,1)} %bitcast.7.rows_ref, bf16[576,768]{1,0:T(8,128)(2,1)} %bitcast.26, ...), custom_call_target="tpu_custom_call" | custom-call | tf_op jit(solution)/shard_map/experts_both_ways/pallas_call | solution.py:421
  247.2 3.7 all-to-all-start.3
  252.0 21.3 %all-to-all-done.3 = bf16[8,72,768]{2,1,0:T(8,128)(2,1)S(1)} async-done(((bf16[8,72,768]{2,1,0:T(8,128)(2,1)}), bf16[8,72,768]{2,1,0:T(8,128)(2,1)S(1)}, u32[]{:S(2)}, u32[]{:S(2)}) %all-to-all-start.3) | async-done | bytes 884768 | tf_op jit(solution)/shard_map/all_to_all | solution.py:647
  274.2 28.8 %head_gather.4 = bf16[4,576,768]{2,1,0:T(8,128)(2,1)} custom-call(bf16[576,768]{1,0:T(8,128)(2,1)} %bitcast.32), custom_call_target="tpu_custom_call" | custom-call | tf_op jit(solution)/shard_map/head_gather/pallas_call | solution.py:499
  303.0 19.6 %combine_backward.1 = (bf16[2304,768]{1,0:T(8,128)(2,1)}, f32[8,768]{1,0:T(8,128)}) custom-call(s32[2304,2]{1,0:T(8,128)} %get-tuple-element.94.col_ref, bf16[2304,768]{1,0:T(8,128)(2,1)} %bitcast.24, bf16[2304,768]{1,0:T(8,128)(2,1)} %bitcast.22, bf16[2304,768]{1,0:T(8,128)(2,1)} %g_ref.1, f32[4,768]{1,0:T(4,128)} %norm_ref.7), custom_call_target="tpu_custom_call" | custom-call | tf_op jit(solution)/shard_map/combine_backward/pallas_call | solution.py:347
  322.7 31.0 %attention_backward.1 = (bf16[2304,768]{1,0:T(8,128)(2,1)}, bf16[1536,768]{1,0:T(8,128)(2,1)}) custom-call(bf16[2304,768]{1,0:T(8,128)(2,1)} %get-tuple-element.57.x1g_ref, bf16[768,768]{1,0:T(8,128)(2,1)} %get-tuple-element.58.w_ref, bf16[2304,768]{1,0:T(8,128)(2,1)} %get-tuple-element.59.xn_ref, bf16[2304,192]{1,0:T(8,128)(2,1)} %get-tuple-element.60.q_ref, ...), custom_call_target="tpu_custom_call" | custom-call | tf_op jit(solution)/shard_map/attention_backward/pallas_call | solution.py:229
  354.8 44.6 %all_to_all.20 = bf16[8,72,768]{2,1,0:T(8,128)(2,1)} all-to-all(bf16[8,72,768]{2,1,0:T(8,128)(2,1)S(1)} %bitcast.35), channel_id=1, replica_groups=mesh['dp'=8,'head'=4] {'dp'}, dimensions={0} | all-to-all | bytes 1769472 | tf_op jit(solution)/shard_map/all_to_all | solution.py:647
  401.5 24.8 %head_scatter.3.n1g_ref = bf16[576,768]{1,0:T(8,128)(2,1)} custom-call(bf16[4,576,768]{2,1,0:T(8,128)(2,1)} %bitcast.29), custom_call_target="tpu_custom_call" | custom-call | tf_op jit(solution)/shard_map/head_scatter/pallas_call | solution.py:566
  428.4 4.0 first_norm_backward.1
  433.2 33.3 %head_gather.5 = bf16[4,576,768]{2,1,0:T(8,128)(2,1)} custom-call(bf16[576,768]{1,0:T(8,128)(2,1)} %get-tuple-element.68.x_ref), custom_call_target="tpu_custom_call" | custom-call | tf_op jit(solution)/shard_map/head_gather/pallas_call | solution.py:499
  467.2 39.2 %psum.7 = f32[12,768]{1,0:T(8,128)S(1)} all-reduce(f32[12,768]{1,0:T(8,128)S(1)} %pad_maximum_fusion), channel_id=1, replica_groups=mesh['dp'=8,'head'=4] {'dp','head'}, use_global_device_ids=true, to_apply=%region_4.5 | all-reduce | flops 9216 | bytes 73728 | tf_op jit(solution)/shard_map/psum | solution.py:684
  508.4 5.6 bitcast_convert_fusion
  514.0 2.7 fusion.19
  516.7 16.0 %combine_forward.1 = bf16[2304,768]{1,0:T(8,128)(2,1)} custom-call(s32[2304,2]{1,0:T(8,128)} %get-tuple-element.94.col_ref, bf16[2304,768]{1,0:T(8,128)(2,1)} %all-gather.11.cloned.1.call-done.held_ref, bf16[2304,768]{1,0:T(8,128)(2,1)} %bitcast.23), custom_call_target="tpu_custom_call" | custom-call | tf_op jit(solution)/shard_map/combine_forward/pallas_call | solution.py:333
  532.7 7.5 %fusion.13 = (bf16[1,768,768]{2,1,0:T(8,128)(2,1)}, f32[1,768,768]{2,1,0:T(8,128)}, f32[1,768,768]{2,1,0:T(8,128)}, f32[1,768,768]{2,1,0:T(8,128)}) fusion(f32[1,768,768]{2,1,0:T(8,128)S(1)} %copy-done, bf16[1,768,768]{2,1,0:T(8,128)(2,1)} %reduce-scatter.8.cloned.1.call-done, f32[1,768,768]{2,1,0:T(8,128)} %param.34, f32[1,768,768]{2,1,0:T(8,128)} %param.35), kind=kLoop, calls=%fused_computation.45 | loop fusion | flops 10027008 | bytes 16515072 | tf_op jit(solution)/shard_map/convert_element_type | solution.py:716
  540.2 35.3 %reduce-scatter.6.cloned.1.call-done = bf16[1,768,768]{2,1,0:T(8,128)(2,1)} async-done(((bf16[4,768,768]{2,1,0:T(8,128)(2,1)}), bf16[1,768,768]{2,1,0:T(8,128)(2,1)}) %reduce-scatter.6.cloned.1.call-update) | async-done | bytes 1179664 | tf_op jit(solution)/shard_map/reduce_scatter | solution.py:675
  575.5 8.0 %fusion.16 = (bf16[1,768,768]{2,1,0:T(8,128)(2,1)}, f32[1,768,768]{2,1,0:T(8,128)}, f32[1,768,768]{2,1,0:T(8,128)}, f32[1,768,768]{2,1,0:T(8,128)}) fusion(f32[1,768,768]{2,1,0:T(8,128)} %param.30, bf16[1,768,768]{2,1,0:T(8,128)(2,1)} %reduce-scatter.6.cloned.1.call-done, f32[1,768,768]{2,1,0:T(8,128)} %param.31, f32[1,768,768]{2,1,0:T(8,128)} %param.32), kind=kLoop, calls=%fused_computation.46 | loop fusion | flops 10027008 | bytes 16515072 | tf_op jit(solution)/shard_map/convert_element_type | solution.py:712
  (72 shorter events, 28.5 us)
Async XLA Ops:
  7.2 73.5 %all-gather.5.cloned.1.call-start = ((), (), s32[]{:S(2)}) async-start(), calls=%async_computation.7 | async-start | bytes 2654208 | tf_op jit(solution)/shard_map/all_gather | solution.py:624
  9.1 3.1 copy-start
  9.1 210.7 %all-gather.7.cloned.1.call-start = ((), (), s32[]{:S(2)}) async-start(), calls=%async_computation.8 | async-start | bytes 5898240 | tf_op jit(solution)/shard_map/all_gather | solution.py:637
  12.1 207.7 %all-gather.9.cloned.1.call-start = ((), (), s32[]{:S(2)}) async-start(), calls=%async_computation.9 | async-start | bytes 5898240 | tf_op jit(solution)/shard_map/all_gather | solution.py:638
  36.6 14.2 %copy-start.12 = (s32[1,96]{1,0:T(1,128)S(1)}, s32[1,96]{1,0:T(1,128)}, u32[]{:S(2)}) copy-start(s32[1,96]{1,0:T(1,128)} %param.26) | copy-start | bytes 1156
  43.2 148.1 %all-to-all-start.1 = ((bf16[8,72,768]{2,1,0:T(8,128)(2,1)}), bf16[8,72,768]{2,1,0:T(8,128)(2,1)S(1)}, u32[]{:S(2)}, u32[]{:S(2)}) async-start(bf16[8,72,768]{2,1,0:T(8,128)(2,1)} %bitcast.28), calls=%async_computation.1 | async-start | bytes 1769472 | tf_op jit(solution)/shard_map/all_to_all | solution.py:647
  182.6 14.4 %copy-start.7 = (f32[8,768]{1,0:T(8,128)S(1)}, f32[8,768]{1,0:T(8,128)}, u32[]{:S(2)}) copy-start(f32[8,768]{1,0:T(8,128)} %param.36) | copy-start | bytes 73732
  191.2 28.5 %copy-start.1 = (bf16[8,72,768]{2,1,0:T(8,128)(2,1)}, bf16[8,72,768]{2,1,0:T(8,128)(2,1)S(1)}, u32[]{:S(2)}) copy-start(bf16[8,72,768]{2,1,0:T(8,128)(2,1)S(1)} %all-to-all-done.1) | copy-start | bytes 2654212
  191.2 28.5 %all-to-all-start = ((bf16[8,72,768]{2,1,0:T(8,128)(2,1)}), bf16[8,72,768]{2,1,0:T(8,128)(2,1)}, u32[]{:S(2)}, u32[]{:S(2)}) async-start(bf16[8,72,768]{2,1,0:T(8,128)(2,1)} %bitcast.31), calls=%async_computation | async-start | bytes 1769472 | tf_op jit(solution)/shard_map/all_to_all | solution.py:647
  247.2 26.1 %all-to-all-start.3 = ((bf16[8,72,768]{2,1,0:T(8,128)(2,1)}), bf16[8,72,768]{2,1,0:T(8,128)(2,1)S(1)}, u32[]{:S(2)}, u32[]{:S(2)}) async-start(bf16[8,72,768]{2,1,0:T(8,128)(2,1)} %bitcast.36), calls=%async_computation.3 | async-start | bytes 1769472 | tf_op jit(solution)/shard_map/all_to_all | solution.py:647
  250.9 263.1 %reduce-scatter.4.cloned.1.call-start = ((), (), s32[]{:S(2)}) async-start(), calls=%async_computation.11 | async-start | bytes 2654208 | tf_op jit(solution)/shard_map/reduce_scatter | solution.py:677
  273.3 0.9 copy-start.2
  353.6 1.2 copy-start.4
  353.7 163.0 %all-gather.11.cloned.1.call-start = ((), (), s32[]{:S(2)}) async-start(), calls=%async_computation.10 | async-start | bytes 4423680 | tf_op jit(solution)/shard_map/all_gather | solution.py:672
  399.4 133.3 %reduce-scatter.8.cloned.1.call-start = ((), (), s32[]{:S(2)}) async-start(), calls=%async_computation.13 | async-start | bytes 5898240 | tf_op jit(solution)/shard_map/reduce_scatter | solution.py:676
  400.0 175.5 %reduce-scatter.6.cloned.1.call-start = ((), (), s32[]{:S(2)}) async-start(), calls=%async_computation.12 | async-start | bytes 5898240 | tf_op jit(solution)/shard_map/reduce_scatter | solution.py:675
  432.4 74.0 %copy-start.6 = (f32[4,768]{1,0:T(4,128)S(1)}, f32[4,768]{1,0:T(4,128)}, u32[]{:S(2)}) copy-start(f32[4,768]{1,0:T(4,128)} %norm_ref.7) | copy-start | bytes 36868
  432.4 74.0 %copy-start.10 = (f32[4,768]{1,0:T(4,128)S(1)}, f32[4,768]{1,0:T(4,128)}, u32[]{:S(2)}) copy-start(f32[4,768]{1,0:T(4,128)} %param.40) | copy-start | bytes 36868
  432.4 74.0 %copy-start.11 = (f32[4,768]{1,0:T(4,128)S(1)}, f32[4,768]{1,0:T(4,128)}, u32[]{:S(2)}) copy-start(f32[4,768]{1,0:T(4,128)} %param.41) | copy-start | bytes 36868
  433.2 74.5 %copy-start.8 = (f32[8,768]{1,0:T(8,128)S(1)}, f32[8,768]{1,0:T(8,128)}, u32[]{:S(2)}) copy-start(f32[8,768]{1,0:T(8,128)} %param.37) | copy-start | bytes 73732
  433.2 74.5 %copy-start.9 = (f32[8,768]{1,0:T(8,128)S(1)}, f32[8,768]{1,0:T(8,128)}, u32[]{:S(2)}) copy-start(f32[8,768]{1,0:T(8,128)} %param.38) | copy-start | bytes 73732
  508.4 5.6 copy-start.3
  508.4 5.6 copy-start.5
Sparse Core Ops, SparseCore 0:
  10.8 69.9 all-gather.4
  82.9 42.7 all-gather.6
  127.8 60.3 all-gather.8
  353.8 81.7 reduce-scatter.3
  437.0 39.0 all-gather.10
  478.5 46.3 reduce-scatter.7
  527.6 47.8 reduce-scatter.5

commit v2 on v1

v2 whole, which is shorter than its diff:
```python
import functools

import jax
import jax.numpy as jnp
from jax import lax
from jax.experimental import pallas as pl
from jax.experimental.pallas import tpu as pltpu
from jax.sharding import PartitionSpec as P

HD = 64
PATCH = 576
TILE = 8
STEP = 10

eps_norm = 1e-06
beta_one = 0.9
beta_two = 0.999
adam_eps = 1e-08
rate_attention = 0.12
rate_up = 0.08
rate_down = 0.3
rate_router = 0.05
rate_norm = 0.4
decay_factor = 0.1

LOW = jnp.bfloat16
FULL = jnp.float32
MESH = pl.DeviceIdType.MESH
VMEM_BYTES = 56 * 1024 * 1024


def adam_update(weight, moment_one, moment_two, gradient, step_rate, weight_decay):
    moment_one = beta_one * moment_one + (1.0 - beta_one) * gradient
    moment_two = beta_two * moment_two + (1.0 - beta_two) * gradient * gradient
    fixed_one = moment_one / (1.0 - beta_one**STEP)
    fixed_two = moment_two / (1.0 - beta_two**STEP)
    weight = weight - step_rate * (
        fixed_one / (jnp.sqrt(fixed_two) + adam_eps) + weight_decay * weight
    )
    return (weight, moment_one, moment_two)


def nn(left, right):
    return lax.dot_general(left, right, (((1,), (0,)), ((), ())), preferred_element_type=FULL)


def nt(left, right):
    return lax.dot_general(left, right, (((1,), (1,)), ((), ())), preferred_element_type=FULL)


def tn(left, right):
    return lax.dot_general(left, right, (((0,), (0,)), ((), ())), preferred_element_type=FULL)


def params(**more):
    return pltpu.CompilerParams(vmem_limit_bytes=VMEM_BYTES, **more)


def whole(shape):
    return pl.BlockSpec(shape, lambda *_: (0,) * len(shape))


def lead(shape):
    return pl.BlockSpec(shape, lambda i: (i,) + (0,) * (len(shape) - 1))


def normalise(values):
    average = jnp.mean(values, axis=-1, keepdims=True)
    centred = values - average
    variance = jnp.mean(centred * centred, axis=-1, keepdims=True)
    scale = lax.rsqrt(variance + eps_norm)
    return centred * scale, scale


def norm_back(normal, scale, gain, upstream):
    inner = upstream * gain
    mean_inner = jnp.mean(inner, axis=-1, keepdims=True)
    mean_cross = jnp.mean(inner * normal, axis=-1, keepdims=True)
    result = scale * (inner - mean_inner - normal * mean_cross)
    gain_sum = jnp.sum(upstream * normal, axis=0, keepdims=True)
    shift_sum = jnp.sum(upstream, axis=0, keepdims=True)
    return result, gain_sum, shift_sum


def one_hot(condition):
    return jnp.where(condition, 1.0, 0.0).astype(LOW)


def remote(src, dst, sends, recvs, index, axis, other):
    return pltpu.make_async_remote_copy(
        src_ref=src, dst_ref=dst, send_sem=sends.at[index], recv_sem=recvs.at[index],
        device_id={axis: other}, device_id_type=MESH,
    )


def greet(*others):
    barrier = pltpu.get_barrier_semaphore()
    for axis, other in others:
        pl.semaphore_signal(barrier, inc=1, device_id={axis: other}, device_id_type=MESH)
    pl.semaphore_wait(barrier, len(others))


def partners():
    me = lax.axis_index("head")
    near = me + 1 - 2 * lax.rem(me, 2)
    far = lax.rem(me + 2, 4)
    corner = lax.rem(near + 2, 4)
    return me, near, far, corner


class LineGather:
    def __init__(self, held, up_send, up_recv, down_send, down_recv, pair_send, pair_recv):
        self.held = held
        self.length = held.shape[0] // 2
        self.sems = ((up_send, up_recv), (down_send, down_recv), (pair_send, pair_recv))
        me = lax.axis_index("dp")
        self.place, self.side = me // 2, lax.rem(me, 2)
        self.above = lax.rem(self.place + 1, self.length) * 2 + self.side
        self.below = lax.rem(self.place + self.length - 1, self.length) * 2 + self.side
        self.other = self.place * 2 + 1 - self.side

    def neighbours(self):
        return ("dp", self.above), ("dp", self.below), ("dp", self.other)

    def copy(self, way, origin, side=None):
        index = origin * 2 + (self.side if side is None else side)
        target = (self.above, self.below, self.other)[way]
        block = self.held.at[index]
        return remote(block, block, *self.sems[way], origin, "dp", target)

    def pass_on(self, origin, up, down):
        @pl.when(up & (self.place < self.length - 1))
        def _():
            self.copy(0, origin).start()

        @pl.when(down & (self.place > 0))
        def _():
            self.copy(1, origin).start()

        self.copy(2, origin).start()

    def start(self):
        self.pass_on(self.place, True, True)

    def step(self, k):
        low, high = self.place - k, self.place + k

        @pl.when(low >= 0)
        def _():
            self.copy(0, low).wait_recv()
            self.pass_on(low, True, False)

        @pl.when(high < self.length)
        def _():
            self.copy(1, high).wait_recv()
            self.pass_on(high, False, True)

    def finish(self):
        @pl.loop(0, self.length)
        def _(origin):
            self.copy(2, origin).wait_recv()
            self.copy(2, origin).wait_send()

            @pl.when((origin <= self.place) & (self.place < self.length - 1))
            def _():
                self.copy(0, origin).wait_send()

            @pl.when((origin >= self.place) & (self.place > 0))
            def _():
                self.copy(1, origin).wait_send()


class ImageSum:
    def __init__(self, stage, corner_in, near_in, passed, mine, far_in, sends, recvs):
        self.stage, self.corner_in, self.near_in = stage, corner_in, near_in
        self.passed, self.mine, self.far_in = passed, mine, far_in
        self.sends, self.recvs = sends, recvs
        self.me, self.near, self.far, self.corner = partners()
        self.core = lax.rem(self.me, 2)

    def image(self, turn):
        base = self.me - self.core
        other = lax.rem(base + 2, 4)
        return jnp.where(turn < 2, other, base - 2) + turn

    def to_corner(self):
        return remote(
            self.stage.at[0], self.corner_in, self.sends, self.recvs, 0, "head", self.near
        )

    def to_near(self):
        return remote(
            self.stage.at[1], self.near_in, self.sends, self.recvs, 1, "head", self.near
        )

    def to_far(self):
        return remote(self.passed, self.far_in, self.sends, self.recvs, 2, "head", self.far)

    def give(self, turn, part):
        theirs = lax.rem(turn, 2) != self.core

        @pl.when((turn < 2) & theirs)
        def _():
            self.stage[0] = part.astype(LOW)
            self.to_corner().start()

        @pl.when((turn >= 2) & theirs)
        def _():
            self.stage[1] = part.astype(LOW)
            self.to_near().start()

        @pl.when((turn < 2) & ~theirs)
        def _():
            self.to_corner().wait_recv()
            self.passed[...] = (part + self.corner_in[...].astype(FULL)).astype(LOW)
            self.to_far().start()

        @pl.when((turn >= 2) & ~theirs)
        def _():
            self.mine[...] = part

    def result(self):
        self.to_near().wait_recv()
        self.to_far().wait_recv()
        return self.mine[...] + self.near_in[...].astype(FULL) + self.far_in[...].astype(FULL)

    def finish(self):
        self.to_corner().wait_send()
        self.to_near().wait_send()
        self.to_far().wait_send()


def image_sum_scratch(width):
    block = pltpu.VMEM((PATCH, width), LOW)
    return [
        pltpu.VMEM((2, PATCH, width), LOW), block, block, block,
        pltpu.VMEM((PATCH, width), FULL), block,
        pltpu.SemaphoreType.DMA((3,)), pltpu.SemaphoreType.DMA((3,)),
    ]


GATHER_CUTS = 4


class ImageGather:
    def __init__(self, held, sends, recvs):
        self.held, self.sends, self.recvs = held, sends, recvs
        self.me, self.near, self.far, self.corner = partners()
        self.size = held.shape[1] // GATHER_CUTS

    def piece(self, image, cut, lane, other):
        span = pl.ds(cut * self.size, self.size)
        block = self.held.at[image, span]
        return remote(block, block, self.sends, self.recvs, lane * GATHER_CUTS + cut, "head", other)

    def start(self):
        for cut in range(GATHER_CUTS):
            self.piece(self.me, cut, 0, self.far).start()
        for cut in range(GATHER_CUTS):
            self.piece(self.me, cut, 1, self.near).start()

    def wait_near(self):
        for cut in range(GATHER_CUTS):
            self.piece(self.me, cut, 1, self.near).wait_recv()

    def wait_far(self):
        for cut in range(GATHER_CUTS):
            self.piece(self.me, cut, 0, self.far).wait_recv()
            self.piece(self.far, cut, 2, self.near).start()

    def wait_corner(self):
        for cut in range(GATHER_CUTS):
            self.piece(self.far, cut, 2, self.near).wait_recv()

    def finish(self):
        for cut in range(GATHER_CUTS):
            self.piece(self.me, cut, 0, self.far).wait_send()
            self.piece(self.me, cut, 1, self.near).wait_send()
            self.piece(self.far, cut, 2, self.near).wait_send()


def image_gather_sems():
    return [pltpu.SemaphoreType.DMA((3 * GATHER_CUTS,)), pltpu.SemaphoreType.DMA((3 * GATHER_CUTS,))]


ANYWHERE = pl.BlockSpec(memory_space=pl.ANY)
INSIDE = pl.BlockSpec(memory_space=pltpu.VMEM)


def prepare_kernel(
    tile_ref, x_ref, g_ref, norm_ref, src_ref, col_ref,
    w_ref, xn_ref, sent_ref,
    held, sent_sum, *sems,
):
    images = x_ref.shape[0]
    gather = LineGather(held, *sems)
    greet(*gather.neighbours())
    me = lax.axis_index("dp")
    held[me] = tile_ref[...].astype(LOW)
    gather.start()

    def image_step(image):
        normal, _ = normalise(x_ref[image].astype(FULL))
        xn_ref[image] = (normal * norm_ref[0:1, :] + norm_ref[1:2, :]).astype(LOW)
        shape = (sent_ref.shape[0], PATCH)
        slots = lax.broadcasted_iota(jnp.int32, shape, 0)
        col = col_ref[image]
        pick = one_hot((slots == col[0:1, :]) | (slots == col[1:2, :]))
        sent_sum[...] += nn(pick, g_ref[image])

    sent_sum[...] = jnp.zeros_like(sent_sum)
    steps = gather.length - 1

    @pl.loop(0, max(steps, images))
    def _(turn):
        @pl.when(turn < images)
        def _():
            image_step(turn)

        @pl.when(turn < steps)
        def _():
            gather.step(turn + 1)

    sent_ref[...] = sent_sum[...].astype(LOW)
    gather.finish()
    rows = w_ref.shape[0] // 4
    blocks, depth, width = held.shape
    for part in range(4):
        block = pl.ds(part * rows, rows)
        lanes = lax.broadcasted_iota(jnp.int32, (rows, blocks * depth), 1)
        pick = one_hot(lanes == src_ref[block, :])
        w_ref[block, :] = nn(pick, held[...].reshape(blocks * depth, width)).astype(LOW)


def prepare(tiles, patches, cotangent, norm_params, src_col, col_rows, slots, dp_count):
    images, _, width = patches.shape
    line = dp_count // 2
    return pl.pallas_call(
        prepare_kernel,
        in_specs=[INSIDE] * 6,
        out_specs=[INSIDE] * 3,
        out_shape=[
            jax.ShapeDtypeStruct((src_col.shape[0], width), LOW),
            jax.ShapeDtypeStruct(patches.shape, LOW),
            jax.ShapeDtypeStruct((slots, width), LOW),
        ],
        scratch_shapes=[
            pltpu.VMEM((dp_count,) + tiles.shape, LOW), pltpu.VMEM((slots, width), FULL),
        ] + [pltpu.SemaphoreType.DMA((line,))] * 6,
        compiler_params=params(collective_id=0, has_side_effects=True),
        name="prepare",
    )(tiles, patches, cotangent, norm_params, src_col, col_rows)


def head_mask(shape, axis, head):
    return lax.broadcasted_iota(jnp.int32, shape, axis) // HD == head


def forward_kernel(
    xn_ref, w_ref, x_ref, norm_ref, col_ref,
    lse_ref, sent_ref, q_out, qt_out, k_out, kt_out, v_out, ot_out, x1_out,
    q_ref, qt_ref, k_ref, kt_ref, v_ref, ot_ref, x1_ref, own_ref, sent_sum,
    save_sems, own_sem, *exchange,
):
    images = xn_ref.shape[0]
    rows = w_ref.shape[0] // 4
    heads = rows // HD
    total_of = ImageSum(*exchange[:8])
    spread = ImageGather(x1_ref, *exchange[8:])
    me, near, far, corner = partners()
    greet(("head", near), ("head", far))
    own = pltpu.make_async_copy(x_ref.at[me], own_ref, own_sem)
    own.start()
    kept = ((q_ref, q_out), (qt_ref, qt_out), (k_ref, k_out), (kt_ref, kt_out), (v_ref, v_out), (ot_ref, ot_out))
    shrink = HD ** (-0.5)

    def save(image):
        return [
            pltpu.make_async_copy(ref.at[image], out.at[image], save_sems.at[index, image])
            for index, (ref, out) in enumerate(kept)
        ]

    @pl.loop(0, images)
    def _(turn):
        image = total_of.image(turn)
        xn = xn_ref[image]
        wq, wk, wv, wo = (w_ref[pl.ds(part * rows, rows), :] for part in range(4))
        q_ref[image] = (nt(xn, wq) * shrink).astype(LOW)
        qt = (nt(wq, xn) * shrink).astype(LOW)
        qt_ref[image] = qt
        k = nt(xn, wk).astype(LOW)
        k_ref[image] = k
        kt_ref[image] = nt(wk, xn).astype(LOW)
        v_ref[image] = nt(xn, wv).astype(LOW)
        vt = nt(wv, xn).astype(LOW)
        mixed = []
        for head in range(heads):
            span = slice(head * HD, (head + 1) * HD)
            only = jnp.where(head_mask(qt.shape, 0, head), qt, jnp.zeros_like(qt))
            scores = nn(k, only)
            top = jnp.max(scores, axis=0, keepdims=True)
            weights = jnp.exp(scores - top)
            total = jnp.sum(weights, axis=0, keepdims=True)
            mixed.append(nn(vt[span], weights.astype(LOW)) / total)
            lse_ref[image, head:head + 1, :] = top + jnp.log(total)
        ot = jnp.concatenate(mixed, axis=0).astype(LOW)
        ot_ref[image] = ot
        total_of.give(turn, tn(ot, wo))
        for copy in save(image):
            copy.start()

    own.wait()
    x1_ref[me] = (own_ref[...].astype(FULL) + total_of.result()).astype(LOW)
    spread.start()
    sent_sum[...] = jnp.zeros_like(sent_sum)

    def place(image):
        normal, _ = normalise(x1_ref[image].astype(FULL))
        low = (normal * norm_ref[2:3, :] + norm_ref[3:4, :]).astype(LOW)
        slots = lax.broadcasted_iota(jnp.int32, (sent_ref.shape[0], PATCH), 0)
        col = col_ref[image]
        pick = one_hot((slots == col[0:1, :]) | (slots == col[1:2, :]))
        sent_sum[...] += nn(pick, low)

    place(me)
    spread.wait_near()
    place(near)
    spread.wait_far()
    place(far)
    spread.wait_corner()
    keep = pltpu.make_async_copy(x1_ref, x1_out, own_sem)
    keep.start()
    place(corner)
    sent_ref[...] = sent_sum[...].astype(LOW)
    spread.finish()
    total_of.finish()
    keep.wait()

    @pl.loop(0, images)
    def _(image):
        for copy in save(image):
            copy.wait()


def attention_forward(xn, w, patches, norm_params, col_rows, slots):
    images, _, width = patches.shape
    rows = w.shape[0] // 4
    flat, turned = (images, PATCH, rows), (images, rows, PATCH)
    saved = [flat, turned, flat, turned, flat, turned, patches.shape]
    return pl.pallas_call(
        forward_kernel,
        in_specs=[INSIDE, INSIDE, ANYWHERE, INSIDE, INSIDE],
        out_specs=[INSIDE, INSIDE] + [ANYWHERE] * 7,
        out_shape=[
            jax.ShapeDtypeStruct((images, 8, PATCH), FULL), jax.ShapeDtypeStruct((slots, width), LOW),
        ] + [jax.ShapeDtypeStruct(shape, LOW) for shape in saved],
        scratch_shapes=[pltpu.VMEM(shape, LOW) for shape in saved]
        + [
            pltpu.VMEM((PATCH, width), LOW), pltpu.VMEM((slots, width), FULL),
            pltpu.SemaphoreType.DMA((6, images)), pltpu.SemaphoreType.DMA,
        ]
        + image_sum_scratch(width) + image_gather_sems(),
        compiler_params=params(collective_id=1, has_side_effects=True),
        name="attention_forward",
    )(xn, w, patches, norm_params, col_rows)


def backward_kernel(
    x1g_ref, w_ref, xn_ref, q_ref, qt_ref, k_ref, kt_ref, v_ref, lse_ref, ot_ref, src_ref,
    x_ref, norm_ref,
    padded_ref, sums_ref, input_out,
    grad_ref, own_ref, input_ref, own_sem, *exchange,
):
    images = x1g_ref.shape[0]
    rows = w_ref.shape[0] // 4
    heads = rows // HD
    total_of = ImageSum(*exchange[:8])
    spread = ImageGather(input_ref, *exchange[8:])
    me, near, far, corner = partners()
    greet(("head", near), ("head", far))
    own = pltpu.make_async_copy(x_ref.at[me], own_ref, own_sem)
    own.start()
    shrink = HD ** (-0.5)
    grad_ref[...] = jnp.zeros_like(grad_ref)

    @pl.loop(0, images)
    def _(turn):
        image = total_of.image(turn)
        wq, wk, wv, wo = (w_ref[pl.ds(part * rows, rows), :] for part in range(4))
        x1g, xn = x1g_ref[image], xn_ref[image]
        q, qt, k, kt = q_ref[image], qt_ref[image], k_ref[image], kt_ref[image]
        v, ot = v_ref[image], ot_ref[image]
        do = nt(x1g, wo).astype(LOW)
        dot = nt(wo, x1g).astype(LOW)
        product = dot.astype(FULL) * ot.astype(FULL)
        dqt, dk, dv = [], None, None
        for head in range(heads):
            span = slice(head * HD, (head + 1) * HD)
            zero_t = jnp.zeros_like(qt)
            mask_t = head_mask(qt.shape, 0, head)
            mask = head_mask(q.shape, 1, head)
            scores = nn(k, jnp.where(mask_t, qt, zero_t))
            weights = jnp.exp(scores - lse_ref[image, head:head + 1, :])
            back = nn(v, jnp.where(mask_t, dot, zero_t))
            delta = jnp.sum(product[span], axis=0, keepdims=True)
            score_grad = (weights * (back - delta)).astype(LOW)
            dqt.append(nn(kt[span], score_grad) * shrink)
            dk_one = nn(score_grad, jnp.where(mask, q, jnp.zeros_like(q)))
            dv_one = nn(weights.astype(LOW), jnp.where(mask, do, jnp.zeros_like(do)))
            dk = dk_one if dk is None else dk + dk_one
            dv = dv_one if dv is None else dv + dv_one
        dqt = jnp.concatenate(dqt, axis=0).astype(LOW)
        dk, dv = dk.astype(LOW), dv.astype(LOW)
        total_of.give(turn, tn(dqt, wq) + nn(dk, wk) + nn(dv, wv))
        pieces = (nn(dqt, xn), tn(dk, xn), tn(dv, xn), nn(ot, x1g))
        for part, piece in enumerate(pieces):
            grad_ref[pl.ds(part * rows, rows), :] += piece

    own.wait()
    normal, scale = normalise(own_ref[...].astype(FULL))
    back, gain_sum, shift_sum = norm_back(normal, scale, norm_ref[0:1, :], total_of.result())
    sums_ref[...] = jnp.zeros_like(sums_ref)
    sums_ref[0:1, :] = gain_sum
    sums_ref[1:2, :] = shift_sum
    input_ref[me] = (x1g_ref[me].astype(FULL) + back).astype(LOW)
    spread.start()
    low = grad_ref[...].astype(LOW)
    cut = padded_ref.shape[0] // 4
    for part in range(4):
        row = lax.broadcasted_iota(jnp.int32, (cut, low.shape[0]), 0) + part * cut
        pick = one_hot(row == src_ref[...])
        padded_ref[pl.ds(part * cut, cut), :] = nn(pick, low).astype(LOW)
    spread.wait_near()
    spread.wait_far()
    spread.wait_corner()
    keep = pltpu.make_async_copy(input_ref, input_out, own_sem)
    keep.start()
    spread.finish()
    total_of.finish()
    keep.wait()


def attention_backward(x1_grad, w, xn, saved, lse, src_row, patches, norm_params, padded_rows):
    q, qt, k, kt, v, ot = saved
    images, _, width = patches.shape
    return pl.pallas_call(
        backward_kernel,
        in_specs=[INSIDE] * 11 + [ANYWHERE, INSIDE],
        out_specs=[INSIDE, INSIDE, ANYWHERE],
        out_shape=[
            jax.ShapeDtypeStruct((padded_rows, width), LOW), jax.ShapeDtypeStruct((8, width), FULL),
            jax.ShapeDtypeStruct(patches.shape, LOW),
        ],
        scratch_shapes=[
            pltpu.VMEM(w.shape, FULL), pltpu.VMEM((PATCH, width), LOW),
            pltpu.VMEM(patches.shape, LOW), pltpu.SemaphoreType.DMA,
        ]
        + image_sum_scratch(width) + image_gather_sems(),
        compiler_params=params(collective_id=2, has_side_effects=True),
        name="attention_backward",
    )(x1_grad, w, xn, q, qt, k, kt, v, lse, ot, src_row, patches, norm_params)


def picked_rows(col_ref, held_ref):
    tokens = col_ref.shape[0]
    slots, width = held_ref.shape
    cut = slots // 4
    total = jnp.zeros((tokens, width), FULL)
    for part in range(4):
        lanes = lax.broadcasted_iota(jnp.int32, (tokens, cut), 1) + part * cut
        pick = one_hot((lanes == col_ref[:, 0:1]) | (lanes == col_ref[:, 1:2]))
        total = total + nn(pick, held_ref[pl.ds(part * cut, cut), :])
    return total


def combine_front(col_ref, held_ref, x1_ref, out_ref):
    mix = picked_rows(col_ref, held_ref)
    out_ref[...] = (x1_ref[...].astype(FULL) + mix).astype(LOW)


def combine_rear(col_ref, held_ref, x1_ref, g_ref, norm_ref, out_ref, sums_ref):
    step = pl.program_id(0)
    upstream = picked_rows(col_ref, held_ref)
    normal, scale = normalise(x1_ref[...].astype(FULL))
    back, gain_sum, shift_sum = norm_back(normal, scale, norm_ref[2:3, :], upstream)
    out_ref[...] = (g_ref[...].astype(FULL) + back).astype(LOW)

    @pl.when(step == 0)
    def _():
        sums_ref[...] = jnp.zeros_like(sums_ref)

    sums_ref[0:1, :] += gain_sum
    sums_ref[1:2, :] += shift_sum


def combine_forward(col, held, x1):
    tokens, width = x1.shape
    wide_spec = lead((PATCH, width))
    return pl.pallas_call(
        combine_front,
        grid=(tokens // PATCH,),
        in_specs=[lead((PATCH, 2)), whole(held.shape), wide_spec],
        out_specs=wide_spec,
        out_shape=jax.ShapeDtypeStruct((tokens, width), LOW),
        compiler_params=params(),
        name="combine_forward",
    )(col, held, x1)


def combine_backward(col, held, x1, cotangent, norm_params):
    tokens, width = x1.shape
    wide_spec = lead((PATCH, width))
    return pl.pallas_call(
        combine_rear,
        grid=(tokens // PATCH,),
        in_specs=[
            lead((PATCH, 2)), whole(held.shape), wide_spec, wide_spec, whole(norm_params.shape)
        ],
        out_specs=[wide_spec, whole((8, width))],
        out_shape=[
            jax.ShapeDtypeStruct((tokens, width), LOW), jax.ShapeDtypeStruct((8, width), FULL)
        ],
        compiler_params=params(),
        name="combine_backward",
    )(col, held, x1, cotangent, norm_params)


def expert_kernel(
    rows_ref, g_ref, up_ref, down_ref, router_ref, own_ref, count_ref,
    back_ref, out_ref, upg_ref, downg_ref, router_grad_ref,
    out_sum, back_sum, og_ref, gate_ref, probs_ref,
):
    step = pl.program_id(0)
    rows = rows_ref[...]

    @pl.when(step == 0)
    def _():
        logits = nt(rows, router_ref[...]) + count_ref[...]
        top = jnp.max(logits, axis=-1, keepdims=True)
        weights = jnp.exp(logits - top)
        probs = weights / jnp.sum(weights, axis=-1, keepdims=True)
        gate = jnp.sum(probs * own_ref[...], axis=-1, keepdims=True)
        probs_ref[...] = probs
        gate_ref[...] = gate
        og_ref[...] = (gate * g_ref[...].astype(FULL)).astype(LOW)
        out_sum[...] = jnp.zeros_like(out_sum)
        back_sum[...] = jnp.zeros_like(back_sum)

    og = og_ref[...]
    up, down = up_ref[0], down_ref[0]
    hidden = nn(rows, up)
    slope = (2.0 / jnp.pi) ** 0.5
    square = hidden * hidden
    bend = jnp.tanh(slope * (hidden + 0.044715 * (square * hidden)))
    act = (0.5 * hidden * (1.0 + bend)).astype(LOW)
    out_sum[...] += nn(act, down)
    act_grad = nt(og, down)
    inner = slope * (1.0 + (3.0 * 0.044715) * square)
    curve = 0.5 * (1.0 + bend) + 0.5 * hidden * (1.0 - bend * bend) * inner
    hidden_grad = (curve * act_grad).astype(LOW)
    back_sum[...] += nt(hidden_grad, up)
    upg_ref[0] = tn(rows, hidden_grad).astype(LOW)
    downg_ref[0] = tn(act, og).astype(LOW)

    @pl.when(step == pl.num_programs(0) - 1)
    def _():
        out = out_sum[...].astype(LOW).astype(FULL)
        gate, probs = gate_ref[...], probs_ref[...]
        out_ref[...] = (gate * out).astype(LOW)
        gate_grad = jnp.sum(g_ref[...].astype(FULL) * out, axis=-1, keepdims=True)
        logit_grad = (gate_grad * (probs * (own_ref[...] - gate))).astype(LOW)
        back = back_sum[...].astype(LOW).astype(FULL) + nn(logit_grad, router_ref[...])
        back_ref[...] = back.astype(LOW)
        router_grad_ref[...] = tn(logit_grad, rows)


def experts_both_ways(rows, g_rows, up, down, router_low, own):
    slots, width = rows.shape
    parts, _, units = up.shape
    experts = router_low.shape[0]
    lanes = 128
    router_wide = jnp.zeros((lanes, width), LOW).at[:experts].set(router_low)
    lane = jnp.arange(lanes, dtype=jnp.int32)[None, :]
    own_row = jnp.where(lane == own, 1.0, 0.0).astype(FULL)
    closed = jnp.where(lane < experts, 0.0, -1e30).astype(FULL)
    wide_spec = whole((slots, width))
    return pl.pallas_call(
        expert_kernel,
        grid=(parts,),
        in_specs=[
            wide_spec, wide_spec, lead((1, width, units)), lead((1, units, width)),
            whole((lanes, width)), whole((1, lanes)), whole((1, lanes)),
        ],
        out_specs=[
            wide_spec, wide_spec, lead((1, width, units)), lead((1, units, width)),
            whole((lanes, width)),
        ],
        out_shape=[
            jax.ShapeDtypeStruct((slots, width), LOW),
            jax.ShapeDtypeStruct((slots, width), LOW),
            jax.ShapeDtypeStruct(up.shape, LOW),
            jax.ShapeDtypeStruct(down.shape, LOW),
            jax.ShapeDtypeStruct((lanes, width), FULL),
        ],
        scratch_shapes=[
            pltpu.VMEM((slots, width), FULL), pltpu.VMEM((slots, width), FULL),
            pltpu.VMEM((slots, width), LOW), pltpu.VMEM((slots, 1), FULL),
            pltpu.VMEM((slots, lanes), FULL),
        ],
        compiler_params=params(),
        name="experts_both_ways",
    )(rows, g_rows, up, down, router_wide, own_row, closed)


def gather_kernel(cuts, x_ref, out_ref, local_sem, send_sem, recv_sem):
    me, near, far, corner = partners()
    greet(("head", near), ("head", far))
    size = x_ref.shape[0] // cuts

    def remote(src, dst, lane, index, other):
        return pltpu.make_async_remote_copy(
            src_ref=src, dst_ref=dst, send_sem=send_sem.at[lane, index],
            recv_sem=recv_sem.at[lane, index], device_id={"head": other}, device_id_type=MESH,
        )

    local = pltpu.make_async_copy(x_ref, out_ref.at[me], local_sem)
    local.start()
    across, beside, onward = [], [], []
    for cut in range(cuts):
        span = pl.ds(cut * size, size)
        across.append(remote(x_ref.at[span], out_ref.at[me, span], 0, cut, far))
        across[-1].start()
    for cut in range(cuts):
        span = pl.ds(cut * size, size)
        beside.append(remote(x_ref.at[span], out_ref.at[me, span], 1, cut, near))
        beside[-1].start()
    for cut in range(cuts):
        span = pl.ds(cut * size, size)
        across[cut].wait_recv()
        onward.append(remote(out_ref.at[far, span], out_ref.at[far, span], 2, cut, near))
        onward[-1].start()
    for cut in range(cuts):
        across[cut].wait_send()
        beside[cut].wait()
        onward[cut].wait()
    local.wait()


def head_gather(x, collective_id, cuts=4):
    return pl.pallas_call(
        functools.partial(gather_kernel, cuts),
        in_specs=[pl.BlockSpec(memory_space=pl.ANY)],
        out_specs=pl.BlockSpec(memory_space=pl.ANY),
        out_shape=jax.ShapeDtypeStruct((4,) + x.shape, x.dtype),
        scratch_shapes=[
            pltpu.SemaphoreType.DMA, pltpu.SemaphoreType.DMA((3, cuts)),
            pltpu.SemaphoreType.DMA((3, cuts)),
        ],
        compiler_params=params(collective_id=collective_id, has_side_effects=True),
        name="head_gather",
    )(x)


def body(
    patches, cotangent, expert_ids, slot_pos, owners,
    tile_master, tile_first, tile_second,
    expert_up, up_first, up_second,
    expert_down, down_first, down_second,
    router, router_first, router_second,
    norm_params, norm_first, norm_second,
):
    tok_rows, width = patches.shape
    experts = router.shape[0]
    capacity = tok_rows // experts
    dp_count = lax.axis_size("dp")
    head_count = lax.axis_size("head")
    me_head = lax.axis_index("head")
    me_dp = lax.axis_index("dp")
    images = tok_rows // PATCH
    share = capacity // head_count
    own_slots = experts * share
    slot_count = tile_master.shape[0]

    owner_row = owners[0]
    tile_count = owner_row.shape[0]
    order_index = jnp.arange(tile_count, dtype=jnp.int32)
    same_owner = owner_row[:, None] == owner_row[None, :]
    earlier = order_index[None, :] < order_index[:, None]
    tile_rank = jnp.sum(jnp.where(same_owner & earlier, 1, 0), axis=1).astype(jnp.int32)
    tile_place = owner_row * slot_count + tile_rank
    src = (tile_place[:, None] * TILE + jnp.arange(TILE, dtype=jnp.int32)[None, :]).reshape(-1)

    up_low = expert_up[0].astype(LOW)
    down_low = expert_down[0].astype(LOW)
    up_all = lax.all_gather(up_low, "head", axis=0)
    down_all = lax.all_gather(down_low, "head", axis=0)

    ids, pos = expert_ids.T, slot_pos.T
    col = (pos // share) * own_slots + ids * share + lax.rem(pos, share)
    col = jnp.where(pos < capacity, col, tok_rows)
    col_rows = (col - me_head * own_slots).reshape(2, images, PATCH).transpose(1, 0, 2)
    col = col.T

    def to_experts(rows):
        rows = rows.reshape(experts, share, width)
        return lax.all_to_all(rows, "dp", 0, 0, tiled=True).reshape(own_slots, width)

    by_image = (images, PATCH, width)
    x_images = patches.reshape(by_image)
    w, xn, g_sent = prepare(
        tile_master.reshape(slot_count * TILE, width), x_images, cotangent.reshape(by_image),
        norm_params, src[:, None], col_rows, own_slots, dp_count,
    )
    g_rows = to_experts(g_sent)
    lse, sent, *saved, x1 = attention_forward(xn, w, x_images, norm_params, col_rows, own_slots)
    x1 = x1.reshape(tok_rows, width)
    rows = to_experts(sent)
    back, out, up_part, down_part, router_part = experts_both_ways(
        rows, g_rows, up_all, down_all, router.astype(LOW), me_dp
    )
    back_all = head_gather(to_experts(back), 3).reshape(tok_rows, width)
    x1_grad, second_sums = combine_backward(col, back_all, x1, cotangent, norm_params)
    padded, first_sums, input_low = attention_backward(
        x1_grad.reshape(by_image), w, xn, saved, lse, src[None, :], x_images, norm_params,
        dp_count * slot_count * TILE,
    )
    input_grad = input_low.reshape(tok_rows, width).astype(FULL)

    out_all = lax.all_gather(to_experts(out), "head", axis=0, tiled=True)
    block_out = combine_forward(col, out_all, x1)

    up_grad = lax.psum_scatter(up_part, "head", scatter_dimension=0).astype(FULL)
    down_grad = lax.psum_scatter(down_part, "head", scatter_dimension=0).astype(FULL)
    owned_grad = lax.psum_scatter(
        padded.reshape(dp_count * slot_count, TILE, width), "dp", scatter_dimension=0, tiled=True
    ).astype(FULL)

    small = jnp.concatenate(
        [router_part[:experts], first_sums[:2], second_sums[:2] * (1.0 / head_count)], axis=0
    )
    small = lax.psum(small, ("dp", "head"))
    router_total, norm_total = small[:experts], small[experts:]

    tile_new, tile_first_new, tile_second_new = adam_update(
        tile_master, tile_first, tile_second, owned_grad, rate_attention, decay_factor
    )
    up_new, up_first_new, up_second_new = adam_update(
        expert_up, up_first, up_second, up_grad[None], rate_up, decay_factor
    )
    down_new, down_first_new, down_second_new = adam_update(
        expert_down, down_first, down_second, down_grad[None], rate_down, decay_factor
    )
    router_new, router_first_new, router_second_new = adam_update(
        router, router_first, router_second, router_total, rate_router, decay_factor
    )
    norm_new, norm_first_new, norm_second_all = adam_update(
        norm_params, norm_first, norm_second, norm_total, rate_norm, 0.0
    )
    return (
        block_out,
        input_grad,
        tile_new,
        tile_first_new,
        tile_second_new,
        tile_new.astype(LOW),
        up_new,
        up_first_new,
        up_second_new,
        up_new.astype(LOW),
        down_new,
        down_first_new,
        down_second_new,
        down_new.astype(LOW),
        router_new,
        router_first_new,
        router_second_new,
        norm_new,
        norm_first_new,
        norm_second_all[:2],
        norm_second_all[2:],
    )


def solution(mesh):
    row = P("dp", None)
    tiles = P(("dp", "head"), None, None)
    up = P("dp", None, "head")
    down = P("dp", "head", None)
    in_specs = (
        row, row, row, row, P("head", None), tiles, tiles, tiles,
        up, up, up, down, down, down, P(), P(), P(), P(), P(), P(),
    )
    out_specs = (
        row, row, tiles, tiles, tiles, tiles, up, up, up, up, down, down, down, down,
        P(), P(), P(), P(), P(), P(), P(),
    )
    return jax.shard_map(body, mesh=mesh, in_specs=in_specs, out_specs=out_specs, check_vma=False)
```

time: 596 us -> 561 us (0.941)
  Pallas kernels: 299 us -> 255 us
  waiting for transfers between devices: 108 us -> 132 us
  other arithmetic: 45.7 us -> 38.2 us
  local copies, waits for them, and re-layouts: 21.8 us -> 15.6 us
    pallas_call x3 -> x1, Pallas kernels: 105 us -> 29.6 us  [head_gather(): pl.pallas_call(functools.partial(gather_kernel, cuts), in_specs=[pl.Block...]
    reduce_scatter x1, waiting for transfers between devices: 0.01 us -> 34.3 us  [body(): lax.psum_scatter(down_part, 'head', scatter_dimension=0).astype(FULL)]
    pallas_call x7 -> x3, Pallas kernels: 131 us -> 162 us  [the longest x1 60.9 us: attention_forward(): pl.pallas_call(forward_kernel, in_specs=[INSIDE, INSIDE, ANYWHERE, INSIDE...]
    all_gather x1 -> x0, waiting for transfers between devices: 28.7 us -> none  [body(): gathered = lax.all_gather(tile_master.astype(LOW), 'dp', axis=0, tiled=True)]
    all_gather x1, waiting for transfers between devices: 0.01 us -> 12.5 us  [body(): out_all = lax.all_gather(to_experts(out), 'head', axis=0, tiled=True)]
    reduce_scatter x1, waiting for transfers between devices: 35.3 us -> 43.2 us  [body(): lax.psum_scatter(up_part, 'head', scatter_dimension=0).astype(FULL)]
    convert_element_type x3 -> x1, other arithmetic: 10.5 us -> 3.74 us  [body(): input_grad = input_low.reshape(tok_rows, width).astype(FULL)]
  transfers between devices with their start and end apart: 10 -> 9, of which waited for: 4 -> 5; matrix products, arithmetic and copies ran while one was open for 9% -> 7% of each run, Pallas kernels for 33% -> 21%
where the time goes in v2:
time: 561 us; the launch traced here: 554 us
  Pallas kernels  255 us (45%)
  waiting for transfers between devices  132 us (24%)
  blocking collectives  84.8 us (15%)
  other arithmetic  38.2 us (7%)
  local copies, waits for them, and re-layouts  15.6 us (3%)
  between operations  14.6 us (3%)
  starting transfers between devices  14.2 us (3%)
    pallas_call x1, Pallas kernels, attention_forward(): pl.pallas_call(forward_kernel, in_specs=[INSIDE, INSIDE, ANYWHERE, INSIDE...  60.9 us
    pallas_call x1, Pallas kernels, attention_backward(): pl.pallas_call(backward_kernel, in_specs=[INSIDE] * 11 + [ANYWHERE, INSID...  60.7 us
    all_to_all x1, blocking collectives, to_experts(): lax.all_to_all(rows, 'dp', 0, 0, tiled=True).reshape(own_slots, width)  44.2 us
    reduce_scatter x1, waiting for transfers between devices, body(): lax.psum_scatter(up_part, 'head', scatter_dimension=0).astype(FULL)  43.2 us
    all_to_all x3, waiting for transfers between devices, to_experts(): lax.all_to_all(rows, 'dp', 0, 0, tiled=True).reshape(own_slots, width)  41.1 us
    pallas_call x1, Pallas kernels, prepare(): pl.pallas_call(prepare_kernel, in_specs=[INSIDE] * 6, out_specs=[INSIDE]...  40.6 us
    psum x1, blocking collectives, body(): small = lax.psum(small, ('dp', 'head'))  40.6 us
    reduce_scatter x1, waiting for transfers between devices, body(): lax.psum_scatter(down_part, 'head', scatter_dimension=0).astype(FULL)  34.3 us
  transfers between devices with their start and end apart: 9, of which 5 were waited for; matrix products, arithmetic and copies ran while one was open for 7% of the time, Pallas kernels for 21%

profile of v2, /device:TPU:0, one launch (start us, length us, event | category | flops | bytes accessed | tf_op | source)
XLA Modules:
  0.0 554.4 jit_solution(3988097167915036586)
XLA Ops:
  7.2 2.9 convert_element_type.39
  10.3 1.1 convert_element_type.40
  14.7 1.1 copy.105
  15.9 1.7 and_select_fusion
  17.5 1.6 copy.106
  19.2 1.4 broadcast_multiply_fusion
  21.7 1.9 fusion.8
  23.6 2.3 copy.111
  25.9 40.6 %prepare.1 = (bf16[768,768]{1,0:T(8,128)(2,1)}, bf16[4,576,768]{2,1,0:T(8,128)(2,1)}, bf16[576,768]{1,0:T(8,128)(2,1)}) custom-call(f32[192,768]{1,0:T(8,128)} %bitcast.51, bf16[4,576,768]{2,1,0:T(8,128)(2,1)} %bitcast.37, bf16[4,576,768]{2,1,0:T(8,128)(2,1)} %bitcast.42, f32[4,768]{1,0:T(4,128)} %norm_ref.7, s32[768,1]{1,0:T(8,128)} %add.168.src_ref, ...), custom_call_target="tpu_custom_call" | custom-call | tf_op jit(solution)/shard_map/prepare/pallas_call | solution.py:338
  66.5 3.8 all-to-all-start.1
  70.3 60.9 %attention_forward.1 = (f32[4,8,576]{2,1,0:T(8,128)}, bf16[576,768]{1,0:T(8,128)(2,1)}, bf16[4,576,192]{2,1,0:T(8,128)(2,1)}, bf16[4,192,576]{2,1,0:T(8,128)(2,1...) custom-call(bf16[4,576,768]{2,1,0:T(8,128)(2,1)} %get-tuple-element., ...), custom_call_target="tpu_custom_call" | custom-call | tf_op jit(solution)/shard_map/attention_forward/pallas_call | solution.py:450
  131.2 6.0 %all-to-all-start = ((bf16[8,72,768]{2,1,0:T(8,128)(2,1)}), bf16[8,72,768]{2,1,0:T(8,128)(2,1)S(1)}, u32[]{:S(2)}, u32[]{:S(2)}) async-start(bf16[8,72,768]{2,1,0:T(8,128)(2,1)} %bitcast.53), calls=%async_computation | async-start | bytes 1769472 | tf_op jit(solution)/shard_map/all_to_all | solution.py:806
  138.5 21.7 %all-to-all-done = bf16[8,72,768]{2,1,0:T(8,128)(2,1)S(1)} async-done(((bf16[8,72,768]{2,1,0:T(8,128)(2,1)}), bf16[8,72,768]{2,1,0:T(8,128)(2,1)S(1)}, u32[]{:S(2)}, u32[]{:S(2)}) %all-to-all-start) | async-done | bytes 884768 | tf_op jit(solution)/shard_map/all_to_all | solution.py:806
  161.1 27.4 %experts_both_ways.1 = (bf16[576,768]{1,0:T(8,128)(2,1)}, bf16[576,768]{1,0:T(8,128)(2,1)}, bf16[4,768,768]{2,1,0:T(8,128)(2,1)}, bf16[4,768,768]{2,1,0:T(8,128)(2,1)}, f32[128,768]{1,0:T(8,128)}) custom-call(bf16[576,768]{1,0:T(8,128)(2,1)} %bitcast.46, bf16[576,768]{1,0:T(8,128)(2,1)} %bitcast.45, ...), custom_call_target="tpu_custom_call" | custom-call | tf_op jit(solution)/shard_map/experts_both_ways/pallas_call | solution.py:687
  188.6 3.7 all-to-all-start.3
  193.8 1.5 add_select_fusion.1.col_ref
  195.4 19.4 %all-to-all-done.3 = bf16[8,72,768]{2,1,0:T(8,128)(2,1)S(1)} async-done(((bf16[8,72,768]{2,1,0:T(8,128)(2,1)}), bf16[8,72,768]{2,1,0:T(8,128)(2,1)S(1)}, u32[]{:S(2)}, u32[]{:S(2)}) %all-to-all-start.3) | async-done | bytes 884768 | tf_op jit(solution)/shard_map/all_to_all | solution.py:806
  215.6 29.6 %head_gather.1 = bf16[4,576,768]{2,1,0:T(8,128)(2,1)} custom-call(bf16[576,768]{1,0:T(8,128)(2,1)} %bitcast.48), custom_call_target="tpu_custom_call" | custom-call | tf_op jit(solution)/shard_map/head_gather/pallas_call | solution.py:750
  245.2 19.6 %combine_backward.1 = (bf16[2304,768]{1,0:T(8,128)(2,1)}, f32[8,768]{1,0:T(8,128)}) custom-call(s32[2304,2]{1,0:T(8,128)} %add_select_fusion.1.col_ref, bf16[2304,768]{1,0:T(8,128)(2,1)} %bitcast.43, bf16[2304,768]{1,0:T(8,128)(2,1)} %bitcast.40, bf16[2304,768]{1,0:T(8,128)(2,1)} %g_ref.1, f32[4,768]{1,0:T(4,128)} %norm_ref.7), custom_call_target="tpu_custom_call" | custom-call | tf_op jit(solution)/shard_map/combine_backward/pallas_call | solution.py:613
  264.9 60.7 %attention_backward.1 = (bf16[1536,768]{1,0:T(8,128)(2,1)}, f32[8,768]{1,0:T(8,128)}, bf16[4,576,768]{2,1,0:T(8,128)(2,1)}) custom-call(bf16[4,576,768]{2,1,0:T(8,128)(2,1)} %bitcast.49, bf16[768,768]{1,0:T(8,128)(2,1)} %get-tuple-element.56.w_ref, bf16[4,576,768]{2,1,0:T(8,128)(2,1)} %get-tuple-element.55.xn_ref, ...), custom_call_target="tpu_custom_call" | custom-call | tf_op jit(solution)/shard_map/attention_backward/pallas_call | solution.py:546
  326.7 44.2 %all_to_all.20 = bf16[8,72,768]{2,1,0:T(8,128)(2,1)} all-to-all(bf16[8,72,768]{2,1,0:T(8,128)(2,1)S(1)} %bitcast.52), channel_id=1, replica_groups=mesh['dp'=8,'head'=4] {'dp'}, dimensions={0} | all-to-all | bytes 1769472 | tf_op jit(solution)/shard_map/all_to_all | solution.py:806
  375.3 40.6 %psum.7 = f32[12,768]{1,0:T(8,128)} all-reduce(f32[12,768]{1,0:T(8,128)} %pad_maximum_fusion), channel_id=1, replica_groups=mesh['dp'=8,'head'=4] {'dp','head'}, use_global_device_ids=true, to_apply=%region_4.5 | all-reduce | flops 9216 | bytes 73728 | tf_op jit(solution)/shard_map/psum | solution.py:841
  415.9 1.4 multiply_subtract_fusion.4
  417.9 1.4 multiply_subtract_fusion.3
  419.3 3.7 bitcast_convert_fusion
  423.1 3.1 fusion.23
  426.2 12.5 %all-gather.8.cloned.1.call-done.held_ref = bf16[2304,768]{1,0:T(8,128)(2,1)} async-done(((bf16[576,768]{1,0:T(8,128)(2,1)}), bf16[2304,768]{1,0:T(8,128)(2,1)}) %all-gather.8.cloned.1.call-update) | async-done | bytes 3538960 | tf_op jit(solution)/shard_map/all_gather | solution.py:829
  438.7 15.9 %combine_forward.1 = bf16[2304,768]{1,0:T(8,128)(2,1)} custom-call(s32[2304,2]{1,0:T(8,128)} %add_select_fusion.1.col_ref, bf16[2304,768]{1,0:T(8,128)(2,1)} %all-gather.8.cloned.1.call-done.held_ref, bf16[2304,768]{1,0:T(8,128)(2,1)} %bitcast.41), custom_call_target="tpu_custom_call" | custom-call | tf_op jit(solution)/shard_map/combine_forward/pallas_call | solution.py:599
  454.7 34.3 %reduce-scatter.8.cloned.1.call-done = bf16[1,768,768]{2,1,0:T(8,128)(2,1)} async-done(((bf16[4,768,768]{2,1,0:T(8,128)(2,1)}), bf16[1,768,768]{2,1,0:T(8,128)(2,1)}) %reduce-scatter.8.cloned.1.call-update) | async-done | bytes 1179664 | tf_op jit(solution)/shard_map/reduce_scatter | solution.py:833
  489.0 7.3 %fusion.17 = (bf16[1,768,768]{2,1,0:T(8,128)(2,1)}, f32[1,768,768]{2,1,0:T(8,128)}, f32[1,768,768]{2,1,0:T(8,128)}, f32[1,768,768]{2,1,0:T(8,128)}) fusion(f32[1,768,768]{2,1,0:T(8,128)S(1)} %copy-done.1, bf16[1,768,768]{2,1,0:T(8,128)(2,1)} %reduce-scatter.8.cloned.1.call-done, f32[1,768,768]{2,1,0:T(8,128)} %param.34, f32[1,768,768]{2,1,0:T(8,128)} %param.35), kind=kLoop, calls=%fused_computation.49 | loop fusion | flops 10027008 | bytes 16515072 | tf_op jit(solution)/shard_map/convert_element_type | solution.py:873
  496.2 43.2 %reduce-scatter.6.cloned.1.call-done = bf16[1,768,768]{2,1,0:T(8,128)(2,1)} async-done(((bf16[4,768,768]{2,1,0:T(8,128)(2,1)}), bf16[1,768,768]{2,1,0:T(8,128)(2,1)}) %reduce-scatter.6.cloned.1.call-update) | async-done | bytes 1179664 | tf_op jit(solution)/shard_map/reduce_scatter | solution.py:832
  539.4 8.0 %fusion.20 = (bf16[1,768,768]{2,1,0:T(8,128)(2,1)}, f32[1,768,768]{2,1,0:T(8,128)}, f32[1,768,768]{2,1,0:T(8,128)}, f32[1,768,768]{2,1,0:T(8,128)}) fusion(f32[1,768,768]{2,1,0:T(8,128)} %param.30, bf16[1,768,768]{2,1,0:T(8,128)(2,1)} %reduce-scatter.6.cloned.1.call-done, f32[1,768,768]{2,1,0:T(8,128)} %param.31, f32[1,768,768]{2,1,0:T(8,128)} %param.32), kind=kLoop, calls=%fused_computation.50 | loop fusion | flops 10027008 | bytes 16515072 | tf_op jit(solution)/shard_map/convert_element_type | solution.py:869
  (62 shorter events, 15.2 us)
Async XLA Ops:
  7.2 3.1 copy-start
  7.2 153.0 %all-gather.4.cloned.1.call-start = ((), (), s32[]{:S(2)}) async-start(), calls=%async_computation.7 | async-start | bytes 5898240 | tf_op jit(solution)/shard_map/all_gather | solution.py:795
  10.2 1.2 copy-start.13
  10.2 3.0 copy-start.11
  10.2 150.0 %all-gather.6.cloned.1.call-start = ((), (), s32[]{:S(2)}) async-start(), calls=%async_computation.8 | async-start | bytes 5898240 | tf_op jit(solution)/shard_map/all_gather | solution.py:796
  11.7 0.6 copy-start.7
  66.5 64.7 %all-to-all-start.1 = ((bf16[8,72,768]{2,1,0:T(8,128)(2,1)}), bf16[8,72,768]{2,1,0:T(8,128)(2,1)S(1)}, u32[]{:S(2)}, u32[]{:S(2)}) async-start(bf16[8,72,768]{2,1,0:T(8,128)(2,1)} %bitcast.55), calls=%async_computation.1 | async-start | bytes 1769472 | tf_op jit(solution)/shard_map/all_to_all | solution.py:806
  70.3 67.0 %copy-start.10 = (f32[8,768]{1,0:T(8,128)S(1)}, f32[8,768]{1,0:T(8,128)}, u32[]{:S(2)}) copy-start(f32[8,768]{1,0:T(8,128)} %param.36) | copy-start | bytes 73732
  131.2 29.0 %copy-start.2 = (bf16[8,72,768]{2,1,0:T(8,128)(2,1)}, bf16[8,72,768]{2,1,0:T(8,128)(2,1)S(1)}, u32[]{:S(2)}) copy-start(bf16[8,72,768]{2,1,0:T(8,128)(2,1)S(1)} %all-to-all-done.1) | copy-start | bytes 2654212
  131.2 29.0 %all-to-all-start = ((bf16[8,72,768]{2,1,0:T(8,128)(2,1)}), bf16[8,72,768]{2,1,0:T(8,128)(2,1)S(1)}, u32[]{:S(2)}, u32[]{:S(2)}) async-start(bf16[8,72,768]{2,1,0:T(8,128)(2,1)} %bitcast.53), calls=%async_computation | async-start | bytes 1769472 | tf_op jit(solution)/shard_map/all_to_all | solution.py:806
  160.2 0.9 copy-start.3
  161.1 31.6 %copy-start.8 = (s32[96,8]{1,0:T(8,128)S(1)}, s32[96,8]{1,0:T(8,128)}, u32[]{:S(2)}) copy-start(s32[96,8]{1,0:T(8,128)} %copy-done.7) | copy-start | bytes 9220
  161.1 32.3 %copy-start.12 = (s32[2304,2]{0,1:T(2,128)S(1)}, s32[2304,2]{0,1:T(2,128)}, u32[]{:S(2)}) copy-start(s32[2304,2]{0,1:T(2,128)} %get-tuple-element.98) | copy-start | bytes 55300
  188.6 26.1 %all-to-all-start.3 = ((bf16[8,72,768]{2,1,0:T(8,128)(2,1)}), bf16[8,72,768]{2,1,0:T(8,128)(2,1)S(1)}, u32[]{:S(2)}, u32[]{:S(2)}) async-start(bf16[8,72,768]{2,1,0:T(8,128)(2,1)} %bitcast.54), calls=%async_computation.3 | async-start | bytes 1769472 | tf_op jit(solution)/shard_map/all_to_all | solution.py:806
  192.2 230.8 %reduce-scatter.4.cloned.1.call-start = ((), (), s32[]{:S(2)}) async-start(), calls=%async_computation.10 | async-start | bytes 2654208 | tf_op jit(solution)/shard_map/reduce_scatter | solution.py:834
  214.7 0.9 copy-start.5
  325.6 1.2 copy-start.6
  325.6 113.1 %all-gather.8.cloned.1.call-start = ((), (), s32[]{:S(2)}) async-start(), calls=%async_computation.9 | async-start | bytes 4423680 | tf_op jit(solution)/shard_map/all_gather | solution.py:829
  370.9 118.1 %reduce-scatter.8.cloned.1.call-start = ((), (), s32[]{:S(2)}) async-start(), calls=%async_computation.12 | async-start | bytes 5898240 | tf_op jit(solution)/shard_map/reduce_scatter | solution.py:833
  371.5 167.9 %reduce-scatter.6.cloned.1.call-start = ((), (), s32[]{:S(2)}) async-start(), calls=%async_computation.11 | async-start | bytes 5898240 | tf_op jit(solution)/shard_map/reduce_scatter | solution.py:832
  371.6 44.3 %copy-start.9 = (f32[4,768]{1,0:T(4,128)S(1)}, f32[4,768]{1,0:T(4,128)}, u32[]{:S(2)}) copy-start(f32[4,768]{1,0:T(4,128)} %norm_ref.7) | copy-start | bytes 36868
  371.6 47.7 %copy-start.4 = (bf16[4,576,768]{2,1,0:T(8,128)(2,1)S(1)}, bf16[4,576,768]{2,1,0:T(8,128)(2,1)}, u32[]{:S(2)}) copy-start(bf16[4,576,768]{2,1,0:T(8,128)(2,1)} %get-tuple-element.70) | copy-start | bytes 10616836
  426.2 62.8 %copy-start.1 = (f32[1,768,768]{2,1,0:T(8,128)S(1)}, f32[1,768,768]{2,1,0:T(8,128)}, u32[]{:S(2)}) copy-start(f32[1,768,768]{2,1,0:T(8,128)} %param.33) | copy-start | bytes 7077892
Sparse Core Ops, SparseCore 0:
  10.3 40.1 all-gather.3
  52.7 41.7 all-gather.5
  325.7 81.3 reduce-scatter.3
  408.5 30.1 all-gather.7
  441.1 47.8 reduce-scatter.7
  491.5 47.8 reduce-scatter.5

commit v3 on v2

--- a/solution.py
+++ b/solution.py
@@ -236,6 +236,190 @@
         pltpu.VMEM((2, PATCH, width), LOW), block, block, block,
         pltpu.VMEM((PATCH, width), FULL), block,
         pltpu.SemaphoreType.DMA((3,)), pltpu.SemaphoreType.DMA((3,)),
+    ]
+
+
+class LineScatter:
+    def __init__(
+        self, blocks, out, pair_in, up_in, down_in, total,
+        up_send, up_recv, down_send, down_recv, pair_send, pair_recv,
+    ):
+        self.blocks, self.out, self.total = blocks, out, total
+        self.arrived = (up_in, down_in, pair_in)
+        self.sems = ((up_send, up_recv), (down_send, down_recv), (pair_send, pair_recv))
+        self.length = blocks.shape[0] // 2
+        me = lax.axis_index("dp")
+        self.place, self.side = me // 2, lax.rem(me, 2)
+        self.targets = (
+            lax.rem(self.place + 1, self.length) * 2 + self.side,
+            lax.rem(self.place + self.length - 1, self.length) * 2 + self.side,
+            self.place * 2 + 1 - self.side,
+        )
+
+    def copy(self, way, block):
+        source = (
+            self.blocks.at[block * 2 + 1 - self.side] if way == 2 else self.total.at[block]
+        )
+        return remote(
+            source, self.arrived[way].at[block], *self.sems[way], block, "dp", self.targets[way]
+        )
+
+    def start(self):
+        @pl.loop(0, self.length)
+        def _(turn):
+            distance = self.length - 1 - turn
+
+            @pl.when(self.place + distance < self.length)
+            def _():
+                self.copy(2, self.place + distance).start()
+
+            @pl.when((self.place >= distance) & (distance > 0))
+            def _():
+                self.copy(2, self.place - distance).start()
+
+    def pair_sum(self, block):
+        self.copy(2, block).wait_recv()
+        own = self.blocks[block * 2 + self.side].astype(FULL)
+        return own + self.arrived[2][block].astype(FULL)
+
+    def forward(self, way, block, first):
+        both = self.pair_sum(block)
+
+        @pl.when(first)
+        def _():
+            self.total[block] = both.astype(LOW)
+
+        @pl.when(~first)
+        def _():
+            self.copy(way, block).wait_recv()
+            self.total[block] = (both + self.arrived[way][block].astype(FULL)).astype(LOW)
+
+        self.copy(way, block).start()
+
+    def step(self, distance):
+        @pl.when(self.place + distance < self.length)
+        def _():
+            self.forward(0, self.place + distance, self.place == 0)
+
+        @pl.when(self.place >= distance)
+        def _():
+            self.forward(1, self.place - distance, self.place == self.length - 1)
+
+    def result(self):
+        self.out[...] = self.pair_sum(self.place)
+
+        @pl.when(self.place > 0)
+        def _():
+            self.copy(0, self.place).wait_recv()
+            self.out[...] += self.arrived[0][self.place].astype(FULL)
+
+        @pl.when(self.place < self.length - 1)
+        def _():
+            self.copy(1, self.place).wait_recv()
+            self.out[...] += self.arrived[1][self.place].astype(FULL)
+
+    def finish(self):
+        @pl.loop(0, self.length)
+        def _(block):
+            self.copy(2, block).wait_send()
+
+            @pl.when(block > self.place)
+            def _():
+                self.copy(0, block).wait_send()
+
+            @pl.when(block < self.place)
+            def _():
+                self.copy(1, block).wait_send()
+
+
+def line_scatter_scratch(dp_count, rows, width):
+    line = dp_count // 2
+    return [pltpu.VMEM((line, rows, width), LOW)] * 4 + [pltpu.SemaphoreType.DMA((line,))] * 6
+
+
+class SmallSum:
+    def __init__(self, flat, head_in, dp_in, done, head_send, head_recv, dp_send, dp_recv):
+        self.flat, self.head_in, self.dp_in, self.done = flat, head_in, dp_in, done
+        self.head_sems, self.dp_sems = (head_send, head_recv), (dp_send, dp_recv)
+        self.me, *self.others = partners()
+        self.place, self.count = lax.axis_index("dp"), dp_in.shape[0]
+
+    def to_head(self, lane):
+        other = self.others[lane]
+        return remote(
+            self.flat.at[other], self.head_in.at[self.me], *self.head_sems, lane, "head", other
+        )
+
+    def back_head(self, lane):
+        block = self.done.at[self.me]
+        return remote(block, block, *self.head_sems, 3 + lane, "head", self.others[lane])
+
+    def to_dp(self, shift):
+        block = self.dp_in.at[self.place]
+        other = lax.rem(self.place + shift, self.count)
+        return remote(block, block, *self.dp_sems, shift, "dp", other)
+
+    def start(self, value):
+        groups, rows, lanes = self.flat.shape
+        flat = jnp.concatenate(
+            [value[:, at:at + lanes] for at in range(0, value.shape[1], lanes)], axis=0
+        )
+        for group in range(groups):
+            self.flat[group] = flat[group * rows:(group + 1) * rows]
+        for lane in range(3):
+            self.to_head(lane).start()
+        self.head_in[self.me] = self.flat[self.me]
+
+    def across(self):
+        for lane in range(3):
+            self.to_head(lane).wait_recv()
+        total = self.head_in[0]
+        for head in range(1, self.head_in.shape[0]):
+            total = total + self.head_in[head]
+        self.dp_in[self.place] = total
+
+        @pl.loop(1, self.count)
+        def _(shift):
+            self.to_dp(shift).start()
+
+    def back(self):
+        @pl.loop(1, self.count)
+        def _(shift):
+            self.to_dp(shift).wait_recv()
+
+        total = lax.fori_loop(
+            1, self.count, lambda at, so_far: so_far + self.dp_in[at], self.dp_in[0]
+        )
+        self.done[self.me] = total
+        for lane in range(3):
+            self.back_head(lane).start()
+
+    def result(self, out):
+        for lane in range(3):
+            self.back_head(lane).wait_recv()
+        flat = jnp.concatenate([self.done[group] for group in range(self.done.shape[0])], axis=0)
+        rows, width = out.shape
+        lanes = flat.shape[1]
+        for at in range(width // lanes):
+            out[:, at * lanes:(at + 1) * lanes] = flat[at * rows:(at + 1) * rows]
+
+    def finish(self):
+        for lane in range(3):
+            self.to_head(lane).wait_send()
+            self.back_head(lane).wait_send()
+
+        @pl.loop(1, self.count)
+        def _(shift):
+            self.to_dp(shift).wait_send()
+
+
+def small_sum_scratch(rows, width, dp_count):
+    block = (rows * width // 128 // 4, 128)
+    return [
+        pltpu.VMEM((4,) + block, FULL), pltpu.VMEM((4,) + block, FULL),
+        pltpu.VMEM((dp_count,) + block, FULL), pltpu.VMEM((4,) + block, FULL),
+        pltpu.SemaphoreType.DMA((6,)), pltpu.SemaphoreType.DMA((6,)),
+        pltpu.SemaphoreType.DMA((dp_count,)), pltpu.SemaphoreType.DMA((dp_count,)),
     ]
 
 
@@ -466,20 +650,41 @@
 
 
 def backward_kernel(
+    experts,
     x1g_ref, w_ref, xn_ref, q_ref, qt_ref, k_ref, kt_ref, v_ref, lse_ref, ot_ref, src_ref,
-    x_ref, norm_ref,
-    padded_ref, sums_ref, input_out,
-    grad_ref, own_ref, input_ref, own_sem, *exchange,
+    norm_ref, small_ref, col_ref, x_ref, out_rows_ref, x1_ref,
+    owned_ref, small_out, block_ref, input_out,
+    grad_ref, own_ref, input_ref, padded_ref, out_ref, own_sem, *exchange,
 ):
     images = x1g_ref.shape[0]
     rows = w_ref.shape[0] // 4
     heads = rows // HD
     total_of = ImageSum(*exchange[:8])
-    spread = ImageGather(input_ref, *exchange[8:])
+    spread = ImageGather(input_ref, *exchange[8:10])
+    spread_out = ImageGather(out_ref, *exchange[10:12])
+    weights_sum = LineScatter(padded_ref, owned_ref, *exchange[12:22])
+    small_sum = SmallSum(*exchange[22:])
     me, near, far, corner = partners()
-    greet(("head", near), ("head", far))
-    own = pltpu.make_async_copy(x_ref.at[me], own_ref, own_sem)
+    dp_count = padded_ref.shape[0]
+    place = lax.axis_index("dp")
+    barrier = pltpu.get_barrier_semaphore()
+    for other in (near, far, corner):
+        pl.semaphore_signal(barrier, inc=1, device_id={"head": other}, device_id_type=MESH)
+
+    @pl.loop(1, dp_count)
+    def _(shift):
+        other = lax.rem(place + shift, dp_count)
+        pl.semaphore_signal(barrier, inc=1, device_id={"dp": other}, device_id_type=MESH)
+
+    own = pltpu.make_async_copy(x_ref.at[me], own_ref, own_sem.at[0])
     own.start()
+    own_out = pltpu.make_async_copy(out_rows_ref, out_ref.at[me], own_sem.at[1])
+    own_out.start()
+    x1_copy = pltpu.make_async_copy(x1_ref, block_ref, own_sem.at[2])
+    x1_copy.start()
+    pl.semaphore_wait(barrier, dp_count + 2)
+    own_out.wait()
+    spread_out.start()
     shrink = HD ** (-0.5)
     grad_ref[...] = jnp.zeros_like(grad_ref)
 
@@ -516,71 +721,117 @@
         for part, piece in enumerate(pieces):
             grad_ref[pl.ds(part * rows, rows), :] += piece
 
+        @pl.when(turn == 2)
+        def _():
+            spread_out.wait_far()
+
     own.wait()
     normal, scale = normalise(own_ref[...].astype(FULL))
     back, gain_sum, shift_sum = norm_back(normal, scale, norm_ref[0:1, :], total_of.result())
-    sums_ref[...] = jnp.zeros_like(sums_ref)
-    sums_ref[0:1, :] = gain_sum
-    sums_ref[1:2, :] = shift_sum
     input_ref[me] = (x1g_ref[me].astype(FULL) + back).astype(LOW)
     spread.start()
     low = grad_ref[...].astype(LOW)
-    cut = padded_ref.shape[0] // 4
-    for part in range(4):
+    depth = padded_ref.shape[1]
+    parts = min(dp_count, 8)
+    cut = dp_count // parts * depth
+    for part in range(parts):
         row = lax.broadcasted_iota(jnp.int32, (cut, low.shape[0]), 0) + part * cut
         pick = one_hot(row == src_ref[...])
-        padded_ref[pl.ds(part * cut, cut), :] = nn(pick, low).astype(LOW)
+        block = nn(pick, low).astype(LOW)
+        padded_ref[pl.ds(part * (dp_count // parts), dp_count // parts)] = block.reshape(
+            dp_count // parts, depth, block.shape[1]
+        )
+    weights_sum.start()
+    small = small_ref[...]
+    row = lax.broadcasted_iota(jnp.int32, small.shape, 0)
+    small = small + jnp.where(row == experts, gain_sum, 0.0)
+    small_sum.start(small + jnp.where(row == experts + 1, shift_sum, 0.0))
+    spread_out.wait_near()
+    spread_out.wait_corner()
+    x1_copy.wait()
+    steps = weights_sum.length
+
+    @pl.loop(0, max(steps, images))
+    def _(turn):
+        @pl.when(turn < images)
+        def _():
+            mix = picked_rows(col_ref[turn], out_ref)
+            block_ref[turn] = (block_ref[turn].astype(FULL) + mix).astype(LOW)
+
+        @pl.when(turn < steps - 1)
+        def _():
+            weights_sum.step(steps - 1 - turn)
+
+        @pl.when(turn == 0)
+        def _():
+            small_sum.across()
+
+        @pl.when(turn == 1)
+        def _():
+            spread.wait_far()
+
+        @pl.when(turn == 2)
+        def _():
+            small_sum.back()
+
+    weights_sum.result()
+    small_sum.result(small_out)
     spread.wait_near()
-    spread.wait_far()
     spread.wait_corner()
-    keep = pltpu.make_async_copy(input_ref, input_out, own_sem)
+    keep = pltpu.make_async_copy(input_ref, input_out, own_sem.at[0])
     keep.start()
     spread.finish()
+    spread_out.finish()
     total_of.finish()
+    weights_sum.finish()
+    small_sum.finish()
     keep.wait()
 
 
-def attention_backward(x1_grad, w, xn, saved, lse, src_row, patches, norm_params, padded_rows):
+def attention_backward(
+    experts, dp_count, depth,
+    x1_grad, w, xn, saved, lse, src_row, norm_params, small, col, patches, out_rows, x1,
+):
     q, qt, k, kt, v, ot = saved
     images, _, width = patches.shape
     return pl.pallas_call(
-        backward_kernel,
-        in_specs=[INSIDE] * 11 + [ANYWHERE, INSIDE],
-        out_specs=[INSIDE, INSIDE, ANYWHERE],
+        functools.partial(backward_kernel, experts),
+        in_specs=[INSIDE] * 14 + [ANYWHERE] * 3,
+        out_specs=[INSIDE, INSIDE, INSIDE, ANYWHERE],
         out_shape=[
-            jax.ShapeDtypeStruct((padded_rows, width), LOW), jax.ShapeDtypeStruct((8, width), FULL),
-            jax.ShapeDtypeStruct(patches.shape, LOW),
+            jax.ShapeDtypeStruct((depth, width), FULL), jax.ShapeDtypeStruct(small.shape, FULL),
+            jax.ShapeDtypeStruct(patches.shape, LOW), jax.ShapeDtypeStruct(patches.shape, LOW),
         ],
         scratch_shapes=[
             pltpu.VMEM(w.shape, FULL), pltpu.VMEM((PATCH, width), LOW),
-            pltpu.VMEM(patches.shape, LOW), pltpu.SemaphoreType.DMA,
+            pltpu.VMEM(patches.shape, LOW), pltpu.VMEM((dp_count, depth, width), LOW),
+            pltpu.VMEM((4,) + out_rows.shape, LOW), pltpu.SemaphoreType.DMA((3,)),
         ]
-        + image_sum_scratch(width) + image_gather_sems(),
+        + image_sum_scratch(width) + image_gather_sems() + image_gather_sems()
+        + line_scatter_scratch(dp_count, depth, width)
+        + small_sum_scratch(small.shape[0], width, dp_count),
         compiler_params=params(collective_id=2, has_side_effects=True),
         name="attention_backward",
-    )(x1_grad, w, xn, q, qt, k, kt, v, lse, ot, src_row, patches, norm_params)
-
-
-def picked_rows(col_ref, held_ref):
-    tokens = col_ref.shape[0]
-    slots, width = held_ref.shape
-    cut = slots // 4
+    )(
+        x1_grad, w, xn, q, qt, k, kt, v, lse, ot, src_row, norm_params, small, col,
+        patches, out_rows, x1,
+    )
+
+
+def picked_rows(col, held_ref):
+    groups, cut, width = held_ref.shape
+    tokens = col.shape[0]
     total = jnp.zeros((tokens, width), FULL)
-    for part in range(4):
+    for part in range(groups):
         lanes = lax.broadcasted_iota(jnp.int32, (tokens, cut), 1) + part * cut
-        pick = one_hot((lanes == col_ref[:, 0:1]) | (lanes == col_ref[:, 1:2]))
-        total = total + nn(pick, held_ref[pl.ds(part * cut, cut), :])
+        pick = one_hot((lanes == col[:, 0:1]) | (lanes == col[:, 1:2]))
+        total = total + nn(pick, held_ref[part])
     return total
-
-
-def combine_front(col_ref, held_ref, x1_ref, out_ref):
-    mix = picked_rows(col_ref, held_ref)
-    out_ref[...] = (x1_ref[...].astype(FULL) + mix).astype(LOW)
 
 
 def combine_rear(col_ref, held_ref, x1_ref, g_ref, norm_ref, out_ref, sums_ref):
     step = pl.program_id(0)
-    upstream = picked_rows(col_ref, held_ref)
+    upstream = picked_rows(col_ref[...], held_ref)
     normal, scale = normalise(x1_ref[...].astype(FULL))
     back, gain_sum, shift_sum = norm_back(normal, scale, norm_ref[2:3, :], upstream)
     out_ref[...] = (g_ref[...].astype(FULL) + back).astype(LOW)
@@ -591,20 +842,6 @@
 
     sums_ref[0:1, :] += gain_sum
     sums_ref[1:2, :] += shift_sum
-
-
-def combine_forward(col, held, x1):
-    tokens, width = x1.shape
-    wide_spec = lead((PATCH, width))
-    return pl.pallas_call(
-        combine_front,
-        grid=(tokens // PATCH,),
-        in_specs=[lead((PATCH, 2)), whole(held.shape), wide_spec],
-        out_specs=wide_spec,
-        out_shape=jax.ShapeDtypeStruct((tokens, width), LOW),
-        compiler_params=params(),
-        name="combine_forward",
-    )(col, held, x1)
 
 
 def combine_backward(col, held, x1, cotangent, norm_params):
@@ -796,7 +1033,8 @@
     down_all = lax.all_gather(down_low, "head", axis=0)
 
     ids, pos = expert_ids.T, slot_pos.T
-    col = (pos // share) * own_slots + ids * share + lax.rem(pos, share)
+    holder = lax.div(pos, share)
+    col = holder * (own_slots - share) + ids * share + pos
     col = jnp.where(pos < capacity, col, tok_rows)
     col_rows = (col - me_head * own_slots).reshape(2, images, PATCH).transpose(1, 0, 2)
     col = col.T
@@ -818,28 +1056,28 @@
     back, out, up_part, down_part, router_part = experts_both_ways(
         rows, g_rows, up_all, down_all, router.astype(LOW), me_dp
     )
-    back_all = head_gather(to_experts(back), 3).reshape(tok_rows, width)
+    back_all = head_gather(to_experts(back), 3)
     x1_grad, second_sums = combine_backward(col, back_all, x1, cotangent, norm_params)
-    padded, first_sums, input_low = attention_backward(
-        x1_grad.reshape(by_image), w, xn, saved, lse, src[None, :], x_images, norm_params,
-        dp_count * slot_count * TILE,
-    )
+    small_rows = -(-(experts + 4) // 16) * 16
+    small = jnp.concatenate(
+        [
+            router_part[:experts], jnp.zeros((2, width), FULL),
+            second_sums[:2] * (1.0 / head_count),
+            jnp.zeros((small_rows - experts - 4, width), FULL),
+        ]
+    )
+    owned_grad, small, block_out, input_low = attention_backward(
+        experts, dp_count, slot_count * TILE,
+        x1_grad.reshape(by_image), w, xn, saved, lse, src[None, :], norm_params, small,
+        col.reshape(images, PATCH, 2), x_images, to_experts(out), x1.reshape(by_image),
+    )
+    block_out = block_out.reshape(tok_rows, width)
+    owned_grad = owned_grad.reshape(slot_count, TILE, width)
     input_grad = input_low.reshape(tok_rows, width).astype(FULL)
-
-    out_all = lax.all_gather(to_experts(out), "head", axis=0, tiled=True)
-    block_out = combine_forward(col, out_all, x1)
 
     up_grad = lax.psum_scatter(up_part, "head", scatter_dimension=0).astype(FULL)
     down_grad = lax.psum_scatter(down_part, "head", scatter_dimension=0).astype(FULL)
-    owned_grad = lax.psum_scatter(
-        padded.reshape(dp_count * slot_count, TILE, width), "dp", scatter_dimension=0, tiled=True
-    ).astype(FULL)
-
-    small = jnp.concatenate(
-        [router_part[:experts], first_sums[:2], second_sums[:2] * (1.0 / head_count)], axis=0
-    )
-    small = lax.psum(small, ("dp", "head"))
-    router_total, norm_total = small[:experts], small[experts:]
+    router_total, norm_total = small[:experts], small[experts:experts + 4]
 
     tile_new, tile_first_new, tile_second_new = adam_update(
         tile_master, tile_first, tile_second, owned_grad, rate_attention, decay_factor

time: 561 us -> 442 us (0.79)
  waiting for transfers between devices: 132 us -> 21.5 us
  Pallas kernels: 255 us -> 292 us
  blocking collectives: 84.8 us -> 55.1 us
  starting transfers between devices: 14.2 us -> 7.52 us
    reduce_scatter x1, waiting for transfers between devices: 43.2 us -> 0.01 us  [body(): lax.psum_scatter(up_part, 'head', scatter_dimension=0).astype(FULL)]
    psum x1 -> x0, blocking collectives: 40.6 us -> none  [body(): small = lax.psum(small, ('dp', 'head'))]
    reduce_scatter x1, waiting for transfers between devices: 34.3 us -> 0.01 us  [body(): lax.psum_scatter(down_part, 'head', scatter_dimension=0).astype(FULL)]
    pallas_call x2 -> x1, Pallas kernels: 76.6 us -> 99.3 us  [attention_backward(): pl.pallas_call(functools.partial(backward_kernel, experts), in_specs=[INS...]
    all_to_all x3 -> x2, waiting for transfers between devices: 41.1 us -> 20.9 us  [to_experts(): lax.all_to_all(rows, 'dp', 0, 0, tiled=True).reshape(own_slots, width)]
    pallas_call x1, Pallas kernels: 60.9 us -> 74.1 us  [attention_forward(): pl.pallas_call(forward_kernel, in_specs=[INSIDE, INSIDE, ANYWHERE, INSIDE...]
    all_gather x1 -> x0, waiting for transfers between devices: 12.5 us -> none  [body(): out_all = lax.all_gather(to_experts(out), 'head', axis=0, tiled=True)]
    all_to_all x1 -> x2, blocking collectives: 44.2 us -> 55.1 us  [to_experts(): lax.all_to_all(rows, 'dp', 0, 0, tiled=True).reshape(own_slots, width)]
  transfers between devices with their start and end apart: 9 -> 6, of which waited for: 5 -> 1; matrix products, arithmetic and copies ran while one was open for 7% -> 7% of each run, Pallas kernels for 21% -> 61%
where the time goes in v3:
time: 442 us; the launch traced here: 435 us
  Pallas kernels  292 us (66%)
  blocking collectives  55.1 us (12%)
  other arithmetic  33.2 us (8%)
  waiting for transfers between devices  21.5 us (5%)
  between operations  14.3 us (3%)
  local copies, waits for them, and re-layouts  10.8 us (2%)
  starting transfers between devices  7.52 us (2%)
    pallas_call x1, Pallas kernels, attention_backward(): pl.pallas_call(functools.partial(backward_kernel, experts), in_specs=[INS...  99.3 us
    pallas_call x1, Pallas kernels, attention_forward(): pl.pallas_call(forward_kernel, in_specs=[INSIDE, INSIDE, ANYWHERE, INSIDE...  74.1 us
    all_to_all x2, blocking collectives, to_experts(): lax.all_to_all(rows, 'dp', 0, 0, tiled=True).reshape(own_slots, width)  55.1 us
    pallas_call x1, Pallas kernels, prepare(): pl.pallas_call(prepare_kernel, in_specs=[INSIDE] * 6, out_specs=[INSIDE]...  40.9 us
    pallas_call x1, Pallas kernels, head_gather(): pl.pallas_call(functools.partial(gather_kernel, cuts), in_specs=[pl.Block...  30.3 us
    pallas_call x1, Pallas kernels, experts_both_ways(): pl.pallas_call(expert_kernel, grid=(parts,), in_specs=[wide_spec, wide_sp...  27.6 us
    all_to_all x2, waiting for transfers between devices, to_experts(): lax.all_to_all(rows, 'dp', 0, 0, tiled=True).reshape(own_slots, width)  20.9 us
    pallas_call x1, Pallas kernels, combine_backward(): pl.pallas_call(combine_rear, grid=(tokens // PATCH,), in_specs=[lead((PAT...  19.9 us
  transfers between devices with their start and end apart: 6, of which 1 were waited for; matrix products, arithmetic and copies ran while one was open for 7% of the time, Pallas kernels for 61%

profile of v3, /device:TPU:0, one launch (start us, length us, event | category | flops | bytes accessed | tf_op | source)
XLA Modules:
  0.0 434.7 jit_solution(16832412299136665143)
XLA Ops:
  7.2 2.9 convert_element_type.36
  10.3 1.1 convert_element_type.37
  11.9 0.6 broadcast_multiply_fusion
  13.5 1.0 copy.84
  14.8 0.9 add.162.src_ref
  15.7 40.9 %prepare.1 = (bf16[768,768]{1,0:T(8,128)(2,1)}, bf16[4,576,768]{2,1,0:T(8,128)(2,1)}, bf16[576,768]{1,0:T(8,128)(2,1)}) custom-call(f32[192,768]{1,0:T(8,128)} %bitcast.60, bf16[4,576,768]{2,1,0:T(8,128)(2,1)} %bitcast.47, bf16[4,576,768]{2,1,0:T(8,128)(2,1)} %bitcast.51, f32[4,768]{1,0:T(4,128)} %norm_ref.7, s32[768,1]{1,0:T(8,128)} %add.162.src_ref, ...), custom_call_target="tpu_custom_call" | custom-call | tf_op jit(solution)/shard_map/prepare/pallas_call | solution.py:522
  56.6 74.1 %attention_forward.1 = (f32[4,8,576]{2,1,0:T(8,128)}, bf16[576,768]{1,0:T(8,128)(2,1)}, bf16[4,576,192]{2,1,0:T(8,128)(2,1)}, bf16[4,192,576]{2,1,0:T(8,128)(2,1...) custom-call(bf16[4,576,768]{2,1,0:T(8,128)(2,1)} %get-tuple-element., ...), custom_call_target="tpu_custom_call" | custom-call | tf_op jit(solution)/shard_map/attention_forward/pallas_call | solution.py:634
  130.7 28.9 %all_to_all.20 = bf16[8,72,768]{2,1,0:T(8,128)(2,1)} all-to-all(bf16[8,72,768]{2,1,0:T(8,128)(2,1)} %bitcast.62), channel_id=1, replica_groups=mesh['dp'=8,'head'=4] {'dp'}, dimensions={0} | all-to-all | bytes 1769472 | tf_op jit(solution)/shard_map/all_to_all | solution.py:1044
  159.7 3.6 all-to-all-start.1
  163.3 0.7 scatter.4.router_ref
  164.5 20.9 %all-to-all-done.1 = bf16[8,72,768]{2,1,0:T(8,128)(2,1)S(1)} async-done(((bf16[8,72,768]{2,1,0:T(8,128)(2,1)}), bf16[8,72,768]{2,1,0:T(8,128)(2,1)S(1)}, u32[]{:S(2)}, u32[]{:S(2)}) %all-to-all-start.1) | async-done | bytes 884768 | tf_op jit(solution)/shard_map/all_to_all | solution.py:1044
  185.5 0.9 copy-done.2
  186.4 27.6 %experts_both_ways.1 = (bf16[576,768]{1,0:T(8,128)(2,1)}, bf16[576,768]{1,0:T(8,128)(2,1)}, bf16[4,768,768]{2,1,0:T(8,128)(2,1)}, bf16[4,768,768]{2,1,0:T(8,128)(2,1)}, f32[128,768]{1,0:T(8,128)}) custom-call(bf16[576,768]{1,0:T(8,128)(2,1)} %bitcast.54, bf16[576,768]{1,0:T(8,128)(2,1)} %bitcast.55, ...), custom_call_target="tpu_custom_call" | custom-call | tf_op jit(solution)/shard_map/experts_both_ways/pallas_call | solution.py:924
  214.7 0.6 copy-done.7
  215.3 26.2 %all_to_all.21 = bf16[8,72,768]{2,1,0:T(8,128)(2,1)} all-to-all(bf16[8,72,768]{2,1,0:T(8,128)(2,1)S(1)} %bitcast.61), channel_id=1, replica_groups=mesh['dp'=8,'head'=4] {'dp'}, dimensions={0} | all-to-all | bytes 1769472 | tf_op jit(solution)/shard_map/all_to_all | solution.py:1044
  241.5 3.8 all-to-all-start.3
  245.3 0.7 add.138.src_ref
  247.0 1.1 broadcast_select_fusion.col_ref
  248.1 0.7 slice.34
  248.9 30.3 %head_gather.1.held_ref = bf16[4,576,768]{2,1,0:T(8,128)(2,1)} custom-call(bf16[576,768]{1,0:T(8,128)(2,1)} %bitcast.59), custom_call_target="tpu_custom_call" | custom-call | tf_op jit(solution)/shard_map/head_gather/pallas_call | solution.py:987
  279.2 19.9 %combine_backward.1 = (bf16[2304,768]{1,0:T(8,128)(2,1)}, f32[8,768]{1,0:T(8,128)}) custom-call(s32[2304,2]{1,0:T(8,128)} %broadcast_select_fusion.col_ref, bf16[4,576,768]{2,1,0:T(8,128)(2,1)} %head_gather.1.held_ref, bf16[2304,768]{1,0:T(8,128)(2,1)} %bitcast.50, bf16[2304,768]{1,0:T(8,128)(2,1)} %g_ref.1, f32[4,768]{1,0:T(4,128)} %norm_ref.7), custom_call_target="tpu_custom_call" | custom-call | tf_op jit(solution)/shard_map/combine_backward/pallas_call | solution.py:850
  299.1 0.7 slice_multiply_fusion
  299.9 0.7 pad_maximum_fusion.small_ref
  300.6 0.9 copy-done.5
  301.5 99.3 %attention_backward.1 = (f32[192,768]{1,0:T(8,128)}, f32[16,768]{1,0:T(8,128)}, bf16[4,576,768]{2,1,0:T(8,128)(2,1)}, bf16[4,576,768]{2,1,0:T(8,128)(2,1)}) custom-call(bf16[4,576,768]{2,1,0:T(8,128)(2,1)} %bitcast.57, bf16[768,768]{1,0:T(8,128)(2,1)} %get-tuple-element.57.w_ref, bf16[4,576,768]{2,1,0:T(8,128)(2,1)} %get-tuple-element.56.xn_ref, ...), custom_call_target="tpu_custom_call" | custom-call | tf_op jit(solution)/shard_map/attention_backward/pallas_call | solution.py:797
  400.9 1.5 multiply_subtract_fusion.4
  403.0 1.4 multiply_subtract_fusion.3
  404.4 2.6 fusion.21
  407.1 3.7 bitcast_convert_fusion
  410.8 7.3 %fusion.18 = (bf16[1,768,768]{2,1,0:T(8,128)(2,1)}, f32[1,768,768]{2,1,0:T(8,128)}, f32[1,768,768]{2,1,0:T(8,128)}, f32[1,768,768]{2,1,0:T(8,128)}) fusion(f32[1,768,768]{2,1,0:T(8,128)S(1)} %copy-done, bf16[1,768,768]{2,1,0:T(8,128)(2,1)} %reduce-scatter.3.cloned.1.call-done, f32[1,768,768]{2,1,0:T(8,128)} %param.31, f32[1,768,768]{2,1,0:T(8,128)} %param.32), kind=kLoop, calls=%fused_computation.45 | loop fusion | flops 10027008 | bytes 16515072 | tf_op jit(solution)/shard_map/convert_element_type | solution.py:1107
  418.1 8.1 %fusion.15 = (bf16[1,768,768]{2,1,0:T(8,128)(2,1)}, f32[1,768,768]{2,1,0:T(8,128)}, f32[1,768,768]{2,1,0:T(8,128)}, f32[1,768,768]{2,1,0:T(8,128)}) fusion(f32[1,768,768]{2,1,0:T(8,128)} %param.33, bf16[1,768,768]{2,1,0:T(8,128)(2,1)} %reduce-scatter.5.cloned.1.call-done, f32[1,768,768]{2,1,0:T(8,128)} %param.34, f32[1,768,768]{2,1,0:T(8,128)} %param.35), kind=kLoop, calls=%fused_computation.44 | loop fusion | flops 10027008 | bytes 16515072 | tf_op jit(solution)/shard_map/convert_element_type | solution.py:1111
  426.1 1.8 copy.87
  (67 shorter events, 4.6 us)
Async XLA Ops:
  7.2 3.1 copy-start.1
  7.2 178.3 %all-gather.3.cloned.1.call-start = ((), (), s32[]{:S(2)}) async-start(), calls=%async_computation.6 | async-start | bytes 5898240 | tf_op jit(solution)/shard_map/all_gather | solution.py:1032
  10.2 1.2 copy-start.11
  10.2 1.7 copy-start.17
  10.2 175.2 %all-gather.5.cloned.1.call-start = ((), (), s32[]{:S(2)}) async-start(), calls=%async_computation.7 | async-start | bytes 5898240 | tf_op jit(solution)/shard_map/all_gather | solution.py:1033
  12.9 1.6 copy-start.20
  130.7 32.6 %copy-start.13 = (f32[8,768]{1,0:T(8,128)S(1)}, f32[8,768]{1,0:T(8,128)}, u32[]{:S(2)}) copy-start(f32[8,768]{1,0:T(8,128)} %param.36) | copy-start | bytes 73732
  159.7 25.8 %all-to-all-start.1 = ((bf16[8,72,768]{2,1,0:T(8,128)(2,1)}), bf16[8,72,768]{2,1,0:T(8,128)(2,1)S(1)}, u32[]{:S(2)}, u32[]{:S(2)}) async-start(bf16[8,72,768]{2,1,0:T(8,128)(2,1)} %bitcast.10), calls=%async_computation.1 | async-start | bytes 1769472 | tf_op jit(solution)/shard_map/all_to_all | solution.py:1044
  163.2 247.6 %reduce-scatter.3.cloned.1.call-start = ((), (), s32[]{:S(2)}) async-start(), calls=%async_computation.8 | async-start | bytes 5898240 | tf_op jit(solution)/shard_map/reduce_scatter | solution.py:1078
  185.5 0.9 copy-start.2
  214.0 204.0 %reduce-scatter.5.cloned.1.call-start = ((), (), s32[]{:S(2)}) async-start(), calls=%async_computation.9 | async-start | bytes 5898240 | tf_op jit(solution)/shard_map/reduce_scatter | solution.py:1079
  214.1 1.2 copy-start.7
  214.6 30.6 %copy-start.12 = (s32[2304,2]{0,1:T(2,128)S(1)}, s32[2304,2]{0,1:T(2,128)}, u32[]{:S(2)}) copy-start(s32[2304,2]{0,1:T(2,128)} %param.25) | copy-start | bytes 55300
  214.6 31.3 %copy-start.14 = (s32[2304,2]{0,1:T(2,128)S(1)}, s32[2304,2]{0,1:T(2,128)}, u32[]{:S(2)}) copy-start(s32[2304,2]{0,1:T(2,128)} %get-tuple-element.98) | copy-start | bytes 55300
  241.5 59.1 %all-to-all-start.3 = ((bf16[8,72,768]{2,1,0:T(8,128)(2,1)}), bf16[8,72,768]{2,1,0:T(8,128)(2,1)S(1)}, u32[]{:S(2)}, u32[]{:S(2)}) async-start(bf16[8,72,768]{2,1,0:T(8,128)(2,1)} %bitcast.17), calls=%async_computation.3 | async-start | bytes 1769472 | tf_op jit(solution)/shard_map/all_to_all | solution.py:1044
  300.6 0.9 copy-start.5
  301.5 99.4 %copy-start.10 = (f32[4,768]{1,0:T(4,128)S(1)}, f32[4,768]{1,0:T(4,128)}, u32[]{:S(2)}) copy-start(f32[4,768]{1,0:T(4,128)} %norm_ref.7) | copy-start | bytes 36868
  301.5 99.4 %copy-start.18 = (f32[4,768]{1,0:T(4,128)S(1)}, f32[4,768]{1,0:T(4,128)}, u32[]{:S(2)}) copy-start(f32[4,768]{1,0:T(4,128)} %param.40) | copy-start | bytes 36868
  301.5 99.4 %copy-start.19 = (f32[4,768]{1,0:T(4,128)S(1)}, f32[4,768]{1,0:T(4,128)}, u32[]{:S(2)}) copy-start(f32[4,768]{1,0:T(4,128)} %param.41) | copy-start | bytes 36868
  301.5 101.5 %copy-start.15 = (f32[8,768]{1,0:T(8,128)S(1)}, f32[8,768]{1,0:T(8,128)}, u32[]{:S(2)}) copy-start(f32[8,768]{1,0:T(8,128)} %param.37) | copy-start | bytes 73732
  301.5 101.5 %copy-start.16 = (f32[8,768]{1,0:T(8,128)S(1)}, f32[8,768]{1,0:T(8,128)}, u32[]{:S(2)}) copy-start(f32[8,768]{1,0:T(8,128)} %param.38) | copy-start | bytes 73732
  301.5 102.9 %copy-start.6 = (f32[24,8,768]{2,1,0:T(8,128)S(1)}, f32[24,8,768]{2,1,0:T(8,128)}, u32[]{:S(2)}) copy-start(f32[24,8,768]{2,1,0:T(8,128)} %param.27) | copy-start | bytes 1769476
  301.5 102.9 %copy-start.8 = (f32[24,8,768]{2,1,0:T(8,128)S(1)}, f32[24,8,768]{2,1,0:T(8,128)}, u32[]{:S(2)}) copy-start(f32[24,8,768]{2,1,0:T(8,128)} %param.28) | copy-start | bytes 1769476
  301.5 102.9 %copy-start.9 = (f32[24,8,768]{2,1,0:T(8,128)S(1)}, f32[24,8,768]{2,1,0:T(8,128)}, u32[]{:S(2)}) copy-start(f32[24,8,768]{2,1,0:T(8,128)} %param.29) | copy-start | bytes 1769476
  400.9 6.2 %copy-start.4 = (bf16[4,576,768]{2,1,0:T(8,128)(2,1)S(1)}, bf16[4,576,768]{2,1,0:T(8,128)(2,1)}, u32[]{:S(2)}) copy-start(bf16[4,576,768]{2,1,0:T(8,128)(2,1)} %get-tuple-element.74) | copy-start | bytes 10616836
  407.1 3.7 copy-start
  418.1 8.1 %copy-start.3 = (bf16[4,576,768]{2,1,0:T(8,128)(2,1)S(1)}, bf16[4,576,768]{2,1,0:T(8,128)(2,1)}, u32[]{:S(2)}) copy-start(bf16[4,576,768]{2,1,0:T(8,128)(2,1)} %get-tuple-element.73) | copy-start | bytes 10616836
Sparse Core Ops, SparseCore 0:
  10.3 40.1 all-gather.2
  52.7 55.1 all-gather.4
  214.2 52.8 reduce-scatter.2
  269.6 49.9 reduce-scatter.4

commit v4 on v3

--- a/solution.py
+++ b/solution.py
@@ -26,7 +26,7 @@
 LOW = jnp.bfloat16
 FULL = jnp.float32
 MESH = pl.DeviceIdType.MESH
-VMEM_BYTES = 56 * 1024 * 1024
+VMEM_BYTES = 60 * 1024 * 1024
 
 
 def adam_update(weight, moment_one, moment_two, gradient, step_rate, weight_decay):
@@ -467,21 +467,233 @@
     return [pltpu.SemaphoreType.DMA((3 * GATHER_CUTS,)), pltpu.SemaphoreType.DMA((3 * GATHER_CUTS,))]
 
 
+class Slots:
+    def __init__(self, count, share):
+        self.count, self.share = count, share
+        self.big = -(-share // 16) * 16
+        rest = 2 * share - self.big
+        self.small = rest if rest > 0 and rest % 16 == 0 else self.big
+        self.more = self.big - self.small
+        self.both = self.big + self.small
+        self.rows = count // 2 * self.both
+        self.turns = count // 4
+        self.phase_rows = self.turns * 2 * self.both
+
+    def size(self, source, head):
+        return self.small + self.more * ((head + source + 1) % 2)
+
+    def packed(self, source, head):
+        return (source // 2) * self.both + (source % 2) * self.size(0, head)
+
+    def row(self, source, head, shift):
+        first = self.size(source, 0) * (head % 2)
+        group = (head // 2) * self.turns * self.both + self.turns * first
+        return (
+            (shift // self.turns) * self.phase_rows + group
+            + (shift % self.turns) * self.size(source, head)
+        )
+
+    def holder(self, source, slot):
+        pair, within = slot // self.both, slot % self.both
+        first = self.size(source, 0)
+        second = jnp.where(within >= first, 1, 0)
+        return 2 * pair + second, within - second * first
+
+    def span(self, start, extra):
+        if extra:
+            return pl.ds(pl.multiple_of(start + self.small, 16), self.more)
+        return pl.ds(pl.multiple_of(start, 16), self.small)
+
+    def each(self, is_big, make, action):
+        getattr(make(False), action)()
+        if self.more:
+            @pl.when(is_big)
+            def _():
+                getattr(make(True), action)()
+
+
+class SlotExchange:
+    def __init__(self, slots, sent, rows, sends, recvs, local_sems):
+        self.slots, self.sent, self.rows = slots, sent, rows
+        self.sems, self.local_sems = (sends, recvs), local_sems
+        self.place, self.head = lax.axis_index("dp"), lax.axis_index("head")
+
+    def out(self, shift, action):
+        slots = self.slots
+        expert = lax.rem(self.place + shift, slots.count)
+        mine = slots.size(self.place, self.head)
+        at, to = expert * mine, slots.packed(self.place, self.head)
+        slots.each(mine > slots.small, lambda extra: remote(
+            self.sent.at[slots.span(at, extra)], self.rows.at[slots.span(to, extra)],
+            *self.sems, 2 * shift + int(extra), "dp", expert,
+        ), action)
+
+    def into(self, shift):
+        slots = self.slots
+        source = lax.rem(self.place + slots.count - shift, slots.count)
+        size = slots.size(source, self.head)
+        to = slots.packed(source, self.head)
+        slots.each(size > slots.small, lambda extra: remote(
+            self.sent.at[slots.span(0, extra)], self.rows.at[slots.span(to, extra)],
+            *self.sems, 2 * shift + int(extra), "dp", source,
+        ), "wait_recv")
+
+    def own(self, action):
+        slots = self.slots
+        mine = slots.size(self.place, self.head)
+        at, to = self.place * mine, slots.packed(self.place, self.head)
+        slots.each(mine > slots.small, lambda extra: pltpu.make_async_copy(
+            self.sent.at[slots.span(at, extra)], self.rows.at[slots.span(to, extra)],
+            self.local_sems.at[int(extra)],
+        ), action)
+
+    def start(self):
+        @pl.loop(1, self.slots.count)
+        def _(shift):
+            self.out(shift, "start")
+
+        self.own("start")
+
+    def finish(self):
+        @pl.loop(1, self.slots.count)
+        def _(shift):
+            self.into(shift)
+            self.out(shift, "wait_send")
+
+        self.own("wait")
+
+
+def slot_exchange_sems(count):
+    return [
+        pltpu.SemaphoreType.DMA((2 * count,)), pltpu.SemaphoreType.DMA((2 * count,)),
+        pltpu.SemaphoreType.DMA((2,)),
+    ]
+
+
+class ReturnGather:
+    def __init__(self, slots, rows, held, sends, recvs, local_sems):
+        self.slots, self.rows, self.held = slots, rows, held
+        self.sems, self.local_sems = (sends, recvs), local_sems
+        self.place = lax.axis_index("dp")
+        self.me, self.near, self.far, self.corner = partners()
+
+    def out(self, shift, action):
+        slots = self.slots
+        source = lax.rem(self.place + shift, slots.count)
+        size = slots.size(source, self.me)
+        at, to = slots.packed(source, self.me), slots.row(source, self.me, shift)
+        slots.each(size > slots.small, lambda extra: remote(
+            self.rows.at[slots.span(at, extra)], self.held.at[slots.span(to, extra)],
+            *self.sems, 2 * shift + int(extra), "dp", source,
+        ), action)
+
+    def own(self, action):
+        slots = self.slots
+        size = slots.size(self.place, self.me)
+        at, to = slots.packed(self.place, self.me), slots.row(self.place, self.me, 0)
+        slots.each(size > slots.small, lambda extra: pltpu.make_async_copy(
+            self.rows.at[slots.span(at, extra)], self.held.at[slots.span(to, extra)],
+            self.local_sems.at[int(extra)],
+        ), action)
+
+    def block(self, lane, head, shift, axis, other, action):
+        slots = self.slots
+        size = slots.size(self.place, head)
+        to = slots.row(self.place, head, shift)
+
+        def make(extra):
+            block = self.held.at[slots.span(to, extra)]
+            index = 2 * (lane * slots.count + shift) + int(extra)
+            return remote(block, block, *self.sems, index, axis, other)
+
+        slots.each(size > slots.small, make, action)
+
+    def start(self):
+        @pl.loop(1, self.slots.count)
+        def _(shift):
+            self.out(shift, "start")
+
+        self.own("start")
+
+    def relay(self, shift):
+        @pl.when(shift == 0)
+        def _():
+            self.own("wait")
+
+        @pl.when(shift > 0)
+        def _():
+            expert = lax.rem(self.place + self.slots.count - shift, self.slots.count)
+            self.block(0, self.me, shift, "dp", expert, "wait_recv")
+
+        self.block(1, self.me, shift, "head", self.far, "start")
+        self.block(2, self.me, shift, "head", self.near, "start")
+
+    def forward(self, shift):
+        self.block(1, self.far, shift, "head", self.far, "wait_recv")
+        self.block(3, self.far, shift, "head", self.near, "start")
+
+    def rest(self, shift):
+        self.block(2, self.near, shift, "head", self.near, "wait_recv")
+        self.block(3, self.corner, shift, "head", self.near, "wait_recv")
+
+    def of_phase(self, phase, action):
+        @pl.loop(0, self.slots.turns)
+        def _(turn):
+            action(phase * self.slots.turns + turn)
+
+    def finish(self):
+        @pl.loop(0, self.slots.count)
+        def _(shift):
+            @pl.when(shift > 0)
+            def _():
+                self.out(shift, "wait_send")
+
+            self.block(1, self.me, shift, "head", self.far, "wait_send")
+            self.block(2, self.me, shift, "head", self.near, "wait_send")
+            self.block(3, self.far, shift, "head", self.near, "wait_send")
+
+
+def return_gather_sems(count):
+    return [
+        pltpu.SemaphoreType.DMA((8 * count,)), pltpu.SemaphoreType.DMA((8 * count,)),
+        pltpu.SemaphoreType.DMA((2,)),
+    ]
+
+
+def greet_all(heads, dp_count):
+    barrier = pltpu.get_barrier_semaphore()
+    place = lax.axis_index("dp")
+    for other in heads:
+        pl.semaphore_signal(barrier, inc=1, device_id={"head": other}, device_id_type=MESH)
+
+    @pl.loop(1, dp_count)
+    def _(shift):
+        other = lax.rem(place + shift, dp_count)
+        pl.semaphore_signal(barrier, inc=1, device_id={"dp": other}, device_id_type=MESH)
+
+    pl.semaphore_wait(barrier, len(heads) + dp_count - 1)
+
+
 ANYWHERE = pl.BlockSpec(memory_space=pl.ANY)
 INSIDE = pl.BlockSpec(memory_space=pltpu.VMEM)
 
 
 def prepare_kernel(
-    tile_ref, x_ref, g_ref, norm_ref, src_ref, col_ref,
-    w_ref, xn_ref, sent_ref,
-    held, sent_sum, *sems,
+    tile_ref, x_ref, g_ref, norm_ref, src_ref, col_ref, up_ref,
+    w_ref, xn_ref, sent_ref, up_out,
+    held, sent_sum, local_sem, *sems,
 ):
     images = x_ref.shape[0]
-    gather = LineGather(held, *sems)
-    greet(*gather.neighbours())
+    gather = LineGather(held, *sems[:6])
+    spread = ImageGather(up_out, *sems[6:])
+    own = pltpu.make_async_copy(up_ref, up_out.at[spread.me], local_sem)
+    own.start()
     me = lax.axis_index("dp")
     held[me] = tile_ref[...].astype(LOW)
+    greet(*gather.neighbours(), ("head", spread.near), ("head", spread.far))
     gather.start()
+    own.wait()
+    spread.start()
 
     def image_step(image):
         normal, _ = normalise(x_ref[image].astype(FULL))
@@ -495,11 +707,11 @@
     sent_sum[...] = jnp.zeros_like(sent_sum)
     steps = gather.length - 1
 
-    @pl.loop(0, max(steps, images))
+    @pl.loop(0, max(steps, (images + 1) // 2))
     def _(turn):
-        @pl.when(turn < images)
-        def _():
-            image_step(turn)
+        @pl.loop(2 * turn, jnp.minimum(2 * turn + 2, images))
+        def _(image):
+            image_step(image)
 
         @pl.when(turn < steps)
         def _():
@@ -514,26 +726,32 @@
         lanes = lax.broadcasted_iota(jnp.int32, (rows, blocks * depth), 1)
         pick = one_hot(lanes == src_ref[block, :])
         w_ref[block, :] = nn(pick, held[...].reshape(blocks * depth, width)).astype(LOW)
-
-
-def prepare(tiles, patches, cotangent, norm_params, src_col, col_rows, slots, dp_count):
+    spread.wait_far()
+    spread.wait_near()
+    spread.wait_corner()
+    spread.finish()
+
+
+def prepare(tiles, patches, cotangent, norm_params, src_col, col_rows, up_low, slots, dp_count):
     images, _, width = patches.shape
     line = dp_count // 2
     return pl.pallas_call(
         prepare_kernel,
-        in_specs=[INSIDE] * 6,
-        out_specs=[INSIDE] * 3,
+        in_specs=[INSIDE] * 6 + [ANYWHERE],
+        out_specs=[INSIDE] * 3 + [ANYWHERE],
         out_shape=[
             jax.ShapeDtypeStruct((src_col.shape[0], width), LOW),
             jax.ShapeDtypeStruct(patches.shape, LOW),
             jax.ShapeDtypeStruct((slots, width), LOW),
+            jax.ShapeDtypeStruct((4,) + up_low.shape, LOW),
         ],
         scratch_shapes=[
             pltpu.VMEM((dp_count,) + tiles.shape, LOW), pltpu.VMEM((slots, width), FULL),
-        ] + [pltpu.SemaphoreType.DMA((line,))] * 6,
+            pltpu.SemaphoreType.DMA,
+        ] + [pltpu.SemaphoreType.DMA((line,))] * 6 + image_gather_sems(),
         compiler_params=params(collective_id=0, has_side_effects=True),
         name="prepare",
-    )(tiles, patches, cotangent, norm_params, src_col, col_rows)
+    )(tiles, patches, cotangent, norm_params, src_col, col_rows, up_low)
 
 
 def head_mask(shape, axis, head):
@@ -541,20 +759,27 @@
 
 
 def forward_kernel(
-    xn_ref, w_ref, x_ref, norm_ref, col_ref,
-    lse_ref, sent_ref, q_out, qt_out, k_out, kt_out, v_out, ot_out, x1_out,
-    q_ref, qt_ref, k_ref, kt_ref, v_ref, ot_ref, x1_ref, own_ref, sent_sum,
+    slots,
+    xn_ref, w_ref, norm_ref, col_ref, x_ref, g_sent_ref, down_ref,
+    lse_ref, q_out, qt_out, k_out, kt_out, v_out, ot_out, x1_out, rows_out, g_rows_out, down_out,
+    q_ref, qt_ref, k_ref, kt_ref, v_ref, ot_ref, x1_ref, own_ref, sent_ref, sent_sum,
     save_sems, own_sem, *exchange,
 ):
     images = xn_ref.shape[0]
     rows = w_ref.shape[0] // 4
     heads = rows // HD
     total_of = ImageSum(*exchange[:8])
-    spread = ImageGather(x1_ref, *exchange[8:])
+    spread = ImageGather(x1_ref, *exchange[8:10])
+    spread_down = ImageGather(down_out, *exchange[10:12])
+    send_g = SlotExchange(slots, g_sent_ref, g_rows_out, *exchange[12:15])
+    send_rows = SlotExchange(slots, sent_ref, rows_out, *exchange[15:])
     me, near, far, corner = partners()
-    greet(("head", near), ("head", far))
-    own = pltpu.make_async_copy(x_ref.at[me], own_ref, own_sem)
+    own = pltpu.make_async_copy(x_ref.at[me], own_ref, own_sem.at[0])
     own.start()
+    own_down = pltpu.make_async_copy(down_ref, down_out.at[me], own_sem.at[1])
+    own_down.start()
+    greet_all((near, far), slots.count)
+    send_g.start()
     kept = ((q_ref, q_out), (qt_ref, qt_out), (k_ref, k_out), (kt_ref, kt_out), (v_ref, v_out), (ot_ref, ot_out))
     shrink = HD ** (-0.5)
 
@@ -612,13 +837,22 @@
     spread.wait_far()
     place(far)
     spread.wait_corner()
-    keep = pltpu.make_async_copy(x1_ref, x1_out, own_sem)
+    keep = pltpu.make_async_copy(x1_ref, x1_out, own_sem.at[0])
     keep.start()
+    own_down.wait()
+    spread_down.start()
     place(corner)
     sent_ref[...] = sent_sum[...].astype(LOW)
+    send_rows.start()
     spread.finish()
     total_of.finish()
     keep.wait()
+    send_g.finish()
+    spread_down.wait_far()
+    spread_down.wait_near()
+    spread_down.wait_corner()
+    spread_down.finish()
+    send_rows.finish()
 
     @pl.loop(0, images)
     def _(image):
@@ -626,31 +860,34 @@
             copy.wait()
 
 
-def attention_forward(xn, w, patches, norm_params, col_rows, slots):
+def attention_forward(slots, xn, w, norm_params, col_rows, patches, g_sent, down_low):
     images, _, width = patches.shape
     rows = w.shape[0] // 4
     flat, turned = (images, PATCH, rows), (images, rows, PATCH)
     saved = [flat, turned, flat, turned, flat, turned, patches.shape]
+    outs = saved + [(slots.rows, width), (slots.rows, width), (4,) + down_low.shape]
+    most = slots.count * slots.big
     return pl.pallas_call(
-        forward_kernel,
-        in_specs=[INSIDE, INSIDE, ANYWHERE, INSIDE, INSIDE],
-        out_specs=[INSIDE, INSIDE] + [ANYWHERE] * 7,
-        out_shape=[
-            jax.ShapeDtypeStruct((images, 8, PATCH), FULL), jax.ShapeDtypeStruct((slots, width), LOW),
-        ] + [jax.ShapeDtypeStruct(shape, LOW) for shape in saved],
+        functools.partial(forward_kernel, slots),
+        in_specs=[INSIDE] * 4 + [ANYWHERE] * 3,
+        out_specs=[INSIDE] + [ANYWHERE] * 10,
+        out_shape=[jax.ShapeDtypeStruct((images, 8, PATCH), FULL)]
+        + [jax.ShapeDtypeStruct(shape, LOW) for shape in outs],
         scratch_shapes=[pltpu.VMEM(shape, LOW) for shape in saved]
         + [
-            pltpu.VMEM((PATCH, width), LOW), pltpu.VMEM((slots, width), FULL),
-            pltpu.SemaphoreType.DMA((6, images)), pltpu.SemaphoreType.DMA,
+            pltpu.VMEM((PATCH, width), LOW), pltpu.VMEM((most, width), LOW),
+            pltpu.VMEM((most, width), FULL),
+            pltpu.SemaphoreType.DMA((6, images)), pltpu.SemaphoreType.DMA((2,)),
         ]
-        + image_sum_scratch(width) + image_gather_sems(),
+        + image_sum_scratch(width) + image_gather_sems() + image_gather_sems()
+        + slot_exchange_sems(slots.count) + slot_exchange_sems(slots.count),
         compiler_params=params(collective_id=1, has_side_effects=True),
         name="attention_forward",
-    )(xn, w, patches, norm_params, col_rows)
+    )(xn, w, norm_params, col_rows, patches, g_sent, down_low)
 
 
 def backward_kernel(
-    experts,
+    experts, slots,
     x1g_ref, w_ref, xn_ref, q_ref, qt_ref, k_ref, kt_ref, v_ref, lse_ref, ot_ref, src_ref,
     norm_ref, small_ref, col_ref, x_ref, out_rows_ref, x1_ref,
     owned_ref, small_out, block_ref, input_out,
@@ -661,30 +898,17 @@
     heads = rows // HD
     total_of = ImageSum(*exchange[:8])
     spread = ImageGather(input_ref, *exchange[8:10])
-    spread_out = ImageGather(out_ref, *exchange[10:12])
-    weights_sum = LineScatter(padded_ref, owned_ref, *exchange[12:22])
-    small_sum = SmallSum(*exchange[22:])
+    back_out = ReturnGather(slots, out_rows_ref, out_ref, *exchange[10:13])
+    weights_sum = LineScatter(padded_ref, owned_ref, *exchange[13:23])
+    small_sum = SmallSum(*exchange[23:])
     me, near, far, corner = partners()
-    dp_count = padded_ref.shape[0]
-    place = lax.axis_index("dp")
-    barrier = pltpu.get_barrier_semaphore()
-    for other in (near, far, corner):
-        pl.semaphore_signal(barrier, inc=1, device_id={"head": other}, device_id_type=MESH)
-
-    @pl.loop(1, dp_count)
-    def _(shift):
-        other = lax.rem(place + shift, dp_count)
-        pl.semaphore_signal(barrier, inc=1, device_id={"dp": other}, device_id_type=MESH)
-
+    dp_count = slots.count
     own = pltpu.make_async_copy(x_ref.at[me], own_ref, own_sem.at[0])
     own.start()
-    own_out = pltpu.make_async_copy(out_rows_ref, out_ref.at[me], own_sem.at[1])
-    own_out.start()
-    x1_copy = pltpu.make_async_copy(x1_ref, block_ref, own_sem.at[2])
+    x1_copy = pltpu.make_async_copy(x1_ref, block_ref, own_sem.at[1])
     x1_copy.start()
-    pl.semaphore_wait(barrier, dp_count + 2)
-    own_out.wait()
-    spread_out.start()
+    greet_all((near, far, corner), dp_count)
+    back_out.start()
     shrink = HD ** (-0.5)
     grad_ref[...] = jnp.zeros_like(grad_ref)
 
@@ -721,9 +945,10 @@
         for part, piece in enumerate(pieces):
             grad_ref[pl.ds(part * rows, rows), :] += piece
 
-        @pl.when(turn == 2)
-        def _():
-            spread_out.wait_far()
+        @pl.when((turn == 1) | (turn == 2))
+        def _():
+            back_out.of_phase(2 * turn - 2, back_out.relay)
+            back_out.of_phase(2 * turn - 1, back_out.relay)
 
     own.wait()
     normal, scale = normalise(own_ref[...].astype(FULL))
@@ -746,8 +971,14 @@
     row = lax.broadcasted_iota(jnp.int32, small.shape, 0)
     small = small + jnp.where(row == experts, gain_sum, 0.0)
     small_sum.start(small + jnp.where(row == experts + 1, shift_sum, 0.0))
-    spread_out.wait_near()
-    spread_out.wait_corner()
+    @pl.loop(0, slots.count)
+    def _(shift):
+        back_out.forward(shift)
+
+    @pl.loop(0, slots.count)
+    def _(shift):
+        back_out.rest(shift)
+
     x1_copy.wait()
     steps = weights_sum.length
 
@@ -755,8 +986,10 @@
     def _(turn):
         @pl.when(turn < images)
         def _():
-            mix = picked_rows(col_ref[turn], out_ref)
-            block_ref[turn] = (block_ref[turn].astype(FULL) + mix).astype(LOW)
+            mix = block_ref[turn].astype(FULL)
+            for phase in range(4):
+                mix = mix + picked_rows(slots, col_ref[turn], out_ref, phase)
+            block_ref[turn] = mix.astype(LOW)
 
         @pl.when(turn < steps - 1)
         def _():
@@ -781,7 +1014,7 @@
     keep = pltpu.make_async_copy(input_ref, input_out, own_sem.at[0])
     keep.start()
     spread.finish()
-    spread_out.finish()
+    back_out.finish()
     total_of.finish()
     weights_sum.finish()
     small_sum.finish()
@@ -789,13 +1022,14 @@
 
 
 def attention_backward(
-    experts, dp_count, depth,
+    experts, slots, depth,
     x1_grad, w, xn, saved, lse, src_row, norm_params, small, col, patches, out_rows, x1,
 ):
     q, qt, k, kt, v, ot = saved
     images, _, width = patches.shape
+    dp_count = slots.count
     return pl.pallas_call(
-        functools.partial(backward_kernel, experts),
+        functools.partial(backward_kernel, experts, slots),
         in_specs=[INSIDE] * 14 + [ANYWHERE] * 3,
         out_specs=[INSIDE, INSIDE, INSIDE, ANYWHERE],
         out_shape=[
@@ -805,9 +1039,9 @@
         scratch_shapes=[
             pltpu.VMEM(w.shape, FULL), pltpu.VMEM((PATCH, width), LOW),
             pltpu.VMEM(patches.shape, LOW), pltpu.VMEM((dp_count, depth, width), LOW),
-            pltpu.VMEM((4,) + out_rows.shape, LOW), pltpu.SemaphoreType.DMA((3,)),
+            pltpu.VMEM((4 * slots.phase_rows, width), LOW), pltpu.SemaphoreType.DMA((2,)),
         ]
-        + image_sum_scratch(width) + image_gather_sems() + image_gather_sems()
+        + image_sum_scratch(width) + image_gather_sems() + return_gather_sems(dp_count)
         + line_scatter_scratch(dp_count, depth, width)
         + small_sum_scratch(small.shape[0], width, dp_count),
         compiler_params=params(collective_id=2, has_side_effects=True),
@@ -818,48 +1052,75 @@
     )
 
 
-def picked_rows(col, held_ref):
-    groups, cut, width = held_ref.shape
-    tokens = col.shape[0]
-    total = jnp.zeros((tokens, width), FULL)
-    for part in range(groups):
-        lanes = lax.broadcasted_iota(jnp.int32, (tokens, cut), 1) + part * cut
-        pick = one_hot((lanes == col[:, 0:1]) | (lanes == col[:, 1:2]))
-        total = total + nn(pick, held_ref[part])
-    return total
-
-
-def combine_rear(col_ref, held_ref, x1_ref, g_ref, norm_ref, out_ref, sums_ref):
-    step = pl.program_id(0)
-    upstream = picked_rows(col_ref[...], held_ref)
-    normal, scale = normalise(x1_ref[...].astype(FULL))
-    back, gain_sum, shift_sum = norm_back(normal, scale, norm_ref[2:3, :], upstream)
-    out_ref[...] = (g_ref[...].astype(FULL) + back).astype(LOW)
-
-    @pl.when(step == 0)
-    def _():
-        sums_ref[...] = jnp.zeros_like(sums_ref)
-
-    sums_ref[0:1, :] += gain_sum
-    sums_ref[1:2, :] += shift_sum
-
-
-def combine_backward(col, held, x1, cotangent, norm_params):
-    tokens, width = x1.shape
-    wide_spec = lead((PATCH, width))
+def picked_rows(slots, col, held_ref, phase):
+    start = phase * slots.phase_rows
+    lanes = lax.broadcasted_iota(jnp.int32, (col.shape[0], slots.phase_rows), 1) + start
+    pick = one_hot((lanes == col[:, 0:1]) | (lanes == col[:, 1:2]))
+    return nn(pick, held_ref[pl.ds(start, slots.phase_rows), :])
+
+
+def combine_kernel(
+    slots,
+    col_ref, x1_ref, g_ref, norm_ref, rows_ref,
+    out_ref, sums_ref,
+    held, total, *sems,
+):
+    images = x1_ref.shape[0]
+    back = ReturnGather(slots, rows_ref, held, *sems)
+    greet_all((back.near, back.far), slots.count)
+    back.start()
+    back.of_phase(0, back.relay)
+
+    @pl.loop(0, 4)
+    def _(phase):
+        back.of_phase(phase, back.forward)
+
+        @pl.when(phase < 3)
+        def _():
+            back.of_phase(phase + 1, back.relay)
+
+        back.of_phase(phase, back.rest)
+
+        @pl.loop(0, images)
+        def _(image):
+            part = picked_rows(slots, col_ref[image], held, phase)
+
+            @pl.when(phase == 0)
+            def _():
+                total[image] = part
+
+            @pl.when(phase > 0)
+            def _():
+                total[image] += part
+
+    sums_ref[...] = jnp.zeros_like(sums_ref)
+
+    @pl.loop(0, images)
+    def _(image):
+        normal, scale = normalise(x1_ref[image].astype(FULL))
+        result, gain_sum, shift_sum = norm_back(normal, scale, norm_ref[2:3, :], total[image])
+        out_ref[image] = (g_ref[image].astype(FULL) + result).astype(LOW)
+        sums_ref[0:1, :] += gain_sum
+        sums_ref[1:2, :] += shift_sum
+
+    back.finish()
+
+
+def combine_backward(slots, col, x1, cotangent, norm_params, rows):
+    images, _, width = x1.shape
     return pl.pallas_call(
-        combine_rear,
-        grid=(tokens // PATCH,),
-        in_specs=[
-            lead((PATCH, 2)), whole(held.shape), wide_spec, wide_spec, whole(norm_params.shape)
+        functools.partial(combine_kernel, slots),
+        in_specs=[INSIDE] * 4 + [ANYWHERE],
+        out_specs=[INSIDE] * 2,
+        out_shape=[
+            jax.ShapeDtypeStruct(x1.shape, LOW), jax.ShapeDtypeStruct((8, width), FULL)
         ],
-        out_specs=[wide_spec, whole((8, width))],
-        out_shape=[
-            jax.ShapeDtypeStruct((tokens, width), LOW), jax.ShapeDtypeStruct((8, width), FULL)
-        ],
-        compiler_params=params(),
+        scratch_shapes=[
+            pltpu.VMEM((4 * slots.phase_rows, width), LOW), pltpu.VMEM(x1.shape, FULL),
+        ] + return_gather_sems(slots.count),
+        compiler_params=params(collective_id=3, has_side_effects=True),
         name="combine_backward",
-    )(col, held, x1, cotangent, norm_params)
+    )(col, x1, cotangent, norm_params, rows)
 
 
 def expert_kernel(
@@ -949,55 +1210,6 @@
     )(rows, g_rows, up, down, router_wide, own_row, closed)
 
 
-def gather_kernel(cuts, x_ref, out_ref, local_sem, send_sem, recv_sem):
-    me, near, far, corner = partners()
-    greet(("head", near), ("head", far))
-    size = x_ref.shape[0] // cuts
-
-    def remote(src, dst, lane, index, other):
-        return pltpu.make_async_remote_copy(
-            src_ref=src, dst_ref=dst, send_sem=send_sem.at[lane, index],
-            recv_sem=recv_sem.at[lane, index], device_id={"head": other}, device_id_type=MESH,
-        )
-
-    local = pltpu.make_async_copy(x_ref, out_ref.at[me], local_sem)
-    local.start()
-    across, beside, onward = [], [], []
-    for cut in range(cuts):
-        span = pl.ds(cut * size, size)
-        across.append(remote(x_ref.at[span], out_ref.at[me, span], 0, cut, far))
-        across[-1].start()
-    for cut in range(cuts):
-        span = pl.ds(cut * size, size)
-        beside.append(remote(x_ref.at[span], out_ref.at[me, span], 1, cut, near))
-        beside[-1].start()
-    for cut in range(cuts):
-        span = pl.ds(cut * size, size)
-        across[cut].wait_recv()
-        onward.append(remote(out_ref.at[far, span], out_ref.at[far, span], 2, cut, near))
-        onward[-1].start()
-    for cut in range(cuts):
-        across[cut].wait_send()
-        beside[cut].wait()
-        onward[cut].wait()
-    local.wait()
-
-
-def head_gather(x, collective_id, cuts=4):
-    return pl.pallas_call(
-        functools.partial(gather_kernel, cuts),
-        in_specs=[pl.BlockSpec(memory_space=pl.ANY)],
-        out_specs=pl.BlockSpec(memory_space=pl.ANY),
-        out_shape=jax.ShapeDtypeStruct((4,) + x.shape, x.dtype),
-        scratch_shapes=[
-            pltpu.SemaphoreType.DMA, pltpu.SemaphoreType.DMA((3, cuts)),
-            pltpu.SemaphoreType.DMA((3, cuts)),
-        ],
-        compiler_params=params(collective_id=collective_id, has_side_effects=True),
-        name="head_gather",
-    )(x)
-
-
 def body(
     patches, cotangent, expert_ids, slot_pos, owners,
     tile_master, tile_first, tile_second,
@@ -1014,8 +1226,7 @@
     me_head = lax.axis_index("head")
     me_dp = lax.axis_index("dp")
     images = tok_rows // PATCH
-    share = capacity // head_count
-    own_slots = experts * share
+    slots = Slots(dp_count, capacity // head_count)
     slot_count = tile_master.shape[0]
 
     owner_row = owners[0]
@@ -1027,37 +1238,30 @@
     tile_place = owner_row * slot_count + tile_rank
     src = (tile_place[:, None] * TILE + jnp.arange(TILE, dtype=jnp.int32)[None, :]).reshape(-1)
 
-    up_low = expert_up[0].astype(LOW)
-    down_low = expert_down[0].astype(LOW)
-    up_all = lax.all_gather(up_low, "head", axis=0)
-    down_all = lax.all_gather(down_low, "head", axis=0)
-
     ids, pos = expert_ids.T, slot_pos.T
-    holder = lax.div(pos, share)
-    col = holder * (own_slots - share) + ids * share + pos
-    col = jnp.where(pos < capacity, col, tok_rows)
-    col_rows = (col - me_head * own_slots).reshape(2, images, PATCH).transpose(1, 0, 2)
-    col = col.T
-
-    def to_experts(rows):
-        rows = rows.reshape(experts, share, width)
-        return lax.all_to_all(rows, "dp", 0, 0, tiled=True).reshape(own_slots, width)
+    kept = pos < capacity
+    holder, within = slots.holder(me_dp, jnp.minimum(pos, capacity - 1))
+    size = slots.size(me_dp, me_head)
+    col_rows = jnp.where(kept & (holder == me_head), ids * size + within, -1)
+    col_rows = col_rows.reshape(2, images, PATCH).transpose(1, 0, 2)
+    shift = (me_dp + dp_count - ids) % dp_count
+    col = jnp.where(kept, slots.row(me_dp, holder, shift) + within, -1)
+    col = col.T.reshape(images, PATCH, 2)
 
     by_image = (images, PATCH, width)
-    x_images = patches.reshape(by_image)
-    w, xn, g_sent = prepare(
-        tile_master.reshape(slot_count * TILE, width), x_images, cotangent.reshape(by_image),
-        norm_params, src[:, None], col_rows, own_slots, dp_count,
-    )
-    g_rows = to_experts(g_sent)
-    lse, sent, *saved, x1 = attention_forward(xn, w, x_images, norm_params, col_rows, own_slots)
-    x1 = x1.reshape(tok_rows, width)
-    rows = to_experts(sent)
+    x_images, g_images = patches.reshape(by_image), cotangent.reshape(by_image)
+    w, xn, g_sent, up_all = prepare(
+        tile_master.reshape(slot_count * TILE, width), x_images, g_images, norm_params,
+        src[:, None], col_rows, expert_up[0].astype(LOW), slots.count * slots.big, dp_count,
+    )
+    lse, *saved, x1, rows, g_rows, down_all = attention_forward(
+        slots, xn, w, norm_params, col_rows, x_images, g_sent, expert_down[0].astype(LOW)
+    )
     back, out, up_part, down_part, router_part = experts_both_ways(
         rows, g_rows, up_all, down_all, router.astype(LOW), me_dp
     )
-    back_all = head_gather(to_experts(back), 3)
-    x1_grad, second_sums = combine_backward(col, back_all, x1, cotangent, norm_params)
+    x1_grad, second_sums = combine_backward(slots, col, x1, g_images, norm_params, back)
+
     small_rows = -(-(experts + 4) // 16) * 16
     small = jnp.concatenate(
         [
@@ -1067,9 +1271,8 @@
         ]
     )
     owned_grad, small, block_out, input_low = attention_backward(
-        experts, dp_count, slot_count * TILE,
-        x1_grad.reshape(by_image), w, xn, saved, lse, src[None, :], norm_params, small,
-        col.reshape(images, PATCH, 2), x_images, to_experts(out), x1.reshape(by_image),
+        experts, slots, slot_count * TILE,
+        x1_grad, w, xn, saved, lse, src[None, :], norm_params, small, col, x_images, out, x1,
     )
     block_out = block_out.reshape(tok_rows, width)
     owned_grad = owned_grad.reshape(slot_count, TILE, width)

time: 442 us -> 438 us (level)
  Pallas kernels: 292 us -> 375 us
  blocking collectives: 55.1 us -> 0 us
  waiting for transfers between devices: 21.5 us -> 0.69 us
  starting transfers between devices: 7.52 us -> 0.08 us
    pallas_call x5 -> x4, Pallas kernels: 265 us -> 348 us  [the longest x1 119 us: attention_backward(): pl.pallas_call(functools.partial(backward_kernel, experts, slots), in_spe...]
    all_to_all x2 -> x0, blocking collectives: 55.1 us -> none  [to_experts(): lax.all_to_all(rows, 'dp', 0, 0, tiled=True).reshape(own_slots, width)]
    all_to_all x2 -> x0, waiting for transfers between devices: 20.9 us -> none  [to_experts(): lax.all_to_all(rows, 'dp', 0, 0, tiled=True).reshape(own_slots, width)]
    all_to_all x2 -> x0, starting transfers between devices: 7.35 us -> none  [to_experts(): lax.all_to_all(rows, 'dp', 0, 0, tiled=True).reshape(own_slots, width)]
  transfers between devices with their start and end apart: 6 -> 2, of which waited for: 1 -> 0; matrix products, arithmetic and copies ran while one was open for 7% -> 5% of each run, Pallas kernels for 61% -> 43%
where the time goes in v4:
time: 438 us; the launch traced here: 432 us
  Pallas kernels  375 us (86%)
  other arithmetic  33.4 us (8%)
  between operations  14.4 us (3%)
  local copies, waits for them, and re-layouts  7.71 us (2%)
    pallas_call x1, Pallas kernels, attention_backward(): pl.pallas_call(functools.partial(backward_kernel, experts, slots), in_spe...  119 us
    pallas_call x1, Pallas kernels, attention_forward(): pl.pallas_call(functools.partial(forward_kernel, slots), in_specs=[INSIDE...  83.8 us
    pallas_call x1, Pallas kernels, prepare(): pl.pallas_call(prepare_kernel, in_specs=[INSIDE] * 6 + [ANYWHERE], out_sp...  76.3 us
    pallas_call x1, Pallas kernels, combine_backward(): pl.pallas_call(functools.partial(combine_kernel, slots), in_specs=[INSIDE...  68.3 us
    pallas_call x1, Pallas kernels, experts_both_ways(): pl.pallas_call(expert_kernel, grid=(parts,), in_specs=[wide_spec, wide_sp...  27.7 us
  transfers between devices with their start and end apart: 2, of which 0 were waited for; matrix products, arithmetic and copies ran while one was open for 5% of the time, Pallas kernels for 43%

profile of v4, /device:TPU:0, one launch (start us, length us, event | category | flops | bytes accessed | tf_op | source)
XLA Modules:
  0.0 431.6 jit_solution(9006662303502938423)
XLA Ops:
  7.3 0.5 compare_select_fusion.6
  7.8 1.0 fusion.8
  8.8 0.1 reshape.183
  8.8 0.6 copy.49
  9.5 0.9 select_reduce_fusion
  10.4 0.7 add_multiply_fusion
  11.1 0.1 iota_add_fusion
  11.1 0.9 add.279.src_ref
  12.0 2.8 convert_bitcast_fusion.1.up_ref
  14.8 1.1 convert_bitcast_fusion.down_ref
  16.0 0.7 scatter.4.router_ref
  16.7 76.3 %prepare.1 = (bf16[768,768]{1,0:T(8,128)(2,1)}, bf16[4,576,768]{2,1,0:T(8,128)(2,1)}, bf16[640,768]{1,0:T(8,128)(2,1)}, bf16[4,768,768]{2,1,0:T(8,128)(2,1)}) custom-call(f32[192,768]{1,0:T(8,128)} %bitcast.61, bf16[4,576,768]{2,1,0:T(8,128)(2,1)} %bitcast.53, bf16[4,576,768]{2,1,0:T(8,128)(2,1)} %bitcast.56, f32[4,768]{1,0:T(4,128)} %norm_ref.7, ...), custom_call_target="tpu_custom_call" | custom-call | tf_op jit(solution)/shard_map/prepare/pallas_call | solution.py:738
  93.0 83.8 %attention_forward.1 = (f32[4,8,576]{2,1,0:T(8,128)}, bf16[4,576,192]{2,1,0:T(8,128)(2,1)}, bf16[4,192,576]{2,1,0:T(8,128)(2,1)}, bf16[4,576,192]{2,1,0:T(8,128)...) custom-call(bf16[4,576,768]{2,1,0:T(8,128)(2,1)} %get-tuple-element., ...), custom_call_target="tpu_custom_call" | custom-call | tf_op jit(solution)/shard_map/attention_forward/pallas_call | solution.py:870
  176.7 27.7 %experts_both_ways.1 = (bf16[576,768]{1,0:T(8,128)(2,1)}, bf16[576,768]{1,0:T(8,128)(2,1)}, bf16[4,768,768]{2,1,0:T(8,128)(2,1)}, bf16[4,768,768]{2,1,0:T(8,128)(2,1)}, f32[128,768]{1,0:T(8,128)}) custom-call(bf16[576,768]{1,0:T(8,128)(2,1)} %get-tuple-element.63.rows_ref, bf16[576,768]{1,0:T(8,128)(2,1)} %get-tuple-element.64.g_ref, ...), custom_call_target="tpu_custom_call" | custom-call | tf_op jit(solution)/shard_map/experts_both_ways/pallas_call | solution.py:1185
  204.5 0.7 reduce-scatter.5.cloned.1.call-update
  205.2 0.7 add.255.src_ref
  205.9 0.3 fusion.22
  206.2 1.4 copy.45
  207.6 0.7 slice.34
  208.3 0.1 pad.4.clone
  208.4 68.3 %combine_backward.1 = (bf16[4,576,768]{2,1,0:T(8,128)(2,1)}, f32[8,768]{1,0:T(8,128)}) custom-call(s32[4,576,2]{2,1,0:T(8,128)} %bitcast.58, bf16[4,576,768]{2,1,0:T(8,128)(2,1)} %get-tuple-element.62.x1_ref, bf16[4,576,768]{2,1,0:T(8,128)(2,1)} %bitcast.57, f32[4,768]{1,0:T(4,128)} %norm_ref.7, bf16[576,768]{1,0:T(8,128)(2,1)} %get-tuple-element.67.rows_ref), custom_call_target="tpu_custom_call" | custom-call | tf_op jit(solution)/shard_map/combine_backward/pallas_call | solution.py:1111
  276.8 0.8 slice_multiply_fusion
  277.5 0.7 pad_maximum_fusion.small_ref
  278.3 119.2 %attention_backward.1 = (f32[192,768]{1,0:T(8,128)}, f32[16,768]{1,0:T(8,128)}, bf16[4,576,768]{2,1,0:T(8,128)(2,1)}, bf16[4,576,768]{2,1,0:T(8,128)(2,1)}) custom-call(bf16[4,576,768]{2,1,0:T(8,128)(2,1)} %get-tuple-element.68.x1g_ref, bf16[768,768]{1,0:T(8,128)(2,1)} %get-tuple-element.60.w_ref, bf16[4,576,768]{2,1,0:T(8,128)(2,1)} %get-tuple-element.59.xn_ref, ...), custom_call_target="tpu_custom_call" | custom-call | tf_op jit(solution)/shard_map/attention_backward/pallas_call | solution.py:1031
  397.5 1.5 multiply_subtract_fusion.4
  399.0 0.6 fusion.35
  399.6 1.4 multiply_subtract_fusion.3
  401.0 2.6 fusion.32
  403.6 3.7 bitcast_convert_fusion
  407.4 7.3 %fusion.29 = (bf16[1,768,768]{2,1,0:T(8,128)(2,1)}, f32[1,768,768]{2,1,0:T(8,128)}, f32[1,768,768]{2,1,0:T(8,128)}, f32[1,768,768]{2,1,0:T(8,128)}) fusion(f32[1,768,768]{2,1,0:T(8,128)S(1)} %copy-done, bf16[1,768,768]{2,1,0:T(8,128)(2,1)} %reduce-scatter.3.cloned.1.call-done, f32[1,768,768]{2,1,0:T(8,128)} %param.31, f32[1,768,768]{2,1,0:T(8,128)} %param.32), kind=kLoop, calls=%fused_computation.81 | loop fusion | flops 10027008 | bytes 16515072 | tf_op jit(solution)/shard_map/convert_element_type | solution.py:1310
  414.6 8.1 %fusion.26 = (bf16[1,768,768]{2,1,0:T(8,128)(2,1)}, f32[1,768,768]{2,1,0:T(8,128)}, f32[1,768,768]{2,1,0:T(8,128)}, f32[1,768,768]{2,1,0:T(8,128)}) fusion(f32[1,768,768]{2,1,0:T(8,128)} %param.33, bf16[1,768,768]{2,1,0:T(8,128)(2,1)} %reduce-scatter.5.cloned.1.call-done, f32[1,768,768]{2,1,0:T(8,128)} %param.34, f32[1,768,768]{2,1,0:T(8,128)} %param.35), kind=kLoop, calls=%fused_computation.80 | loop fusion | flops 10027008 | bytes 16515072 | tf_op jit(solution)/shard_map/convert_element_type | solution.py:1314
  422.7 1.8 copy.51
  (38 shorter events, 0.2 us)
Async XLA Ops:
  7.2 7.7 %copy-start.1 = (f32[1,768,768]{2,1,0:T(8,128)S(1)}, f32[1,768,768]{2,1,0:T(8,128)}, u32[]{:S(2)}) copy-start(f32[1,768,768]{2,1,0:T(8,128)} %param.33) | copy-start | bytes 7077892
  7.2 400.2 %reduce-scatter.3.cloned.1.call-start = ((), (), s32[]{:S(2)}) async-start(), calls=%async_computation.2 | async-start | bytes 5898240 | tf_op jit(solution)/shard_map/reduce_scatter | solution.py:1281
  14.8 1.1 copy-start.8
  204.4 210.2 %reduce-scatter.5.cloned.1.call-start = ((), (), s32[]{:S(2)}) async-start(), calls=%async_computation.3 | async-start | bytes 5898240 | tf_op jit(solution)/shard_map/reduce_scatter | solution.py:1282
  204.5 1.4 copy-start.9
  204.5 1.4 copy-start.10
  278.2 119.2 %copy-start.7 = (f32[4,768]{1,0:T(4,128)S(1)}, f32[4,768]{1,0:T(4,128)}, u32[]{:S(2)}) copy-start(f32[4,768]{1,0:T(4,128)} %norm_ref.7) | copy-start | bytes 36868
  278.2 119.2 %copy-start.13 = (f32[4,768]{1,0:T(4,128)S(1)}, f32[4,768]{1,0:T(4,128)}, u32[]{:S(2)}) copy-start(f32[4,768]{1,0:T(4,128)} %param.40) | copy-start | bytes 36868
  278.2 119.3 %copy-start.14 = (f32[4,768]{1,0:T(4,128)S(1)}, f32[4,768]{1,0:T(4,128)}, u32[]{:S(2)}) copy-start(f32[4,768]{1,0:T(4,128)} %param.41) | copy-start | bytes 36868
  278.2 121.4 %copy-start.11 = (f32[8,768]{1,0:T(8,128)S(1)}, f32[8,768]{1,0:T(8,128)}, u32[]{:S(2)}) copy-start(f32[8,768]{1,0:T(8,128)} %param.37) | copy-start | bytes 73732
  278.2 121.4 %copy-start.12 = (f32[8,768]{1,0:T(8,128)S(1)}, f32[8,768]{1,0:T(8,128)}, u32[]{:S(2)}) copy-start(f32[8,768]{1,0:T(8,128)} %param.38) | copy-start | bytes 73732
  278.2 122.8 %copy-start.4 = (f32[24,8,768]{2,1,0:T(8,128)S(1)}, f32[24,8,768]{2,1,0:T(8,128)}, u32[]{:S(2)}) copy-start(f32[24,8,768]{2,1,0:T(8,128)} %param.27) | copy-start | bytes 1769476
  278.3 122.7 %copy-start.5 = (f32[24,8,768]{2,1,0:T(8,128)S(1)}, f32[24,8,768]{2,1,0:T(8,128)}, u32[]{:S(2)}) copy-start(f32[24,8,768]{2,1,0:T(8,128)} %param.28) | copy-start | bytes 1769476
  278.3 122.7 %copy-start.6 = (f32[24,8,768]{2,1,0:T(8,128)S(1)}, f32[24,8,768]{2,1,0:T(8,128)}, u32[]{:S(2)}) copy-start(f32[24,8,768]{2,1,0:T(8,128)} %param.29) | copy-start | bytes 1769476
  397.4 6.2 %copy-start.3 = (bf16[4,576,768]{2,1,0:T(8,128)(2,1)S(1)}, bf16[4,576,768]{2,1,0:T(8,128)(2,1)}, u32[]{:S(2)}) copy-start(bf16[4,576,768]{2,1,0:T(8,128)(2,1)} %get-tuple-element.80) | copy-start | bytes 10616836
  403.6 3.7 copy-start
  414.6 8.1 %copy-start.2 = (bf16[4,576,768]{2,1,0:T(8,128)(2,1)S(1)}, bf16[4,576,768]{2,1,0:T(8,128)(2,1)}, u32[]{:S(2)}) copy-start(bf16[4,576,768]{2,1,0:T(8,128)(2,1)} %get-tuple-element.79) | copy-start | bytes 10616836
Sparse Core Ops, SparseCore 0:
  204.6 62.3 reduce-scatter.2
  269.6 60.5 reduce-scatter.4

commit v5 on v4

--- a/solution.py
+++ b/solution.py
@@ -230,11 +230,11 @@
         self.to_far().wait_send()
 
 
-def image_sum_scratch(width):
-    block = pltpu.VMEM((PATCH, width), LOW)
+def image_sum_scratch(rows, width):
+    block = pltpu.VMEM((rows, width), LOW)
     return [
-        pltpu.VMEM((2, PATCH, width), LOW), block, block, block,
-        pltpu.VMEM((PATCH, width), FULL), block,
+        pltpu.VMEM((2, rows, width), LOW), block, block, block,
+        pltpu.VMEM((rows, width), FULL), block,
         pltpu.SemaphoreType.DMA((3,)), pltpu.SemaphoreType.DMA((3,)),
     ]
 
@@ -427,44 +427,99 @@
 
 
 class ImageGather:
-    def __init__(self, held, sends, recvs):
+    def __init__(self, held, sends, recvs, own=None, local_sem=None):
         self.held, self.sends, self.recvs = held, sends, recvs
         self.me, self.near, self.far, self.corner = partners()
+        self.own = held.at[self.me] if own is None else own
+        self.local = None if own is None else pltpu.make_async_copy(own, held.at[self.me], local_sem)
         self.size = held.shape[1] // GATHER_CUTS
 
-    def piece(self, image, cut, lane, other):
+    def piece(self, lane, cut):
         span = pl.ds(cut * self.size, self.size)
+        image = self.far if lane == 2 else self.me
         block = self.held.at[image, span]
-        return remote(block, block, self.sends, self.recvs, lane * GATHER_CUTS + cut, "head", other)
+        source = block if lane == 2 else self.own.at[span]
+        other = self.far if lane == 0 else self.near
+        index = lane * GATHER_CUTS + cut
+        return remote(source, block, self.sends, self.recvs, index, "head", other)
+
+    def start_far(self, first=0, last=GATHER_CUTS):
+        for cut in range(first, last):
+            self.piece(0, cut).start()
+
+    def start_near(self):
+        for cut in range(GATHER_CUTS):
+            self.piece(1, cut).start()
+        if self.local is not None:
+            self.local.start()
 
     def start(self):
-        for cut in range(GATHER_CUTS):
-            self.piece(self.me, cut, 0, self.far).start()
-        for cut in range(GATHER_CUTS):
-            self.piece(self.me, cut, 1, self.near).start()
+        self.start_far()
+        self.start_near()
 
     def wait_near(self):
         for cut in range(GATHER_CUTS):
-            self.piece(self.me, cut, 1, self.near).wait_recv()
+            self.piece(1, cut).wait_recv()
 
     def wait_far(self):
         for cut in range(GATHER_CUTS):
-            self.piece(self.me, cut, 0, self.far).wait_recv()
-            self.piece(self.far, cut, 2, self.near).start()
+            self.piece(0, cut).wait_recv()
+            self.piece(2, cut).start()
 
     def wait_corner(self):
         for cut in range(GATHER_CUTS):
-            self.piece(self.far, cut, 2, self.near).wait_recv()
+            self.piece(2, cut).wait_recv()
 
     def finish(self):
         for cut in range(GATHER_CUTS):
-            self.piece(self.me, cut, 0, self.far).wait_send()
-            self.piece(self.me, cut, 1, self.near).wait_send()
-            self.piece(self.far, cut, 2, self.near).wait_send()
+            for lane in range(3):
+                self.piece(lane, cut).wait_send()
+        if self.local is not None:
+            self.local.wait()
 
 
 def image_gather_sems():
     return [pltpu.SemaphoreType.DMA((3 * GATHER_CUTS,)), pltpu.SemaphoreType.DMA((3 * GATHER_CUTS,))]
+
+
+class BlockSum:
+    def __init__(self, parts, mine, passed, corner_in, near_in, far_in, local_sems, sends, recvs):
+        self.mine, self.passed, self.corner_in = mine, passed, corner_in
+        self.near_in, self.far_in = near_in, far_in
+        me, near, far, corner = partners()
+        self.to_corner = remote(parts.at[corner], corner_in, sends, recvs, 0, "head", near)
+        self.to_near = remote(parts.at[near], near_in, sends, recvs, 1, "head", near)
+        self.to_far = remote(passed, far_in, sends, recvs, 2, "head", far)
+        self.load_far = pltpu.make_async_copy(parts.at[far], passed, local_sems.at[0])
+        self.load_mine = pltpu.make_async_copy(parts.at[me], mine, local_sems.at[1])
+
+    def start(self):
+        for copy in (self.to_corner, self.load_far, self.to_near, self.load_mine):
+            copy.start()
+
+    def across(self):
+        self.load_far.wait()
+        self.to_corner.wait_recv()
+        both = self.passed[...].astype(FULL) + self.corner_in[...].astype(FULL)
+        self.passed[...] = both.astype(LOW)
+        self.to_far.start()
+
+    def result(self):
+        self.load_mine.wait()
+        self.to_near.wait_recv()
+        self.to_far.wait_recv()
+        total = self.mine[...].astype(FULL) + self.near_in[...].astype(FULL)
+        return total + self.far_in[...].astype(FULL)
+
+    def finish(self):
+        for copy in (self.to_corner, self.to_near, self.to_far):
+            copy.wait_send()
+
+
+def block_sum_scratch(rows, width):
+    return [pltpu.VMEM((rows, width), LOW)] * 5 + [
+        pltpu.SemaphoreType.DMA((2,)), pltpu.SemaphoreType.DMA((3,)), pltpu.SemaphoreType.DMA((3,)),
+    ]
 
 
 class Slots:
@@ -563,6 +618,76 @@
         self.own("wait")
 
 
+class SlotReturn:
+    def __init__(self, slots, rows, back, zeros, sends, recvs, local_sems):
+        self.slots, self.rows, self.back, self.zeros = slots, rows, back, zeros
+        self.sems, self.local_sems = (sends, recvs), local_sems
+        self.place, self.head = lax.axis_index("dp"), lax.axis_index("head")
+        self.mine = slots.size(self.place, self.head)
+
+    def out(self, shift, action):
+        slots = self.slots
+        source = lax.rem(self.place + shift, slots.count)
+        size = slots.size(source, self.head)
+        at, to = slots.packed(source, self.head), shift * size
+        slots.each(size > slots.small, lambda extra: remote(
+            self.rows.at[slots.span(at, extra)], self.back.at[slots.span(to, extra)],
+            *self.sems, 2 * shift + int(extra), "dp", source,
+        ), action)
+
+    def into(self, shift):
+        slots = self.slots
+        expert = lax.rem(self.place + slots.count - shift, slots.count)
+        slots.each(self.mine > slots.small, lambda extra: remote(
+            self.rows.at[slots.span(0, extra)], self.back.at[slots.span(shift * self.mine, extra)],
+            *self.sems, 2 * shift + int(extra), "dp", expert,
+        ), "wait_recv")
+
+    def own(self, action):
+        slots = self.slots
+        at = slots.packed(self.place, self.head)
+        slots.each(self.mine > slots.small, lambda extra: pltpu.make_async_copy(
+            self.rows.at[slots.span(at, extra)], self.back.at[slots.span(0, extra)],
+            self.local_sems.at[int(extra)],
+        ), action)
+
+    def blank(self, action):
+        slots = self.slots
+        if slots.more:
+            @pl.when(self.mine == slots.small)
+            def _():
+                tail = self.back.at[pl.ds(slots.count * slots.small, slots.count * slots.more)]
+                copy = pltpu.make_async_copy(self.zeros, tail, self.local_sems.at[2])
+                getattr(copy, action)()
+
+    def start(self):
+        if self.slots.more:
+            self.zeros[...] = jnp.zeros_like(self.zeros)
+        self.blank("start")
+
+        @pl.loop(1, self.slots.count)
+        def _(shift):
+            self.out(shift, "start")
+
+        self.own("start")
+
+    def finish(self):
+        @pl.loop(1, self.slots.count)
+        def _(shift):
+            self.into(shift)
+            self.out(shift, "wait_send")
+
+        self.own("wait")
+        self.blank("wait")
+
+
+def slot_return_scratch(slots, width):
+    return [pltpu.VMEM((max(slots.count * slots.more, 16), width), LOW)] + [
+        pltpu.SemaphoreType.DMA((2 * slots.count,)), pltpu.SemaphoreType.DMA((2 * slots.count,)),
+        pltpu.SemaphoreType.DMA((3,)),
+    ]
+
+
 def slot_exchange_sems(count):
     return [
         pltpu.SemaphoreType.DMA((2 * count,)), pltpu.SemaphoreType.DMA((2 * count,)),
@@ -679,33 +804,50 @@
 
 
 def prepare_kernel(
-    tile_ref, x_ref, g_ref, norm_ref, src_ref, col_ref, up_ref,
-    w_ref, xn_ref, sent_ref, up_out,
-    held, sent_sum, local_sem, *sems,
+    tile_ref, norm_ref, src_ref, col_ref, up_ref, x_in, g_in,
+    w_ref, xn_out, sent_out, up_out,
+    x_ref, g_ref, xn_ref, up_full, up_low, held, sent_sum, sent_ref,
+    load_sems, save_sems, *sems,
 ):
     images = x_ref.shape[0]
     gather = LineGather(held, *sems[:6])
-    spread = ImageGather(up_out, *sems[6:])
-    own = pltpu.make_async_copy(up_ref, up_out.at[spread.me], local_sem)
-    own.start()
+    spread = ImageGather(up_out, *sems[6:8], own=up_low, local_sem=sems[8])
+    load_up = pltpu.make_async_copy(up_ref, up_full, load_sems.at[2, 0])
+    load_up.start()
+
+    def load(image):
+        return (
+            pltpu.make_async_copy(x_in.at[image], x_ref.at[image], load_sems.at[0, image]),
+            pltpu.make_async_copy(g_in.at[image], g_ref.at[image], load_sems.at[1, image]),
+        )
+
+    def save(image):
+        return pltpu.make_async_copy(xn_ref.at[image], xn_out.at[image], save_sems.at[image])
+
+    for image in range(images):
+        for copy in load(image):
+            copy.start()
     me = lax.axis_index("dp")
     held[me] = tile_ref[...].astype(LOW)
     greet(*gather.neighbours(), ("head", spread.near), ("head", spread.far))
     gather.start()
-    own.wait()
+    load_up.wait()
+    up_low[...] = up_full[...].astype(LOW)
     spread.start()
+    shape = (sent_ref.shape[0], PATCH)
+    sent_sum[...] = jnp.zeros_like(sent_sum)
+    steps = gather.length - 1
 
     def image_step(image):
+        for copy in load(image):
+            copy.wait()
         normal, _ = normalise(x_ref[image].astype(FULL))
         xn_ref[image] = (normal * norm_ref[0:1, :] + norm_ref[1:2, :]).astype(LOW)
-        shape = (sent_ref.shape[0], PATCH)
+        save(image).start()
         slots = lax.broadcasted_iota(jnp.int32, shape, 0)
         col = col_ref[image]
         pick = one_hot((slots == col[0:1, :]) | (slots == col[1:2, :]))
         sent_sum[...] += nn(pick, g_ref[image])
-
-    sent_sum[...] = jnp.zeros_like(sent_sum)
-    steps = gather.length - 1
 
     @pl.loop(0, max(steps, (images + 1) // 2))
     def _(turn):
@@ -718,6 +860,8 @@
             gather.step(turn + 1)
 
     sent_ref[...] = sent_sum[...].astype(LOW)
+    save_sent = pltpu.make_async_copy(sent_ref, sent_out, load_sems.at[2, 1])
+    save_sent.start()
     gather.finish()
     rows = w_ref.shape[0] // 4
     blocks, depth, width = held.shape
@@ -730,28 +874,37 @@
     spread.wait_near()
     spread.wait_corner()
     spread.finish()
-
-
-def prepare(tiles, patches, cotangent, norm_params, src_col, col_rows, up_low, slots, dp_count):
+    save_sent.wait()
+
+    @pl.loop(0, images)
+    def _(image):
+        save(image).wait()
+
+
+def prepare(tiles, patches, cotangent, norm_params, src_col, col_rows, up, slots, dp_count):
     images, _, width = patches.shape
     line = dp_count // 2
     return pl.pallas_call(
         prepare_kernel,
-        in_specs=[INSIDE] * 6 + [ANYWHERE],
-        out_specs=[INSIDE] * 3 + [ANYWHERE],
+        in_specs=[INSIDE] * 4 + [ANYWHERE] * 3,
+        out_specs=[INSIDE] + [ANYWHERE] * 3,
         out_shape=[
             jax.ShapeDtypeStruct((src_col.shape[0], width), LOW),
             jax.ShapeDtypeStruct(patches.shape, LOW),
             jax.ShapeDtypeStruct((slots, width), LOW),
-            jax.ShapeDtypeStruct((4,) + up_low.shape, LOW),
+            jax.ShapeDtypeStruct((4,) + up.shape, LOW),
         ],
-        scratch_shapes=[
+        scratch_shapes=[pltpu.VMEM(patches.shape, LOW)] * 3
+        + [
+            pltpu.VMEM(up.shape, FULL), pltpu.VMEM(up.shape, LOW),
             pltpu.VMEM((dp_count,) + tiles.shape, LOW), pltpu.VMEM((slots, width), FULL),
-            pltpu.SemaphoreType.DMA,
-        ] + [pltpu.SemaphoreType.DMA((line,))] * 6 + image_gather_sems(),
+            pltpu.VMEM((slots, width), LOW),
+            pltpu.SemaphoreType.DMA((3, images)), pltpu.SemaphoreType.DMA((images,)),
+        ]
+        + [pltpu.SemaphoreType.DMA((line,))] * 6 + image_gather_sems() + [pltpu.SemaphoreType.DMA],
         compiler_params=params(collective_id=0, has_side_effects=True),
         name="prepare",
-    )(tiles, patches, cotangent, norm_params, src_col, col_rows, up_low)
+    )(tiles, norm_params, src_col, col_rows, up, patches, cotangent)
 
 
 def head_mask(shape, axis, head):
@@ -760,25 +913,36 @@
 
 def forward_kernel(
     slots,
-    xn_ref, w_ref, norm_ref, col_ref, x_ref, g_sent_ref, down_ref,
+    w_ref, norm_ref, col_ref, xn_in, x_ref, g_sent_ref, down_ref,
     lse_ref, q_out, qt_out, k_out, kt_out, v_out, ot_out, x1_out, rows_out, g_rows_out, down_out,
-    q_ref, qt_ref, k_ref, kt_ref, v_ref, ot_ref, x1_ref, own_ref, sent_ref, sent_sum,
-    save_sems, own_sem, *exchange,
+    q_ref, qt_ref, k_ref, kt_ref, v_ref, ot_ref, x1_ref, xn_ref, own_ref, sent_ref, sent_sum,
+    down_full, down_low, save_sems, own_sem, *exchange,
 ):
     images = xn_ref.shape[0]
     rows = w_ref.shape[0] // 4
     heads = rows // HD
     total_of = ImageSum(*exchange[:8])
     spread = ImageGather(x1_ref, *exchange[8:10])
-    spread_down = ImageGather(down_out, *exchange[10:12])
-    send_g = SlotExchange(slots, g_sent_ref, g_rows_out, *exchange[12:15])
-    send_rows = SlotExchange(slots, sent_ref, rows_out, *exchange[15:])
+    spread_down = ImageGather(down_out, *exchange[10:12], own=down_low, local_sem=exchange[12])
+    send_g = SlotExchange(slots, g_sent_ref, g_rows_out, *exchange[13:16])
+    send_rows = SlotExchange(slots, sent_ref, rows_out, *exchange[16:])
     me, near, far, corner = partners()
+
+    def load(turn):
+        image = total_of.image(turn)
+        return pltpu.make_async_copy(xn_in.at[image], xn_ref.at[image], save_sems.at[6, turn])
+
+    for turn in range(images):
+        load(turn).start()
+    load_down = pltpu.make_async_copy(down_ref, down_full, own_sem.at[1])
+    load_down.start()
     own = pltpu.make_async_copy(x_ref.at[me], own_ref, own_sem.at[0])
     own.start()
-    own_down = pltpu.make_async_copy(down_ref, down_out.at[me], own_sem.at[1])
-    own_down.start()
     greet_all((near, far), slots.count)
+    load_down.wait()
+    down_low[...] = down_full[...].astype(LOW)
+    spread_down.start_far(0, 1)
+    spread_down.start_near()
     send_g.start()
     kept = ((q_ref, q_out), (qt_ref, qt_out), (k_ref, k_out), (kt_ref, kt_out), (v_ref, v_out), (ot_ref, ot_out))
     shrink = HD ** (-0.5)
@@ -792,6 +956,7 @@
     @pl.loop(0, images)
     def _(turn):
         image = total_of.image(turn)
+        load(turn).wait()
         xn = xn_ref[image]
         wq, wk, wv, wo = (w_ref[pl.ds(part * rows, rows), :] for part in range(4))
         q_ref[image] = (nt(xn, wq) * shrink).astype(LOW)
@@ -839,8 +1004,7 @@
     spread.wait_corner()
     keep = pltpu.make_async_copy(x1_ref, x1_out, own_sem.at[0])
     keep.start()
-    own_down.wait()
-    spread_down.start()
+    spread_down.start_far(1)
     place(corner)
     sent_ref[...] = sent_sum[...].astype(LOW)
     send_rows.start()
@@ -860,65 +1024,91 @@
             copy.wait()
 
 
-def attention_forward(slots, xn, w, norm_params, col_rows, patches, g_sent, down_low):
+def attention_forward(slots, xn, w, norm_params, col_rows, patches, g_sent, down):
     images, _, width = patches.shape
     rows = w.shape[0] // 4
     flat, turned = (images, PATCH, rows), (images, rows, PATCH)
     saved = [flat, turned, flat, turned, flat, turned, patches.shape]
-    outs = saved + [(slots.rows, width), (slots.rows, width), (4,) + down_low.shape]
+    outs = saved + [(slots.rows, width), (slots.rows, width), (4,) + down.shape]
     most = slots.count * slots.big
     return pl.pallas_call(
         functools.partial(forward_kernel, slots),
-        in_specs=[INSIDE] * 4 + [ANYWHERE] * 3,
+        in_specs=[INSIDE] * 3 + [ANYWHERE] * 4,
         out_specs=[INSIDE] + [ANYWHERE] * 10,
         out_shape=[jax.ShapeDtypeStruct((images, 8, PATCH), FULL)]
         + [jax.ShapeDtypeStruct(shape, LOW) for shape in outs],
         scratch_shapes=[pltpu.VMEM(shape, LOW) for shape in saved]
         + [
+            pltpu.VMEM(patches.shape, LOW),
             pltpu.VMEM((PATCH, width), LOW), pltpu.VMEM((most, width), LOW),
             pltpu.VMEM((most, width), FULL),
-            pltpu.SemaphoreType.DMA((6, images)), pltpu.SemaphoreType.DMA((2,)),
+            pltpu.VMEM(down.shape, FULL), pltpu.VMEM(down.shape, LOW),
+            pltpu.SemaphoreType.DMA((7, images)), pltpu.SemaphoreType.DMA((2,)),
         ]
-        + image_sum_scratch(width) + image_gather_sems() + image_gather_sems()
+        + image_sum_scratch(PATCH, width) + image_gather_sems() + image_gather_sems()
+        + [pltpu.SemaphoreType.DMA]
         + slot_exchange_sems(slots.count) + slot_exchange_sems(slots.count),
         compiler_params=params(collective_id=1, has_side_effects=True),
         name="attention_forward",
-    )(xn, w, norm_params, col_rows, patches, g_sent, down_low)
+    )(w, norm_params, col_rows, xn, patches, g_sent, down)
 
 
 def backward_kernel(
     experts, slots,
-    x1g_ref, w_ref, xn_ref, q_ref, qt_ref, k_ref, kt_ref, v_ref, lse_ref, ot_ref, src_ref,
-    norm_ref, small_ref, col_ref, x_ref, out_rows_ref, x1_ref,
-    owned_ref, small_out, block_ref, input_out,
-    grad_ref, own_ref, input_ref, padded_ref, out_ref, own_sem, *exchange,
+    w_ref, lse_ref, src_ref, norm_ref, small_ref,
+    x1g_in, xn_in, q_in, qt_in, k_in, kt_in, v_in, ot_in, x_ref, out_rows_ref, down_part,
+    owned_ref, small_out, down_grad_ref, input_out, out_back,
+    x1g_ref, xn_ref, q_ref, qt_ref, k_ref, kt_ref, v_ref, ot_ref,
+    grad_ref, own_ref, input_ref, padded_ref, load_sems, own_sem, *exchange,
 ):
     images = x1g_ref.shape[0]
     rows = w_ref.shape[0] // 4
     heads = rows // HD
     total_of = ImageSum(*exchange[:8])
     spread = ImageGather(input_ref, *exchange[8:10])
-    back_out = ReturnGather(slots, out_rows_ref, out_ref, *exchange[10:13])
-    weights_sum = LineScatter(padded_ref, owned_ref, *exchange[13:23])
-    small_sum = SmallSum(*exchange[23:])
+    back_out = SlotReturn(slots, out_rows_ref, out_back, *exchange[10:14])
+    weights_sum = LineScatter(padded_ref, owned_ref, *exchange[14:24])
+    down_sum = BlockSum(down_part, *exchange[24:32])
+    small_sum = SmallSum(*exchange[32:])
     me, near, far, corner = partners()
     dp_count = slots.count
+    streamed = (
+        (xn_in, xn_ref), (q_in, q_ref), (qt_in, qt_ref), (k_in, k_ref), (kt_in, kt_ref),
+        (v_in, v_ref), (ot_in, ot_ref),
+    )
+
+    def load(turn):
+        image, slot = total_of.image(turn), lax.rem(turn, 2)
+        copies = [
+            pltpu.make_async_copy(source.at[image], target.at[slot], load_sems.at[index, slot])
+            for index, (source, target) in enumerate(streamed)
+        ]
+        copies.append(
+            pltpu.make_async_copy(x1g_in.at[image], x1g_ref.at[image], load_sems.at[7, slot])
+        )
+        return copies
+
+    for turn in range(2):
+        for copy in load(turn):
+            copy.start()
     own = pltpu.make_async_copy(x_ref.at[me], own_ref, own_sem.at[0])
     own.start()
-    x1_copy = pltpu.make_async_copy(x1_ref, block_ref, own_sem.at[1])
-    x1_copy.start()
     greet_all((near, far, corner), dp_count)
+    down_sum.start()
     back_out.start()
+    down_sum.across()
     shrink = HD ** (-0.5)
     grad_ref[...] = jnp.zeros_like(grad_ref)
 
     @pl.loop(0, images)
     def _(turn):
-        image = total_of.image(turn)
+        image, slot = total_of.image(turn), lax.rem(turn, 2)
+        for copy in load(turn):
+            copy.wait()
         wq, wk, wv, wo = (w_ref[pl.ds(part * rows, rows), :] for part in range(4))
-        x1g, xn = x1g_ref[image], xn_ref[image]
-        q, qt, k, kt = q_ref[image], qt_ref[image], k_ref[image], kt_ref[image]
-        v, ot = v_ref[image], ot_ref[image]
+        x1g, xn = x1g_ref[image], xn_ref[slot]
+        q, qt, k, kt = q_ref[slot], qt_ref[slot], k_ref[slot], kt_ref[slot]
+        v, ot = v_ref[slot], ot_ref[slot]
         do = nt(x1g, wo).astype(LOW)
         dot = nt(wo, x1g).astype(LOW)
         product = dot.astype(FULL) * ot.astype(FULL)
@@ -945,16 +1135,20 @@
         for part, piece in enumerate(pieces):
             grad_ref[pl.ds(part * rows, rows), :] += piece
 
-        @pl.when((turn == 1) | (turn == 2))
-        def _():
-            back_out.of_phase(2 * turn - 2, back_out.relay)
-            back_out.of_phase(2 * turn - 1, back_out.relay)
+        @pl.when(turn + 2 < images)
+        def _():
+            for copy in load(turn + 2):
+                copy.start()
 
     own.wait()
     normal, scale = normalise(own_ref[...].astype(FULL))
     back, gain_sum, shift_sum = norm_back(normal, scale, norm_ref[0:1, :], total_of.result())
     input_ref[me] = (x1g_ref[me].astype(FULL) + back).astype(LOW)
     spread.start()
+    small = small_ref[...]
+    row = lax.broadcasted_iota(jnp.int32, small.shape, 0)
+    small = small + jnp.where(row == experts, gain_sum, 0.0)
+    small_sum.start(small + jnp.where(row == experts + 1, shift_sum, 0.0))
     low = grad_ref[...].astype(LOW)
     depth = padded_ref.shape[1]
     parts = min(dp_count, 8)
@@ -967,88 +1161,72 @@
             dp_count // parts, depth, block.shape[1]
         )
     weights_sum.start()
-    small = small_ref[...]
-    row = lax.broadcasted_iota(jnp.int32, small.shape, 0)
-    small = small + jnp.where(row == experts, gain_sum, 0.0)
-    small_sum.start(small + jnp.where(row == experts + 1, shift_sum, 0.0))
-    @pl.loop(0, slots.count)
-    def _(shift):
-        back_out.forward(shift)
-
-    @pl.loop(0, slots.count)
-    def _(shift):
-        back_out.rest(shift)
-
-    x1_copy.wait()
+    small_sum.across()
     steps = weights_sum.length
 
-    @pl.loop(0, max(steps, images))
+    @pl.loop(0, steps - 1)
     def _(turn):
-        @pl.when(turn < images)
-        def _():
-            mix = block_ref[turn].astype(FULL)
-            for phase in range(4):
-                mix = mix + picked_rows(slots, col_ref[turn], out_ref, phase)
-            block_ref[turn] = mix.astype(LOW)
-
-        @pl.when(turn < steps - 1)
-        def _():
-            weights_sum.step(steps - 1 - turn)
+        weights_sum.step(steps - 1 - turn)
 
         @pl.when(turn == 0)
         def _():
-            small_sum.across()
-
-        @pl.when(turn == 1)
+            small_sum.back()
+
+        @pl.when(turn == steps - 2)
         def _():
             spread.wait_far()
-
-        @pl.when(turn == 2)
-        def _():
-            small_sum.back()
 
     weights_sum.result()
     small_sum.result(small_out)
+    down_grad_ref[...] = down_sum.result()
     spread.wait_near()
     spread.wait_corner()
     keep = pltpu.make_async_copy(input_ref, input_out, own_sem.at[0])
     keep.start()
+    back_out.finish()
     spread.finish()
-    back_out.finish()
     total_of.finish()
     weights_sum.finish()
     small_sum.finish()
+    down_sum.finish()
     keep.wait()
 
 
 def attention_backward(
     experts, slots, depth,
-    x1_grad, w, xn, saved, lse, src_row, norm_params, small, col, patches, out_rows, x1,
+    x1_grad, w, xn, saved, lse, src_row, norm_params, small, patches, out_rows, down_part,
 ):
-    q, qt, k, kt, v, ot = saved
     images, _, width = patches.shape
+    rows = w.shape[0] // 4
     dp_count = slots.count
+    flat, turned = (2, PATCH, rows), (2, rows, PATCH)
+    units = down_part.shape[1]
     return pl.pallas_call(
         functools.partial(backward_kernel, experts, slots),
-        in_specs=[INSIDE] * 14 + [ANYWHERE] * 3,
-        out_specs=[INSIDE, INSIDE, INSIDE, ANYWHERE],
+        in_specs=[INSIDE] * 5 + [ANYWHERE] * 11,
+        out_specs=[INSIDE] * 3 + [ANYWHERE] * 2,
         out_shape=[
             jax.ShapeDtypeStruct((depth, width), FULL), jax.ShapeDtypeStruct(small.shape, FULL),
-            jax.ShapeDtypeStruct(patches.shape, LOW), jax.ShapeDtypeStruct(patches.shape, LOW),
+            jax.ShapeDtypeStruct((units, width), FULL),
+            jax.ShapeDtypeStruct(patches.shape, LOW),
+            jax.ShapeDtypeStruct((dp_count * slots.big, width), LOW),
         ],
-        scratch_shapes=[
+        scratch_shapes=[pltpu.VMEM(patches.shape, LOW), pltpu.VMEM((2, PATCH, width), LOW)]
+        + [pltpu.VMEM(shape, LOW) for shape in (flat, turned, flat, turned, flat, turned)]
+        + [
             pltpu.VMEM(w.shape, FULL), pltpu.VMEM((PATCH, width), LOW),
             pltpu.VMEM(patches.shape, LOW), pltpu.VMEM((dp_count, depth, width), LOW),
-            pltpu.VMEM((4 * slots.phase_rows, width), LOW), pltpu.SemaphoreType.DMA((2,)),
+            pltpu.SemaphoreType.DMA((8, 2)), pltpu.SemaphoreType.DMA((2,)),
         ]
-        + image_sum_scratch(width) + image_gather_sems() + return_gather_sems(dp_count)
+        + image_sum_scratch(PATCH, width) + image_gather_sems()
+        + slot_return_scratch(slots, width)
         + line_scatter_scratch(dp_count, depth, width)
+        + block_sum_scratch(units, width)
         + small_sum_scratch(small.shape[0], width, dp_count),
         compiler_params=params(collective_id=2, has_side_effects=True),
         name="attention_backward",
     )(
-        x1_grad, w, xn, q, qt, k, kt, v, lse, ot, src_row, norm_params, small, col,
-        patches, out_rows, x1,
+        w, lse, src_row, norm_params, small, x1_grad, xn, *saved, patches, out_rows, down_part,
     )
 
 
@@ -1059,16 +1237,138 @@
     return nn(pick, held_ref[pl.ds(start, slots.phase_rows), :])
 
 
-def combine_kernel(
+def combine_kernel(col_ref, x1_ref, *refs):
+    *held, out_ref = refs
+    total = x1_ref[0].astype(FULL)
+    col = col_ref[0]
+    for part, rows_ref in enumerate(held):
+        count = rows_ref.shape[0]
+        lanes = lax.broadcasted_iota(jnp.int32, (col.shape[0], count), 1) + part * count
+        pick = one_hot((lanes == col[:, 0:1]) | (lanes == col[:, 1:2]))
+        total = total + nn(pick, rows_ref[...])
+    out_ref[0] = total.astype(LOW)
+
+
+def combine_forward(col, x1, held):
+    images, _, width = x1.shape
+    wide = lead((1, PATCH, width))
+    return pl.pallas_call(
+        combine_kernel,
+        grid=(images,),
+        in_specs=[lead((1, PATCH, 2)), wide] + [whole(rows.shape) for rows in held],
+        out_specs=wide,
+        out_shape=jax.ShapeDtypeStruct(x1.shape, LOW),
+        compiler_params=params(),
+        cost_estimate=pl.CostEstimate(
+            flops=2 * images * PATCH * sum(rows.size for rows in held),
+            bytes_accessed=4 * x1.size + 2 * sum(rows.size for rows in held), transcendentals=0,
+        ),
+        name="combine_forward",
+    )(col, x1, *held)
+
+
+def expert_kernel(
     slots,
-    col_ref, x1_ref, g_ref, norm_ref, rows_ref,
-    out_ref, sums_ref,
-    held, total, *sems,
+    rows_ref, g_ref, router_ref, own_ref, closed_ref, col_ref, norm_ref,
+    up_in, down_in, x1_in, cot_in,
+    up_grad_ref, router_grad_ref, sums_ref, down_out, out_out, x1g_out,
+    up_ref, down_ref, og_ref, gate_ref, probs_ref, down_stage, out_ref, back_ref,
+    held, total, x1_ref, cot_ref, x1g_ref,
+    load_sems, save_sems, image_sems, out_sem, *exchange,
 ):
-    images = x1_ref.shape[0]
-    back = ReturnGather(slots, rows_ref, held, *sems)
+    images, count = x1_in.shape[0], rows_ref.shape[0]
+    out_sum, back_sum = total.at[pl.ds(0, count)], total.at[pl.ds(count, count)]
+    up_sum = ImageSum(*exchange[:8])
+    back = ReturnGather(slots, back_ref, held, *exchange[8:])
+    parts = up_in.shape[0]
+
+    def load(turn):
+        part, slot = up_sum.image(turn), lax.rem(turn, 2)
+        return (
+            pltpu.make_async_copy(up_in.at[part], up_ref.at[slot], load_sems.at[0, slot]),
+            pltpu.make_async_copy(down_in.at[part], down_ref.at[slot], load_sems.at[1, slot]),
+        )
+
+    def save(turn):
+        slot = lax.rem(turn, 2)
+        return pltpu.make_async_copy(
+            down_stage.at[slot], down_out.at[up_sum.image(turn)], save_sems.at[slot]
+        )
+
+    for turn in range(2):
+        for copy in load(turn):
+            copy.start()
+    rows = rows_ref[...]
+    logits = nt(rows, router_ref[...]) + closed_ref[...]
+    top = jnp.max(logits, axis=-1, keepdims=True)
+    weights = jnp.exp(logits - top)
+    probs = weights / jnp.sum(weights, axis=-1, keepdims=True)
+    gate = jnp.sum(probs * own_ref[...], axis=-1, keepdims=True)
+    probs_ref[...] = probs
+    gate_ref[...] = gate
+    og_ref[...] = (gate * g_ref[...].astype(FULL)).astype(LOW)
+    out_sum[...] = jnp.zeros_like(out_sum)
+    back_sum[...] = jnp.zeros_like(back_sum)
     greet_all((back.near, back.far), slots.count)
+
+    @pl.loop(0, parts)
+    def _(turn):
+        slot = lax.rem(turn, 2)
+        for copy in load(turn):
+            copy.wait()
+        rows, og = rows_ref[...], og_ref[...]
+        up, down = up_ref[slot], down_ref[slot]
+        hidden = nn(rows, up)
+        slope = (2.0 / jnp.pi) ** 0.5
+        square = hidden * hidden
+        bend = jnp.tanh(slope * (hidden + 0.044715 * (square * hidden)))
+        act = (0.5 * hidden * (1.0 + bend)).astype(LOW)
+        out_sum[...] += nn(act, down)
+        act_grad = nt(og, down)
+        inner = slope * (1.0 + (3.0 * 0.044715) * square)
+        curve = 0.5 * (1.0 + bend) + 0.5 * hidden * (1.0 - bend * bend) * inner
+        hidden_grad = (curve * act_grad).astype(LOW)
+        back_sum[...] += nt(hidden_grad, up)
+        up_sum.give(turn, tn(rows, hidden_grad))
+
+        @pl.when(turn >= 2)
+        def _():
+            save(turn - 2).wait()
+
+        down_stage[lax.rem(turn, 2)] = tn(act, og).astype(LOW)
+        save(turn).start()
+
+        @pl.when(turn + 2 < parts)
+        def _():
+            for copy in load(turn + 2):
+                copy.start()
+
+    out = out_sum[...].astype(LOW).astype(FULL)
+    gate, probs = gate_ref[...], probs_ref[...]
+    gate_grad = jnp.sum(g_ref[...].astype(FULL) * out, axis=-1, keepdims=True)
+    logit_grad = (gate_grad * (probs * (own_ref[...] - gate))).astype(LOW)
+    plain = back_sum[...].astype(LOW).astype(FULL)
+    back_ref[...] = (plain + nn(logit_grad, router_ref[...])).astype(LOW)
     back.start()
+    out_ref[...] = (gate * out).astype(LOW)
+    save_out = pltpu.make_async_copy(out_ref, out_out, out_sem)
+    save_out.start()
+    router_grad_ref[...] = tn(logit_grad, rows_ref[...])
+
+    def image_load(image):
+        slot = lax.rem(image, 2)
+        return (
+            pltpu.make_async_copy(x1_in.at[image], x1_ref.at[slot], image_sems.at[0, slot]),
+            pltpu.make_async_copy(cot_in.at[image], cot_ref.at[slot], image_sems.at[1, slot]),
+        )
+
+    def image_save(image):
+        slot = lax.rem(image, 2)
+        return pltpu.make_async_copy(x1g_ref.at[slot], x1g_out.at[image], image_sems.at[2, slot])
+
+    for image in range(2):
+        for copy in image_load(image):
+            copy.start()
     back.of_phase(0, back.relay)
 
     @pl.loop(0, 4)
@@ -1087,127 +1387,86 @@
 
             @pl.when(phase == 0)
             def _():
-                total[image] = part
+                total[pl.ds(image * PATCH, PATCH)] = part
 
             @pl.when(phase > 0)
             def _():
-                total[image] += part
+                total[pl.ds(image * PATCH, PATCH)] += part
 
     sums_ref[...] = jnp.zeros_like(sums_ref)
 
     @pl.loop(0, images)
     def _(image):
-        normal, scale = normalise(x1_ref[image].astype(FULL))
-        result, gain_sum, shift_sum = norm_back(normal, scale, norm_ref[2:3, :], total[image])
-        out_ref[image] = (g_ref[image].astype(FULL) + result).astype(LOW)
+        slot = lax.rem(image, 2)
+        for copy in image_load(image):
+            copy.wait()
+
+        @pl.when(image >= 2)
+        def _():
+            image_save(image - 2).wait()
+
+        normal, scale = normalise(x1_ref[slot].astype(FULL))
+        upstream = total[pl.ds(image * PATCH, PATCH)]
+        result, gain_sum, shift_sum = norm_back(normal, scale, norm_ref[2:3, :], upstream)
+        x1g_ref[slot] = (cot_ref[slot].astype(FULL) + result).astype(LOW)
         sums_ref[0:1, :] += gain_sum
         sums_ref[1:2, :] += shift_sum
-
+        image_save(image).start()
+
+        @pl.when(image + 2 < images)
+        def _():
+            for copy in image_load(image + 2):
+                copy.start()
+
+    up_grad_ref[...] = up_sum.result()
     back.finish()
-
-
-def combine_backward(slots, col, x1, cotangent, norm_params, rows):
-    images, _, width = x1.shape
-    return pl.pallas_call(
-        functools.partial(combine_kernel, slots),
-        in_specs=[INSIDE] * 4 + [ANYWHERE],
-        out_specs=[INSIDE] * 2,
-        out_shape=[
-            jax.ShapeDtypeStruct(x1.shape, LOW), jax.ShapeDtypeStruct((8, width), FULL)
-        ],
-        scratch_shapes=[
-            pltpu.VMEM((4 * slots.phase_rows, width), LOW), pltpu.VMEM(x1.shape, FULL),
-        ] + return_gather_sems(slots.count),
-        compiler_params=params(collective_id=3, has_side_effects=True),
-        name="combine_backward",
-    )(col, x1, cotangent, norm_params, rows)
-
-
-def expert_kernel(
-    rows_ref, g_ref, up_ref, down_ref, router_ref, own_ref, count_ref,
-    back_ref, out_ref, upg_ref, downg_ref, router_grad_ref,
-    out_sum, back_sum, og_ref, gate_ref, probs_ref,
-):
-    step = pl.program_id(0)
-    rows = rows_ref[...]
-
-    @pl.when(step == 0)
-    def _():
-        logits = nt(rows, router_ref[...]) + count_ref[...]
-        top = jnp.max(logits, axis=-1, keepdims=True)
-        weights = jnp.exp(logits - top)
-        probs = weights / jnp.sum(weights, axis=-1, keepdims=True)
-        gate = jnp.sum(probs * own_ref[...], axis=-1, keepdims=True)
-        probs_ref[...] = probs
-        gate_ref[...] = gate
-        og_ref[...] = (gate * g_ref[...].astype(FULL)).astype(LOW)
-        out_sum[...] = jnp.zeros_like(out_sum)
-        back_sum[...] = jnp.zeros_like(back_sum)
-
-    og = og_ref[...]
-    up, down = up_ref[0], down_ref[0]
-    hidden = nn(rows, up)
-    slope = (2.0 / jnp.pi) ** 0.5
-    square = hidden * hidden
-    bend = jnp.tanh(slope * (hidden + 0.044715 * (square * hidden)))
-    act = (0.5 * hidden * (1.0 + bend)).astype(LOW)
-    out_sum[...] += nn(act, down)
-    act_grad = nt(og, down)
-    inner = slope * (1.0 + (3.0 * 0.044715) * square)
-    curve = 0.5 * (1.0 + bend) + 0.5 * hidden * (1.0 - bend * bend) * inner
-    hidden_grad = (curve * act_grad).astype(LOW)
-    back_sum[...] += nt(hidden_grad, up)
-    upg_ref[0] = tn(rows, hidden_grad).astype(LOW)
-    downg_ref[0] = tn(act, og).astype(LOW)
-
-    @pl.when(step == pl.num_programs(0) - 1)
-    def _():
-        out = out_sum[...].astype(LOW).astype(FULL)
-        gate, probs = gate_ref[...], probs_ref[...]
-        out_ref[...] = (gate * out).astype(LOW)
-        gate_grad = jnp.sum(g_ref[...].astype(FULL) * out, axis=-1, keepdims=True)
-        logit_grad = (gate_grad * (probs * (own_ref[...] - gate))).astype(LOW)
-        back = back_sum[...].astype(LOW).astype(FULL) + nn(logit_grad, router_ref[...])
-        back_ref[...] = back.astype(LOW)
-        router_grad_ref[...] = tn(logit_grad, rows)
-
-
-def experts_both_ways(rows, g_rows, up, down, router_low, own):
-    slots, width = rows.shape
+    up_sum.finish()
+    save_out.wait()
+    for turn in range(parts - 2, parts):
+        save(turn).wait()
+    for image in range(images - 2, images):
+        image_save(image).wait()
+
+
+def expert_stage(slots, rows, g_rows, up, down, router_low, own, col, x1, cotangent, norm_params):
+    count, width = rows.shape
     parts, _, units = up.shape
+    images = x1.shape[0]
     experts = router_low.shape[0]
     lanes = 128
     router_wide = jnp.zeros((lanes, width), LOW).at[:experts].set(router_low)
     lane = jnp.arange(lanes, dtype=jnp.int32)[None, :]
     own_row = jnp.where(lane == own, 1.0, 0.0).astype(FULL)
     closed = jnp.where(lane < experts, 0.0, -1e30).astype(FULL)
-    wide_spec = whole((slots, width))
+    flat = pltpu.VMEM((count, width), LOW)
+    pair = pltpu.VMEM((2, PATCH, width), LOW)
     return pl.pallas_call(
-        expert_kernel,
-        grid=(parts,),
-        in_specs=[
-            wide_spec, wide_spec, lead((1, width, units)), lead((1, units, width)),
-            whole((lanes, width)), whole((1, lanes)), whole((1, lanes)),
-        ],
-        out_specs=[
-            wide_spec, wide_spec, lead((1, width, units)), lead((1, units, width)),
-            whole((lanes, width)),
-        ],
+        functools.partial(expert_kernel, slots),
+        in_specs=[INSIDE] * 7 + [ANYWHERE] * 4,
+        out_specs=[INSIDE] * 3 + [ANYWHERE] * 3,
         out_shape=[
-            jax.ShapeDtypeStruct((slots, width), LOW),
-            jax.ShapeDtypeStruct((slots, width), LOW),
-            jax.ShapeDtypeStruct(up.shape, LOW),
+            jax.ShapeDtypeStruct((width, units), FULL),
+            jax.ShapeDtypeStruct((lanes, width), FULL),
+            jax.ShapeDtypeStruct((8, width), FULL),
             jax.ShapeDtypeStruct(down.shape, LOW),
-            jax.ShapeDtypeStruct((lanes, width), FULL),
+            jax.ShapeDtypeStruct((count, width), LOW),
+            jax.ShapeDtypeStruct(x1.shape, LOW),
         ],
         scratch_shapes=[
-            pltpu.VMEM((slots, width), FULL), pltpu.VMEM((slots, width), FULL),
-            pltpu.VMEM((slots, width), LOW), pltpu.VMEM((slots, 1), FULL),
-            pltpu.VMEM((slots, lanes), FULL),
-        ],
-        compiler_params=params(),
-        name="experts_both_ways",
-    )(rows, g_rows, up, down, router_wide, own_row, closed)
+            pltpu.VMEM((2,) + up.shape[1:], LOW), pltpu.VMEM((2,) + down.shape[1:], LOW), flat,
+            pltpu.VMEM((count, 1), FULL), pltpu.VMEM((count, lanes), FULL),
+            pltpu.VMEM((2, units, width), LOW), flat, flat,
+            pltpu.VMEM((4 * slots.phase_rows, width), LOW),
+            pltpu.VMEM((max(images * PATCH, 2 * count), width), FULL), pair, pair, pair,
+            pltpu.SemaphoreType.DMA((2, 2)), pltpu.SemaphoreType.DMA((2,)),
+            pltpu.SemaphoreType.DMA((3, 2)), pltpu.SemaphoreType.DMA,
+        ]
+        + image_sum_scratch(width, units) + return_gather_sems(slots.count),
+        compiler_params=params(collective_id=3, has_side_effects=True),
+        name="expert_stage",
+    )(
+        rows, g_rows, router_wide, own_row, closed, col, norm_params, up, down, x1, cotangent,
+    )
 
 
 def body(
@@ -1247,20 +1506,23 @@
     shift = (me_dp + dp_count - ids) % dp_count
     col = jnp.where(kept, slots.row(me_dp, holder, shift) + within, -1)
     col = col.T.reshape(images, PATCH, 2)
+    seen = lax.bitwise_xor(holder, me_head) * (dp_count * slots.big)
+    col_out = jnp.where(kept, seen + shift * slots.size(me_dp, holder) + within, -1)
+    col_out = col_out.T.reshape(images, PATCH, 2)
 
     by_image = (images, PATCH, width)
     x_images, g_images = patches.reshape(by_image), cotangent.reshape(by_image)
     w, xn, g_sent, up_all = prepare(
         tile_master.reshape(slot_count * TILE, width), x_images, g_images, norm_params,
-        src[:, None], col_rows, expert_up[0].astype(LOW), slots.count * slots.big, dp_count,
+        src[:, None], col_rows, expert_up[0], slots.count * slots.big, dp_count,
     )
     lse, *saved, x1, rows, g_rows, down_all = attention_forward(
-        slots, xn, w, norm_params, col_rows, x_images, g_sent, expert_down[0].astype(LOW)
-    )
-    back, out, up_part, down_part, router_part = experts_both_ways(
-        rows, g_rows, up_all, down_all, router.astype(LOW), me_dp
-    )
-    x1_grad, second_sums = combine_backward(slots, col, x1, g_images, norm_params, back)
+        slots, xn, w, norm_params, col_rows, x_images, g_sent, expert_down[0]
+    )
+    up_grad, router_part, second_sums, down_part, out, x1_grad = expert_stage(
+        slots, rows, g_rows, up_all, down_all, router.astype(LOW), me_dp, col, x1, g_images,
+        norm_params,
+    )
 
     small_rows = -(-(experts + 4) // 16) * 16
     small = jnp.concatenate(
@@ -1270,16 +1532,20 @@
             jnp.zeros((small_rows - experts - 4, width), FULL),
         ]
     )
-    owned_grad, small, block_out, input_low = attention_backward(
+    owned_grad, small, down_grad, input_low, out_back = attention_backward(
         experts, slots, slot_count * TILE,
-        x1_grad, w, xn, saved, lse, src[None, :], norm_params, small, col, x_images, out, x1,
-    )
-    block_out = block_out.reshape(tok_rows, width)
+        x1_grad, w, xn, saved, lse, src[None, :], norm_params, small, x_images, out, down_part,
+    )
     owned_grad = owned_grad.reshape(slot_count, TILE, width)
     input_grad = input_low.reshape(tok_rows, width).astype(FULL)
 
-    up_grad = lax.psum_scatter(up_part, "head", scatter_dimension=0).astype(FULL)
-    down_grad = lax.psum_scatter(down_part, "head", scatter_dimension=0).astype(FULL)
+    def from_head(rows, apart):
+        return lax.ppermute(rows, "head", [(at, at ^ apart) for at in range(head_count)])
+
+    out_far = from_head(out_back, 2)
+    held = [out_back, from_head(out_back, 1), out_far, from_head(out_far, 1)]
+    block_out = combine_forward(col_out, x1, held).reshape(tok_rows, width)
+
     router_total, norm_total = small[:experts], small[experts:experts + 4]
 
     tile_new, tile_first_new, tile_second_new = adam_update(

time: 438 us -> 370 us (0.84)
  Pallas kernels: 375 us -> 324 us
  between operations: 14.4 us -> 1.08 us
  other arithmetic: 33.4 us -> 26.7 us
    pallas_call x3, Pallas kernels: 172 us -> 137 us  [the longest x1 79.6 us: expert_stage(): pl.pallas_call(functools.partial(expert_kernel, slots), in_specs=[INSIDE]...]
    pallas_call x1, Pallas kernels: 119 us -> 111 us  [attention_backward(): pl.pallas_call(functools.partial(backward_kernel, experts, slots), in_spe...]
    pallas_call x1, Pallas kernels: 83.8 us -> 76.5 us  [attention_forward(): pl.pallas_call(functools.partial(forward_kernel, slots), in_specs=[INSIDE...]
  transfers between devices with their start and end apart: 2 -> 3, of which waited for: 0 -> 1; matrix products, arithmetic and copies ran while one was open for 5% -> 6% of each run, Pallas kernels for 43% -> 0%
where the time goes in v5:
time: 370 us; the launch traced here: 363 us
  Pallas kernels  324 us (88%)
  other arithmetic  26.7 us (7%)
  local copies, waits for them, and re-layouts  8.54 us (2%)
    pallas_call x1, Pallas kernels, attention_backward(): pl.pallas_call(functools.partial(backward_kernel, experts, slots), in_spe...  111 us
    pallas_call x1, Pallas kernels, expert_stage(): pl.pallas_call(functools.partial(expert_kernel, slots), in_specs=[INSIDE]...  79.6 us
    pallas_call x1, Pallas kernels, attention_forward(): pl.pallas_call(functools.partial(forward_kernel, slots), in_specs=[INSIDE...  76.5 us
    pallas_call x1, Pallas kernels, prepare(): pl.pallas_call(prepare_kernel, in_specs=[INSIDE] * 4 + [ANYWHERE] * 3, ou...  41.3 us
    pallas_call x1, Pallas kernels, combine_forward(): pl.pallas_call(combine_kernel, grid=(images,), in_specs=[lead((1, PATCH,...  16 us
    convert_element_type x1, other arithmetic, body(): down_new.astype(LOW)  7.7 us
  transfers between devices with their start and end apart: 3, of which 1 were waited for; matrix products, arithmetic and copies ran while one was open for 6% of the time, Pallas kernels for 0%

profile of v5, /device:TPU:0, one launch (start us, length us, event | category | flops | bytes accessed | tf_op | source)
XLA Modules:
  0.0 363.0 jit_solution(7363703146212710879)
XLA Ops:
  0.7 0.5 compare_select_fusion.6
  1.2 0.9 select_reduce_fusion
  2.1 0.7 add_multiply_fusion
  2.9 0.9 add.294.src_ref
  3.8 0.7 add.264.src_ref
  4.4 0.8 fusion.8
  5.3 0.1 reshape.182
  5.4 0.6 copy.52
  6.0 1.0 fusion.22
  7.1 1.4 copy.50
  8.5 0.7 convert_element_type.18
  9.2 0.7 scatter.4.router_ref
  9.9 41.3 %prepare.1 = (bf16[768,768]{1,0:T(8,128)(2,1)}, bf16[4,576,768]{2,1,0:T(8,128)(2,1)}, bf16[640,768]{1,0:T(8,128)(2,1)}, bf16[4,768,768]{2,1,0:T(8,128)(2,1)}) custom-call(f32[192,768]{1,0:T(8,128)} %bitcast.76, f32[4,768]{1,0:T(4,128)} %norm_ref.7, s32[768,1]{1,0:T(8,128)} %add.294.src_ref, s32[4,2,576]{2,1,0:T(2,128)} %bitcast.78, f32[768,768]{1,0:T(8,128)} %bitcast.73, ...), custom_call_target="tpu_custom_call" | custom-call | tf_op jit(solution)/shard_map/prepare/pallas_call | solution.py:887
  51.2 76.5 %attention_forward.1 = (f32[4,8,576]{2,1,0:T(8,128)}, bf16[4,576,192]{2,1,0:T(8,128)(2,1)}, bf16[4,192,576]{2,1,0:T(8,128)(2,1)}, bf16[4,576,192]{2,1,0:T(8,128)...) custom-call(bf16[768,768]{1,0:T(8,128)(2,1)} %get-tuple-element.59.w, ...), custom_call_target="tpu_custom_call" | custom-call | tf_op jit(solution)/shard_map/attention_forward/pallas_call | solution.py:1034
  127.7 79.6 %expert_stage.1 = (f32[768,768]{1,0:T(8,128)}, f32[128,768]{1,0:T(8,128)}, f32[8,768]{1,0:T(8,128)}, bf16[4,768,768]{2,1,0:T(8,128)(2,1)}, bf16[576,768]{1,0:T(8,128)(2,1)}, /*index=5*/bf16[4,576,768]{2,1,0:T(8,128)(2,1)}) custom-call(bf16[576,768]{1,0:T(8,128)(2,1)} %get-tuple-element.64.rows_ref, bf16[576,768]{1,0:T(8,128)(2,1)} %get-tuple-element.65.g_ref, ...), custom_call_target="tpu_custom_call" | custom-call | tf_op jit(solution)/shard_map/expert_stage/pallas_call | solution.py:1443
  207.4 0.7 slice.34
  208.1 0.7 slice_multiply_fusion
  208.9 0.7 pad_maximum_fusion.small_ref
  209.7 110.6 %attention_backward.1 = (f32[192,768]{1,0:T(8,128)}, f32[16,768]{1,0:T(8,128)}, f32[768,768]{1,0:T(8,128)}, bf16[4,576,768]{2,1,0:T(8,128)(2,1)}, bf16[640,768]{1,0:T(8,128)(2,1)}) custom-call(bf16[768,768]{1,0:T(8,128)(2,1)} %get-tuple-element.59.w_ref, f32[4,8,576]{2,1,0:T(8,128)} %get-tuple-element.63.lse_ref, s32[1,768]{1,0:T(1,128)} %add.264.src_ref, ...), custom_call_target="tpu_custom_call" | custom-call | tf_op jit(solution)/shard_map/attention_backward/pallas_call | solution.py:1204
  320.5 0.1 add_select_fusion
  320.7 1.4 copy.47
  322.1 1.4 multiply_subtract_fusion.3
  323.5 1.4 multiply_subtract_fusion.5
  324.9 7.7 %fusion.26 = (bf16[1,768,768]{2,1,0:T(8,128)(2,1)}, f32[1,768,768]{2,1,0:T(8,128)}, f32[1,768,768]{2,1,0:T(8,128)}, f32[1,768,768]{2,1,0:T(8,128)}) fusion(f32[1,768,768]{2,1,0:T(8,128)S(1)} %copy-done.1, f32[768,768]{1,0:T(8,128)} %get-tuple-element.83, f32[1,768,768]{2,1,0:T(8,128)} %param.34, f32[1,768,768]{2,1,0:T(8,128)} %param.35), kind=kLoop, calls=%fused_computation.81 | loop fusion | flops 9437184 | bytes 17694720 | tf_op jit(solution)/shard_map/convert_element_type | solution.py:1580
  332.7 1.6 fusion.30
  334.3 0.6 fusion.34
  334.9 0.2 copy-done
  335.1 4.5 %fusion.28 = (bf16[1,768,768]{2,1,0:T(8,128)(2,1)}, f32[1,768,768]{2,1,0:T(8,128)}, f32[1,768,768]{2,1,0:T(8,128)}, f32[1,768,768]{2,1,0:T(8,128)}) fusion(f32[1,768,768]{2,1,0:T(8,128)S(1)} %copy-done, f32[768,768]{1,0:T(8,128)S(1)} %copy-done.5, f32[1,768,768]{2,1,0:T(8,128)S(1)} %copy-done.3, f32[1,768,768]{2,1,0:T(8,128)S(1)} %copy-done.4), kind=kLoop, calls=%fused_computation.82 | loop fusion | flops 9437184 | bytes 17694720 | tf_op jit(solution)/shard_map/convert_element_type | solution.py:1576
  339.6 2.4 collective-permute-done.1.refs_2_
  342.1 3.7 %bitcast_convert_fusion = f32[2304,768]{1,0:T(8,128)} fusion(bf16[4,576,768]{2,1,0:T(8,128)(2,1)S(1)} %copy-done.2), kind=kLoop, calls=%fused_computation | loop fusion | flops 1769472 | bytes 10616832 | tf_op jit(solution)/shard_map/convert_element_type | solution.py:1540
  345.8 1.0 copy-done.19
  346.8 16.0 %combine_forward.1 = bf16[4,576,768]{2,1,0:T(8,128)(2,1)} custom-call(s32[4,576,2]{2,1,0:T(8,128)} %bitcast.77, bf16[4,576,768]{2,1,0:T(8,128)(2,1)} %get-tuple-element.62.x1_in.x1_ref, bf16[640,768]{1,0:T(8,128)(2,1)} %get-tuple-element.79.refs_0_, bf16[640,768]{1,0:T(8,128)(2,1)} %collective-permute-done.refs_1_, bf16[640,768]{1,0:T(8,128)(2,1)} %copy-done.18, ...), custom_call_target="tpu_custom_call" | custom-call | flops 9059696640 | bytes 11010048 | tf_op jit(solution)/shard_map/combine_forward/pallas_call | solution.py:1255
  (47 shorter events, 0.4 us)
Async XLA Ops:
  209.6 110.9 %copy-start.11 = (s32[2304,2]{0,1:T(2,128)S(1)}, s32[2304,2]{0,1:T(2,128)}, u32[]{:S(2)}) copy-start(s32[2304,2]{0,1:T(2,128)} %param.25) | copy-start | bytes 55300
  209.6 110.9 %copy-start.12 = (s32[2304,2]{0,1:T(2,128)S(1)}, s32[2304,2]{0,1:T(2,128)}, u32[]{:S(2)}) copy-start(s32[2304,2]{0,1:T(2,128)} %param.24) | copy-start | bytes 55300
  209.6 112.5 %copy-start.13 = (f32[8,768]{1,0:T(8,128)S(1)}, f32[8,768]{1,0:T(8,128)}, u32[]{:S(2)}) copy-start(f32[8,768]{1,0:T(8,128)} %param.36) | copy-start | bytes 73732
  209.6 112.5 %copy-start.14 = (f32[8,768]{1,0:T(8,128)S(1)}, f32[8,768]{1,0:T(8,128)}, u32[]{:S(2)}) copy-start(f32[8,768]{1,0:T(8,128)} %param.37) | copy-start | bytes 73732
  209.6 112.5 %copy-start.15 = (f32[8,768]{1,0:T(8,128)S(1)}, f32[8,768]{1,0:T(8,128)}, u32[]{:S(2)}) copy-start(f32[8,768]{1,0:T(8,128)} %param.38) | copy-start | bytes 73732
  209.6 113.8 %copy-start.10 = (f32[4,768]{1,0:T(4,128)S(1)}, f32[4,768]{1,0:T(4,128)}, u32[]{:S(2)}) copy-start(f32[4,768]{1,0:T(4,128)} %norm_ref.7) | copy-start | bytes 36868
  209.7 113.8 %copy-start.16 = (f32[4,768]{1,0:T(4,128)S(1)}, f32[4,768]{1,0:T(4,128)}, u32[]{:S(2)}) copy-start(f32[4,768]{1,0:T(4,128)} %param.40) | copy-start | bytes 36868
  209.7 113.8 %copy-start.17 = (f32[4,768]{1,0:T(4,128)S(1)}, f32[4,768]{1,0:T(4,128)}, u32[]{:S(2)}) copy-start(f32[4,768]{1,0:T(4,128)} %param.41) | copy-start | bytes 36868
  209.7 115.2 %copy-start.1 = (f32[1,768,768]{2,1,0:T(8,128)S(1)}, f32[1,768,768]{2,1,0:T(8,128)}, u32[]{:S(2)}) copy-start(f32[1,768,768]{2,1,0:T(8,128)} %param.33) | copy-start | bytes 7077892
  320.3 21.7 %collective-permute-start.1 = (bf16[640,768]{1,0:T(8,128)(2,1)}, bf16[640,768]{1,0:T(8,128)(2,1)S(1)}, u32[]{:S(2)}, u32[]{:S(2)}) collective-permute-start(bf16[640,768]{1,0:T(8,128)(2,1)} %get-tuple-element.79.refs_0_), channel_id=1, source_target_pairs={{0,2},{1,3},{2,0},{3,1},{4,6},{5,7},{6,4},{7,5},{8,10},{9,11},{10,... | collective-permute-start | bytes 2949128 | tf_op jit(solution)/shard_map/ppermute | solution.py:1543
  320.4 25.4 %collective-permute-start = (bf16[640,768]{1,0:T(8,128)(2,1)}, bf16[640,768]{1,0:T(8,128)(2,1)}, u32[]{:S(2)}, u32[]{:S(2)}) collective-permute-start(bf16[640,768]{1,0:T(8,128)(2,1)} %get-tuple-element.79.refs_0_), channel_id=1, source_target_pairs={{0,1},{1,0},{2,3},{3,2},{4,5},{5,4},{6,7},{7,6},{8,9},{9,8},{10,11... | collective-permute-start | bytes 2949128 | tf_op jit(solution)/shard_map/ppermute | solution.py:1543
  324.9 7.8 %copy-start.6 = (f32[24,8,768]{2,1,0:T(8,128)S(1)}, f32[24,8,768]{2,1,0:T(8,128)}, u32[]{:S(2)}) copy-start(f32[24,8,768]{2,1,0:T(8,128)} %param.27) | copy-start | bytes 1769476
  324.9 7.8 %copy-start.7 = (f32[24,8,768]{2,1,0:T(8,128)S(1)}, f32[24,8,768]{2,1,0:T(8,128)}, u32[]{:S(2)}) copy-start(f32[24,8,768]{2,1,0:T(8,128)} %param.28) | copy-start | bytes 1769476
  324.9 7.8 %copy-start.8 = (f32[24,8,768]{2,1,0:T(8,128)S(1)}, f32[24,8,768]{2,1,0:T(8,128)}, u32[]{:S(2)}) copy-start(f32[24,8,768]{2,1,0:T(8,128)} %param.29) | copy-start | bytes 1769476
  324.9 7.8 %copy-start.9 = (f32[192,768]{1,0:T(8,128)S(1)}, f32[192,768]{1,0:T(8,128)}, u32[]{:S(2)}) copy-start(f32[192,768]{1,0:T(8,128)} %get-tuple-element.81) | copy-start | bytes 1769476
  324.9 10.0 %copy-start.3 = (f32[1,768,768]{2,1,0:T(8,128)S(1)}, f32[1,768,768]{2,1,0:T(8,128)}, u32[]{:S(2)}) copy-start(f32[1,768,768]{2,1,0:T(8,128)} %param.31) | copy-start | bytes 7077892
  324.9 10.0 %copy-start.4 = (f32[1,768,768]{2,1,0:T(8,128)S(1)}, f32[1,768,768]{2,1,0:T(8,128)}, u32[]{:S(2)}) copy-start(f32[1,768,768]{2,1,0:T(8,128)} %param.32) | copy-start | bytes 7077892
  324.9 9.9 %copy-start.5 = (f32[768,768]{1,0:T(8,128)S(1)}, f32[768,768]{1,0:T(8,128)}, u32[]{:S(2)}) copy-start(f32[768,768]{1,0:T(8,128)} %get-tuple-element.82) | copy-start | bytes 7077892
  332.6 2.5 copy-start
  335.1 7.0 %copy-start.2 = (bf16[4,576,768]{2,1,0:T(8,128)(2,1)S(1)}, bf16[4,576,768]{2,1,0:T(8,128)(2,1)}, u32[]{:S(2)}) copy-start(bf16[4,576,768]{2,1,0:T(8,128)(2,1)} %get-tuple-element.80) | copy-start | bytes 10616836
  342.1 3.8 %copy-start.18 = (bf16[640,768]{1,0:T(8,128)(2,1)}, bf16[640,768]{1,0:T(8,128)(2,1)S(1)}, u32[]{:S(2)}) copy-start(bf16[640,768]{1,0:T(8,128)(2,1)S(1)} %collective-permute-done.1.refs_2_) | copy-start | bytes 2949124
  342.1 3.8 %collective-permute-start.2 = (bf16[640,768]{1,0:T(8,128)(2,1)S(1)}, bf16[640,768]{1,0:T(8,128)(2,1)S(1)}, u32[]{:S(2)}, u32[]{:S(2)}) collective-permute-start(bf16[640,768]{1,0:T(8,128)(2,1)S(1)} %collective-permute-done.1.refs_2_), channel_id=1, source_target_pairs={{0,1},{1,0},{2,3},{3,2},{4,5},{5,4},{6,7},{7,6},{8,9},{9,8},{10,11... | collective-permute-start | bytes 2949128 | tf_op jit(solution)/shard_map/ppermute | solution.py:1543
  345.8 1.0 copy-start.19

commit v6 on v5

--- a/solution.py
+++ b/solution.py
@@ -423,6 +423,76 @@
     ]
 
 
+class LateSum:
+    def __init__(self, dp_in, head_in, dp_send, dp_recv, head_send, head_recv):
+        self.dp_in, self.head_in = dp_in, head_in
+        self.dp_sems, self.head_sems = (dp_send, dp_recv), (head_send, head_recv)
+        self.me, *self.others = partners()
+        self.place, self.count = lax.axis_index("dp"), dp_in.shape[0]
+
+    def to_dp(self, shift):
+        block = self.dp_in.at[self.place]
+        other = lax.rem(self.place + shift, self.count)
+        return remote(block, block, *self.dp_sems, shift, "dp", other)
+
+    def to_head(self, lane):
+        block = self.head_in.at[self.me]
+        return remote(block, block, *self.head_sems, lane, "head", self.others[lane])
+
+    def start(self, rows):
+        lanes = self.dp_in.shape[2]
+        cuts = [
+            row[:, at:at + lanes] for row in rows for at in range(0, row.shape[1], lanes)
+        ]
+        cuts += [jnp.zeros_like(cuts[0])] * (self.dp_in.shape[1] - len(cuts))
+        self.dp_in[self.place] = jnp.concatenate(cuts, axis=0)
+
+        @pl.loop(1, self.count)
+        def _(shift):
+            self.to_dp(shift).start()
+
+    def across(self):
+        @pl.loop(1, self.count)
+        def _(shift):
+            self.to_dp(shift).wait_recv()
+
+        self.head_in[self.me] = lax.fori_loop(
+            1, self.count, lambda at, so_far: so_far + self.dp_in[at], self.dp_in[0]
+        )
+        for lane in range(3):
+            self.to_head(lane).start()
+
+    def result(self, out, first):
+        for lane in range(3):
+            self.to_head(lane).wait_recv()
+        total = self.head_in[0]
+        for head in range(1, self.head_in.shape[0]):
+            total = total + self.head_in[head]
+        lanes = total.shape[1]
+        cuts = out.shape[1] // lanes
+        for row in range(2):
+            for at in range(cuts):
+                piece = total[row * cuts + at:row * cuts + at + 1]
+                out[first + row:first + row + 1, at * lanes:(at + 1) * lanes] = piece
+
+    def finish(self):
+        for lane in range(3):
+            self.to_head(lane).wait_send()
+
+        @pl.loop(1, self.count)
+        def _(shift):
+            self.to_dp(shift).wait_send()
+
+
+def late_sum_scratch(width, dp_count):
+    block = (-(-2 * width // 128 // 8) * 8, 128)
+    return [
+        pltpu.VMEM((dp_count,) + block, FULL), pltpu.VMEM((4,) + block, FULL),
+        pltpu.SemaphoreType.DMA((dp_count,)), pltpu.SemaphoreType.DMA((dp_count,)),
+        pltpu.SemaphoreType.DMA((3,)), pltpu.SemaphoreType.DMA((3,)),
+    ]
+
+
 GATHER_CUTS = 4
 
 
@@ -461,8 +531,8 @@
         for cut in range(GATHER_CUTS):
             self.piece(1, cut).wait_recv()
 
-    def wait_far(self):
-        for cut in range(GATHER_CUTS):
+    def wait_far(self, first=0, last=GATHER_CUTS):
+        for cut in range(first, last):
             self.piece(0, cut).wait_recv()
             self.piece(2, cut).start()
 
@@ -803,10 +873,29 @@
 INSIDE = pl.BlockSpec(memory_space=pltpu.VMEM)
 
 
+def digits(values):
+    high = lax.div(values, 64)
+    return high.astype(FULL), (values - high * 64).astype(FULL)
+
+
+def turned_column(columns):
+    count = columns[0].shape[0]
+    lanes = lax.broadcasted_iota(jnp.int32, (count, 128), 1)
+    spread = jnp.zeros((count, 128), FULL)
+    for index, column in enumerate(columns):
+        for at, digit in enumerate(digits(column)):
+            spread = spread + jnp.where(lanes == 2 * index + at, digit, 0.0)
+    shape = (8, 128)
+    eye = lax.broadcasted_iota(jnp.int32, shape, 0) == lax.broadcasted_iota(jnp.int32, shape, 1)
+    rows = nt(one_hot(eye), spread.astype(LOW)).astype(jnp.int32)
+    return [rows[2 * at:2 * at + 1] * 64 + rows[2 * at + 1:2 * at + 2] for at in range(len(columns))]
+
+
 def prepare_kernel(
-    tile_ref, norm_ref, src_ref, col_ref, up_ref, x_in, g_in,
-    w_ref, xn_out, sent_out, up_out,
-    x_ref, g_ref, xn_ref, up_full, up_low, held, sent_sum, sent_ref,
+    slots, slot_count, capacity,
+    tile_ref, norm_ref, owner_ref, ids_ref, pos_ref, up_ref, x_in, g_in,
+    w_ref, src_ref, col_ref, col_back_ref, col_out_ref, xn_out, hat_out, sent_out, up_out,
+    x_ref, g_ref, xn_ref, hat_ref, up_full, up_low, held, sent_sum, sent_ref,
     load_sems, save_sems, *sems,
 ):
     images = x_ref.shape[0]
@@ -822,12 +911,15 @@
         )
 
     def save(image):
-        return pltpu.make_async_copy(xn_ref.at[image], xn_out.at[image], save_sems.at[image])
+        return (
+            pltpu.make_async_copy(xn_ref.at[image], xn_out.at[image], save_sems.at[0, image]),
+            pltpu.make_async_copy(hat_ref.at[image], hat_out.at[image], save_sems.at[1, image]),
+        )
 
     for image in range(images):
         for copy in load(image):
             copy.start()
-    me = lax.axis_index("dp")
+    me, head = lax.axis_index("dp"), lax.axis_index("head")
     held[me] = tile_ref[...].astype(LOW)
     greet(*gather.neighbours(), ("head", spread.near), ("head", spread.far))
     gather.start()
@@ -842,11 +934,27 @@
         for copy in load(image):
             copy.wait()
         normal, _ = normalise(x_ref[image].astype(FULL))
+        hat_ref[image] = normal.astype(LOW)
         xn_ref[image] = (normal * norm_ref[0:1, :] + norm_ref[1:2, :]).astype(LOW)
-        save(image).start()
-        slots = lax.broadcasted_iota(jnp.int32, shape, 0)
-        col = col_ref[image]
-        pick = one_hot((slots == col[0:1, :]) | (slots == col[1:2, :]))
+        for copy in save(image):
+            copy.start()
+
+        ids, pos = ids_ref[image], pos_ref[image]
+        kept = pos < capacity
+        holder, within = slots.holder(me, jnp.minimum(pos, capacity - 1))
+        sent_at = ids * slots.size(me, head) + within
+        sent_at = jnp.where(kept & (holder == head), sent_at, slots.count * slots.big)
+        shift = me - ids
+        shift = jnp.where(shift < 0, shift + slots.count, shift)
+        col_back_ref[image] = jnp.where(kept, slots.row(me, holder, shift) + within, -1)
+        other_pair = jnp.where(lax.div(holder, 2) == lax.div(head, 2), 0, 2)
+        apart = other_pair + jnp.where(lax.rem(holder, 2) == lax.rem(head, 2), 0, 1)
+        out_at = apart * (slots.count * slots.big) + shift * slots.size(me, holder) + within
+        col_out_ref[image] = jnp.where(kept, out_at, -1)
+        first, second = turned_column([sent_at[:, 0:1], sent_at[:, 1:2]])
+        col_ref[image] = jnp.concatenate([first, second], axis=0)
+        sent_slots = lax.broadcasted_iota(jnp.int32, shape, 0)
+        pick = one_hot((sent_slots == first) | (sent_slots == second))
         sent_sum[...] += nn(pick, g_ref[image])
 
     @pl.loop(0, max(steps, (images + 1) // 2))
@@ -859,18 +967,35 @@
         def _():
             gather.step(turn + 1)
 
+        @pl.when(turn == 1)
+        def _():
+            spread.wait_far(0, 1)
+
     sent_ref[...] = sent_sum[...].astype(LOW)
     save_sent = pltpu.make_async_copy(sent_ref, sent_out, load_sems.at[2, 1])
     save_sent.start()
+
+    rows = w_ref.shape[0]
+    tiles = owner_ref.shape[1]
+    row_tile = lax.div(lax.broadcasted_iota(jnp.int32, (rows, tiles), 0), TILE)
+    lane_tile = lax.broadcasted_iota(jnp.int32, (rows, tiles), 1)
+    owner_rows = jnp.broadcast_to(owner_ref[...].astype(FULL), (8, tiles)).astype(LOW)
+    owner = nt(one_hot(lane_tile == row_tile), owner_rows)[:, 0:1].astype(jnp.int32)
+    before = (owner_ref[...] == owner) & (lane_tile < row_tile)
+    rank = jnp.sum(jnp.where(before, 1.0, 0.0), axis=1, keepdims=True).astype(jnp.int32)
+    within = lax.rem(lax.broadcasted_iota(jnp.int32, (rows, 1), 0), TILE)
+    src = (owner * slot_count + rank) * TILE + within
+    src_ref[...] = turned_column([src])[0]
+    spread.wait_far(1, 3)
     gather.finish()
-    rows = w_ref.shape[0] // 4
     blocks, depth, width = held.shape
+    cut = rows // 4
     for part in range(4):
-        block = pl.ds(part * rows, rows)
-        lanes = lax.broadcasted_iota(jnp.int32, (rows, blocks * depth), 1)
-        pick = one_hot(lanes == src_ref[block, :])
-        w_ref[block, :] = nn(pick, held[...].reshape(blocks * depth, width)).astype(LOW)
-    spread.wait_far()
+        lanes = lax.broadcasted_iota(jnp.int32, (cut, blocks * depth), 1)
+        pick = one_hot(lanes == src[part * cut:(part + 1) * cut])
+        block = nn(pick, held[...].reshape(blocks * depth, width))
+        w_ref[pl.ds(part * cut, cut), :] = block.astype(LOW)
+    spread.wait_far(3)
     spread.wait_near()
     spread.wait_corner()
     spread.finish()
@@ -878,33 +1003,39 @@
 
     @pl.loop(0, images)
     def _(image):
-        save(image).wait()
-
-
-def prepare(tiles, patches, cotangent, norm_params, src_col, col_rows, up, slots, dp_count):
+        for copy in save(image):
+            copy.wait()
+
+
+def prepare(slots, tiles, patches, cotangent, norm_params, owners, ids, pos, up, weight_rows):
     images, _, width = patches.shape
-    line = dp_count // 2
+    slot_count = tiles.shape[0] // TILE
+    line = slots.count // 2
+    most = slots.count * slots.big
+    capacity = images * PATCH // slots.count
+    wide = jax.ShapeDtypeStruct(patches.shape, LOW)
+    pairs = jax.ShapeDtypeStruct((images, PATCH, 2), jnp.int32)
     return pl.pallas_call(
-        prepare_kernel,
-        in_specs=[INSIDE] * 4 + [ANYWHERE] * 3,
-        out_specs=[INSIDE] + [ANYWHERE] * 3,
+        functools.partial(prepare_kernel, slots, slot_count, capacity),
+        in_specs=[INSIDE] * 5 + [ANYWHERE] * 3,
+        out_specs=[INSIDE] * 5 + [ANYWHERE] * 4,
         out_shape=[
-            jax.ShapeDtypeStruct((src_col.shape[0], width), LOW),
-            jax.ShapeDtypeStruct(patches.shape, LOW),
-            jax.ShapeDtypeStruct((slots, width), LOW),
-            jax.ShapeDtypeStruct((4,) + up.shape, LOW),
+            jax.ShapeDtypeStruct((weight_rows, width), LOW),
+            jax.ShapeDtypeStruct((1, weight_rows), jnp.int32),
+            jax.ShapeDtypeStruct((images, 2, PATCH), jnp.int32), pairs, pairs, wide, wide,
+            jax.ShapeDtypeStruct((most, width), LOW), jax.ShapeDtypeStruct((4,) + up.shape, LOW),
         ],
-        scratch_shapes=[pltpu.VMEM(patches.shape, LOW)] * 3
+        scratch_shapes=[pltpu.VMEM(patches.shape, LOW)] * 4
         + [
             pltpu.VMEM(up.shape, FULL), pltpu.VMEM(up.shape, LOW),
-            pltpu.VMEM((dp_count,) + tiles.shape, LOW), pltpu.VMEM((slots, width), FULL),
-            pltpu.VMEM((slots, width), LOW),
-            pltpu.SemaphoreType.DMA((3, images)), pltpu.SemaphoreType.DMA((images,)),
+            pltpu.VMEM((slots.count,) + tiles.shape, LOW), pltpu.VMEM((most, width), FULL),
+            pltpu.VMEM((most, width), LOW),
+            pltpu.SemaphoreType.DMA((3, images)), pltpu.SemaphoreType.DMA((2, images)),
         ]
         + [pltpu.SemaphoreType.DMA((line,))] * 6 + image_gather_sems() + [pltpu.SemaphoreType.DMA],
         compiler_params=params(collective_id=0, has_side_effects=True),
         name="prepare",
-    )(tiles, norm_params, src_col, col_rows, up, patches, cotangent)
+    )(tiles, norm_params, owners, ids, pos, up, patches, cotangent)
 
 
 def head_mask(shape, axis, head):
@@ -1056,9 +1187,9 @@
 def backward_kernel(
     experts, slots,
     w_ref, lse_ref, src_ref, norm_ref, small_ref,
-    x1g_in, xn_in, q_in, qt_in, k_in, kt_in, v_in, ot_in, x_ref, out_rows_ref, down_part,
+    x1g_in, xn_in, hat_in, q_in, qt_in, k_in, kt_in, v_in, ot_in, x_ref, out_rows_ref, down_part,
     owned_ref, small_out, down_grad_ref, input_out, out_back,
-    x1g_ref, xn_ref, q_ref, qt_ref, k_ref, kt_ref, v_ref, ot_ref,
+    x1g_ref, xn_ref, hat_ref, q_ref, qt_ref, k_ref, kt_ref, v_ref, ot_ref, late_ref,
     grad_ref, own_ref, input_ref, padded_ref, load_sems, own_sem, *exchange,
 ):
     images = x1g_ref.shape[0]
@@ -1069,11 +1200,12 @@
     back_out = SlotReturn(slots, out_rows_ref, out_back, *exchange[10:14])
     weights_sum = LineScatter(padded_ref, owned_ref, *exchange[14:24])
     down_sum = BlockSum(down_part, *exchange[24:32])
-    small_sum = SmallSum(*exchange[32:])
+    small_sum = SmallSum(*exchange[32:40])
+    late_sum = LateSum(*exchange[40:])
     me, near, far, corner = partners()
     dp_count = slots.count
     streamed = (
-        (xn_in, xn_ref), (q_in, q_ref), (qt_in, qt_ref), (k_in, k_ref), (kt_in, kt_ref),
+        (xn_in, xn_ref), (hat_in, hat_ref), (q_in, q_ref), (qt_in, qt_ref), (k_in, k_ref), (kt_in, kt_ref),
         (v_in, v_ref), (ot_in, ot_ref),
     )
 
@@ -1084,7 +1216,7 @@
             for index, (source, target) in enumerate(streamed)
         ]
         copies.append(
-            pltpu.make_async_copy(x1g_in.at[image], x1g_ref.at[image], load_sems.at[7, slot])
+            pltpu.make_async_copy(x1g_in.at[image], x1g_ref.at[image], load_sems.at[8, slot])
         )
         return copies
 
@@ -1094,9 +1226,11 @@
     own = pltpu.make_async_copy(x_ref.at[me], own_ref, own_sem.at[0])
     own.start()
     greet_all((near, far, corner), dp_count)
+    small_sum.start(small_ref[...])
     down_sum.start()
     back_out.start()
     down_sum.across()
+    late_ref[...] = jnp.zeros_like(late_ref)
     shrink = HD ** (-0.5)
     grad_ref[...] = jnp.zeros_like(grad_ref)
 
@@ -1130,7 +1264,10 @@
             dv = dv_one if dv is None else dv + dv_one
         dqt = jnp.concatenate(dqt, axis=0).astype(LOW)
         dk, dv = dk.astype(LOW), dv.astype(LOW)
-        total_of.give(turn, tn(dqt, wq) + nn(dk, wk) + nn(dv, wv))
+        part = tn(dqt, wq) + nn(dk, wk) + nn(dv, wv)
+        total_of.give(turn, part)
+        late_ref[0:1, :] += jnp.sum(part * hat_ref[slot].astype(FULL), axis=0, keepdims=True)
+        late_ref[1:2, :] += jnp.sum(part, axis=0, keepdims=True)
         pieces = (nn(dqt, xn), tn(dk, xn), tn(dv, xn), nn(ot, x1g))
         for part, piece in enumerate(pieces):
             grad_ref[pl.ds(part * rows, rows), :] += piece
@@ -1140,15 +1277,11 @@
             for copy in load(turn + 2):
                 copy.start()
 
-    own.wait()
-    normal, scale = normalise(own_ref[...].astype(FULL))
-    back, gain_sum, shift_sum = norm_back(normal, scale, norm_ref[0:1, :], total_of.result())
-    input_ref[me] = (x1g_ref[me].astype(FULL) + back).astype(LOW)
-    spread.start()
-    small = small_ref[...]
-    row = lax.broadcasted_iota(jnp.int32, small.shape, 0)
-    small = small + jnp.where(row == experts, gain_sum, 0.0)
-    small_sum.start(small + jnp.where(row == experts + 1, shift_sum, 0.0))
+        @pl.when(turn == 1)
+        def _():
+            small_sum.across()
+
+    late_sum.start([late_ref[0:1, :], late_ref[1:2, :]])
     low = grad_ref[...].astype(LOW)
     depth = padded_ref.shape[1]
     parts = min(dp_count, 8)
@@ -1161,23 +1294,26 @@
             dp_count // parts, depth, block.shape[1]
         )
     weights_sum.start()
-    small_sum.across()
+    small_sum.back()
+    own.wait()
+    normal, scale = normalise(own_ref[...].astype(FULL))
+    back = norm_back(normal, scale, norm_ref[0:1, :], total_of.result())[0]
+    input_ref[me] = (x1g_ref[me].astype(FULL) + back).astype(LOW)
+    spread.start()
+    late_sum.across()
     steps = weights_sum.length
 
     @pl.loop(0, steps - 1)
     def _(turn):
         weights_sum.step(steps - 1 - turn)
 
-        @pl.when(turn == 0)
-        def _():
-            small_sum.back()
-
         @pl.when(turn == steps - 2)
         def _():
             spread.wait_far()
 
     weights_sum.result()
     small_sum.result(small_out)
+    late_sum.result(small_out, experts)
     down_grad_ref[...] = down_sum.result()
     spread.wait_near()
     spread.wait_corner()
@@ -1188,13 +1324,14 @@
     total_of.finish()
     weights_sum.finish()
     small_sum.finish()
+    late_sum.finish()
     down_sum.finish()
     keep.wait()
 
 
 def attention_backward(
     experts, slots, depth,
-    x1_grad, w, xn, saved, lse, src_row, norm_params, small, patches, out_rows, down_part,
+    x1_grad, w, xn, hat, saved, lse, src_row, norm_params, small, patches, out_rows, down_part,
 ):
     images, _, width = patches.shape
     rows = w.shape[0] // 4
@@ -1203,7 +1340,7 @@
     units = down_part.shape[1]
     return pl.pallas_call(
         functools.partial(backward_kernel, experts, slots),
-        in_specs=[INSIDE] * 5 + [ANYWHERE] * 11,
+        in_specs=[INSIDE] * 5 + [ANYWHERE] * 12,
         out_specs=[INSIDE] * 3 + [ANYWHERE] * 2,
         out_shape=[
             jax.ShapeDtypeStruct((depth, width), FULL), jax.ShapeDtypeStruct(small.shape, FULL),
@@ -1211,41 +1348,43 @@
             jax.ShapeDtypeStruct(patches.shape, LOW),
             jax.ShapeDtypeStruct((dp_count * slots.big, width), LOW),
         ],
-        scratch_shapes=[pltpu.VMEM(patches.shape, LOW), pltpu.VMEM((2, PATCH, width), LOW)]
+        scratch_shapes=[pltpu.VMEM(patches.shape, LOW)]
+        + [pltpu.VMEM((2, PATCH, width), LOW)] * 2
         + [pltpu.VMEM(shape, LOW) for shape in (flat, turned, flat, turned, flat, turned)]
         + [
-            pltpu.VMEM(w.shape, FULL), pltpu.VMEM((PATCH, width), LOW),
+            pltpu.VMEM((8, width), FULL), pltpu.VMEM(w.shape, FULL), pltpu.VMEM((PATCH, width), LOW),
             pltpu.VMEM(patches.shape, LOW), pltpu.VMEM((dp_count, depth, width), LOW),
-            pltpu.SemaphoreType.DMA((8, 2)), pltpu.SemaphoreType.DMA((2,)),
+            pltpu.SemaphoreType.DMA((9, 2)), pltpu.SemaphoreType.DMA((2,)),
         ]
         + image_sum_scratch(PATCH, width) + image_gather_sems()
         + slot_return_scratch(slots, width)
         + line_scatter_scratch(dp_count, depth, width)
         + block_sum_scratch(units, width)
-        + small_sum_scratch(small.shape[0], width, dp_count),
+        + small_sum_scratch(small.shape[0], width, dp_count)
+        + late_sum_scratch(width, dp_count),
         compiler_params=params(collective_id=2, has_side_effects=True),
         name="attention_backward",
     )(
-        w, lse, src_row, norm_params, small, x1_grad, xn, *saved, patches, out_rows, down_part,
+        w, lse, src_row, norm_params, small, x1_grad, xn, hat, *saved, patches, out_rows, down_part,
     )
 
 
-def picked_rows(slots, col, held_ref, phase):
-    start = phase * slots.phase_rows
-    lanes = lax.broadcasted_iota(jnp.int32, (col.shape[0], slots.phase_rows), 1) + start
+def picked_rows(col, held_ref, start, count):
+    lanes = lax.broadcasted_iota(jnp.int32, (col.shape[0], count), 1) + start
     pick = one_hot((lanes == col[:, 0:1]) | (lanes == col[:, 1:2]))
-    return nn(pick, held_ref[pl.ds(start, slots.phase_rows), :])
+    return nn(pick, held_ref[pl.ds(start, count), :])
 
 
 def combine_kernel(col_ref, x1_ref, *refs):
     *held, out_ref = refs
     total = x1_ref[0].astype(FULL)
     col = col_ref[0]
-    for part, rows_ref in enumerate(held):
-        count = rows_ref.shape[0]
+    count = 2 * held[0].shape[0]
+    for part in range(2):
         lanes = lax.broadcasted_iota(jnp.int32, (col.shape[0], count), 1) + part * count
         pick = one_hot((lanes == col[:, 0:1]) | (lanes == col[:, 1:2]))
-        total = total + nn(pick, rows_ref[...])
+        rows = jnp.concatenate([held[2 * part][...], held[2 * part + 1][...]], axis=0)
+        total = total + nn(pick, rows)
     out_ref[0] = total.astype(LOW)
 
 
@@ -1269,10 +1408,10 @@
 
 def expert_kernel(
     slots,
-    rows_ref, g_ref, router_ref, own_ref, closed_ref, col_ref, norm_ref,
+    rows_ref, g_ref, router_in, col_ref, norm_ref,
     up_in, down_in, x1_in, cot_in,
-    up_grad_ref, router_grad_ref, sums_ref, down_out, out_out, x1g_out,
-    up_ref, down_ref, og_ref, gate_ref, probs_ref, down_stage, out_ref, back_ref,
+    up_grad_ref, small_ref, down_out, out_out, x1g_out,
+    router_ref, up_ref, down_ref, og_ref, gate_ref, probs_ref, down_stage, out_ref, back_ref,
     held, total, x1_ref, cot_ref, x1g_ref,
     load_sems, save_sems, image_sems, out_sem, *exchange,
 ):
@@ -1299,11 +1438,16 @@
         for copy in load(turn):
             copy.start()
     rows = rows_ref[...]
-    logits = nt(rows, router_ref[...]) + closed_ref[...]
+    experts = router_in.shape[0]
+    router_ref[...] = jnp.zeros_like(router_ref)
+    router_ref[0:experts, :] = router_in[...]
+    lane = lax.broadcasted_iota(jnp.int32, (1, router_ref.shape[0]), 1)
+    mine = jnp.where(lane == lax.axis_index("dp"), 1.0, 0.0)
+    logits = nt(rows, router_ref[...].astype(LOW)) + jnp.where(lane < experts, 0.0, -1e30)
     top = jnp.max(logits, axis=-1, keepdims=True)
     weights = jnp.exp(logits - top)
     probs = weights / jnp.sum(weights, axis=-1, keepdims=True)
-    gate = jnp.sum(probs * own_ref[...], axis=-1, keepdims=True)
+    gate = jnp.sum(probs * mine, axis=-1, keepdims=True)
     probs_ref[...] = probs
     gate_ref[...] = gate
     og_ref[...] = (gate * g_ref[...].astype(FULL)).astype(LOW)
@@ -1346,14 +1490,15 @@
     out = out_sum[...].astype(LOW).astype(FULL)
     gate, probs = gate_ref[...], probs_ref[...]
     gate_grad = jnp.sum(g_ref[...].astype(FULL) * out, axis=-1, keepdims=True)
-    logit_grad = (gate_grad * (probs * (own_ref[...] - gate))).astype(LOW)
+    logit_grad = (gate_grad * (probs * (mine - gate))).astype(LOW)
     plain = back_sum[...].astype(LOW).astype(FULL)
-    back_ref[...] = (plain + nn(logit_grad, router_ref[...])).astype(LOW)
+    back_ref[...] = (plain + nn(logit_grad, router_ref[...].astype(LOW))).astype(LOW)
     back.start()
     out_ref[...] = (gate * out).astype(LOW)
     save_out = pltpu.make_async_copy(out_ref, out_out, out_sem)
     save_out.start()
-    router_grad_ref[...] = tn(logit_grad, rows_ref[...])
+    small_ref[...] = jnp.zeros_like(small_ref)
+    small_ref[0:experts, :] = tn(logit_grad, rows_ref[...])[0:experts]
 
     def image_load(image):
         slot = lax.rem(image, 2)
@@ -1370,30 +1515,30 @@
         for copy in image_load(image):
             copy.start()
     back.of_phase(0, back.relay)
-
-    @pl.loop(0, 4)
-    def _(phase):
+    total_rows = held.shape[0]
+    piece = 3 * 256
+    if total_rows % piece:
+        piece = slots.phase_rows
+    done = 0
+    for phase in range(4):
         back.of_phase(phase, back.forward)
-
-        @pl.when(phase < 3)
-        def _():
+        if phase < 3:
             back.of_phase(phase + 1, back.relay)
-
         back.of_phase(phase, back.rest)
-
-        @pl.loop(0, images)
-        def _(image):
-            part = picked_rows(slots, col_ref[image], held, phase)
-
-            @pl.when(phase == 0)
-            def _():
-                total[pl.ds(image * PATCH, PATCH)] = part
-
-            @pl.when(phase > 0)
-            def _():
-                total[pl.ds(image * PATCH, PATCH)] += part
-
-    sums_ref[...] = jnp.zeros_like(sums_ref)
+        ready = (phase + 1) * slots.phase_rows
+        while done + piece <= ready:
+            @pl.loop(0, images)
+            def _(image, start=done):
+                part = picked_rows(col_ref[image], held, start, piece)
+                span = pl.ds(image * PATCH, PATCH)
+                if start == 0:
+                    total[span] = part
+                else:
+                    total[span] += part
+
+            done += piece
+
+    back_scale = 1.0 / 4.0
 
     @pl.loop(0, images)
     def _(image):
@@ -1409,8 +1554,8 @@
         upstream = total[pl.ds(image * PATCH, PATCH)]
         result, gain_sum, shift_sum = norm_back(normal, scale, norm_ref[2:3, :], upstream)
         x1g_ref[slot] = (cot_ref[slot].astype(FULL) + result).astype(LOW)
-        sums_ref[0:1, :] += gain_sum
-        sums_ref[1:2, :] += shift_sum
+        small_ref[experts + 2:experts + 3, :] += gain_sum * back_scale
+        small_ref[experts + 3:experts + 4, :] += shift_sum * back_scale
         image_save(image).start()
 
         @pl.when(image + 2 < images)
@@ -1428,31 +1573,27 @@
         image_save(image).wait()
 
 
-def expert_stage(slots, rows, g_rows, up, down, router_low, own, col, x1, cotangent, norm_params):
+def expert_stage(slots, rows, g_rows, up, down, router, col, x1, cotangent, norm_params):
     count, width = rows.shape
     parts, _, units = up.shape
     images = x1.shape[0]
-    experts = router_low.shape[0]
+    small_rows = -(-(router.shape[0] + 4) // 16) * 16
     lanes = 128
-    router_wide = jnp.zeros((lanes, width), LOW).at[:experts].set(router_low)
-    lane = jnp.arange(lanes, dtype=jnp.int32)[None, :]
-    own_row = jnp.where(lane == own, 1.0, 0.0).astype(FULL)
-    closed = jnp.where(lane < experts, 0.0, -1e30).astype(FULL)
     flat = pltpu.VMEM((count, width), LOW)
     pair = pltpu.VMEM((2, PATCH, width), LOW)
     return pl.pallas_call(
         functools.partial(expert_kernel, slots),
-        in_specs=[INSIDE] * 7 + [ANYWHERE] * 4,
-        out_specs=[INSIDE] * 3 + [ANYWHERE] * 3,
+        in_specs=[INSIDE] * 5 + [ANYWHERE] * 4,
+        out_specs=[INSIDE] * 2 + [ANYWHERE] * 3,
         out_shape=[
             jax.ShapeDtypeStruct((width, units), FULL),
-            jax.ShapeDtypeStruct((lanes, width), FULL),
-            jax.ShapeDtypeStruct((8, width), FULL),
+            jax.ShapeDtypeStruct((small_rows, width), FULL),
             jax.ShapeDtypeStruct(down.shape, LOW),
             jax.ShapeDtypeStruct((count, width), LOW),
             jax.ShapeDtypeStruct(x1.shape, LOW),
         ],
         scratch_shapes=[
+            pltpu.VMEM((lanes, width), FULL),
             pltpu.VMEM((2,) + up.shape[1:], LOW), pltpu.VMEM((2,) + down.shape[1:], LOW), flat,
             pltpu.VMEM((count, 1), FULL), pltpu.VMEM((count, lanes), FULL),
             pltpu.VMEM((2, units, width), LOW), flat, flat,
@@ -1465,7 +1606,7 @@
         compiler_params=params(collective_id=3, has_side_effects=True),
         name="expert_stage",
     )(
-        rows, g_rows, router_wide, own_row, closed, col, norm_params, up, down, x1, cotangent,
+        rows, g_rows, router, col, norm_params, up, down, x1, cotangent,
     )
 
 
@@ -1482,59 +1623,27 @@
     capacity = tok_rows // experts
     dp_count = lax.axis_size("dp")
     head_count = lax.axis_size("head")
-    me_head = lax.axis_index("head")
-    me_dp = lax.axis_index("dp")
     images = tok_rows // PATCH
     slots = Slots(dp_count, capacity // head_count)
     slot_count = tile_master.shape[0]
 
-    owner_row = owners[0]
-    tile_count = owner_row.shape[0]
-    order_index = jnp.arange(tile_count, dtype=jnp.int32)
-    same_owner = owner_row[:, None] == owner_row[None, :]
-    earlier = order_index[None, :] < order_index[:, None]
-    tile_rank = jnp.sum(jnp.where(same_owner & earlier, 1, 0), axis=1).astype(jnp.int32)
-    tile_place = owner_row * slot_count + tile_rank
-    src = (tile_place[:, None] * TILE + jnp.arange(TILE, dtype=jnp.int32)[None, :]).reshape(-1)
-
-    ids, pos = expert_ids.T, slot_pos.T
-    kept = pos < capacity
-    holder, within = slots.holder(me_dp, jnp.minimum(pos, capacity - 1))
-    size = slots.size(me_dp, me_head)
-    col_rows = jnp.where(kept & (holder == me_head), ids * size + within, -1)
-    col_rows = col_rows.reshape(2, images, PATCH).transpose(1, 0, 2)
-    shift = (me_dp + dp_count - ids) % dp_count
-    col = jnp.where(kept, slots.row(me_dp, holder, shift) + within, -1)
-    col = col.T.reshape(images, PATCH, 2)
-    seen = lax.bitwise_xor(holder, me_head) * (dp_count * slots.big)
-    col_out = jnp.where(kept, seen + shift * slots.size(me_dp, holder) + within, -1)
-    col_out = col_out.T.reshape(images, PATCH, 2)
-
     by_image = (images, PATCH, width)
     x_images, g_images = patches.reshape(by_image), cotangent.reshape(by_image)
-    w, xn, g_sent, up_all = prepare(
-        tile_master.reshape(slot_count * TILE, width), x_images, g_images, norm_params,
-        src[:, None], col_rows, expert_up[0], slots.count * slots.big, dp_count,
+    pairs = (images, PATCH, 2)
+    w, src, col_rows, col, col_out, xn, hat, g_sent, up_all = prepare(
+        slots, tile_master.reshape(slot_count * TILE, width), x_images, g_images, norm_params,
+        owners, expert_ids.reshape(pairs), slot_pos.reshape(pairs), expert_up[0],
+        owners.shape[1] * TILE,
     )
     lse, *saved, x1, rows, g_rows, down_all = attention_forward(
         slots, xn, w, norm_params, col_rows, x_images, g_sent, expert_down[0]
     )
-    up_grad, router_part, second_sums, down_part, out, x1_grad = expert_stage(
-        slots, rows, g_rows, up_all, down_all, router.astype(LOW), me_dp, col, x1, g_images,
-        norm_params,
-    )
-
-    small_rows = -(-(experts + 4) // 16) * 16
-    small = jnp.concatenate(
-        [
-            router_part[:experts], jnp.zeros((2, width), FULL),
-            second_sums[:2] * (1.0 / head_count),
-            jnp.zeros((small_rows - experts - 4, width), FULL),
-        ]
+    up_grad, small, down_part, out, x1_grad = expert_stage(
+        slots, rows, g_rows, up_all, down_all, router, col, x1, g_images, norm_params
     )
     owned_grad, small, down_grad, input_low, out_back = attention_backward(
         experts, slots, slot_count * TILE,
-        x1_grad, w, xn, saved, lse, src[None, :], norm_params, small, x_images, out, down_part,
+        x1_grad, w, xn, hat, saved, lse, src, norm_params, small, x_images, out, down_part,
     )
     owned_grad = owned_grad.reshape(slot_count, TILE, width)
     input_grad = input_low.reshape(tok_rows, width).astype(FULL)

time: 370 us -> 340 us (0.919)
  Pallas kernels: 324 us -> 301 us
  other arithmetic: 26.7 us -> 19.9 us
    pallas_call x1, Pallas kernels: 111 us -> 87.2 us  [attention_backward(): pl.pallas_call(functools.partial(backward_kernel, experts, slots), in_spe...]
    convert_element_type x2 -> x0, other arithmetic: 5.26 us -> none  [the longest x1 4.52 us: body(): up_new.astype(LOW)]
    unnamed x40 -> x20, local copies, waits for them, and re-layouts: 1.27 us -> 6.26 us
    pallas_call x1, Pallas kernels: 76.5 us -> 81.2 us  [attention_forward(): pl.pallas_call(functools.partial(forward_kernel, slots), in_specs=[INSIDE...]
where the time goes in v6:
time: 340 us; the launch traced here: 335 us
  Pallas kernels  301 us (89%)
  other arithmetic  19.9 us (6%)
  local copies, waits for them, and re-layouts  6.87 us (2%)
  waiting for transfers between devices  5.34 us (2%)
    pallas_call x1, Pallas kernels, attention_backward(): pl.pallas_call(functools.partial(backward_kernel, experts, slots), in_spe...  87.2 us
    pallas_call x1, Pallas kernels, attention_forward(): pl.pallas_call(functools.partial(forward_kernel, slots), in_specs=[INSIDE...  81.2 us
    pallas_call x1, Pallas kernels, expert_stage(): pl.pallas_call(functools.partial(expert_kernel, slots), in_specs=[INSIDE]...  77.7 us
    pallas_call x1, Pallas kernels, prepare(): pl.pallas_call(functools.partial(prepare_kernel, slots, slot_count, capac...  41.5 us
    pallas_call x1, Pallas kernels, combine_forward(): pl.pallas_call(combine_kernel, grid=(images,), in_specs=[lead((1, PATCH,...  13.7 us
    convert_element_type x1, other arithmetic, body(): down_new.astype(LOW)  10.6 us
  transfers between devices with their start and end apart: 3, of which 1 were waited for; matrix products, arithmetic and copies ran while one was open for 6% of the time, Pallas kernels for 0%

profile of v6, /device:TPU:0, one launch (start us, length us, event | category | flops | bytes accessed | tf_op | source)
XLA Modules:
  0.0 334.5 jit_solution(10287779934215238525)
XLA Ops:
  0.7 2.1 copy.41
  2.8 2.1 copy.42
  4.9 41.5 %prepare.1 = (bf16[768,768]{1,0:T(8,128)(2,1)}, s32[1,768]{1,0:T(1,128)}, s32[4,2,576]{2,1,0:T(2,128)}, s32[4,576,2]{2,1,0:T(8,128)}, s32[4,576,2]{2,1,0:T(8,128...) custom-call(f32[192,768]{1,0:T(8,128)} %bitcast.43, ...), custom_call_target="tpu_custom_call" | custom-call | tf_op jit(solution)/shard_map/prepare/pallas_call | solution.py:1018
  46.5 81.2 %attention_forward.1 = (f32[4,8,576]{2,1,0:T(8,128)}, bf16[4,576,192]{2,1,0:T(8,128)(2,1)}, bf16[4,192,576]{2,1,0:T(8,128)(2,1)}, bf16[4,576,192]{2,1,0:T(8,128)...) custom-call(bf16[768,768]{1,0:T(8,128)(2,1)} %get-tuple-element.52.w, ...), custom_call_target="tpu_custom_call" | custom-call | tf_op jit(solution)/shard_map/attention_forward/pallas_call | solution.py:1165
  127.6 77.7 %expert_stage.1 = (f32[768,768]{1,0:T(8,128)}, f32[16,768]{1,0:T(8,128)}, bf16[4,768,768]{2,1,0:T(8,128)(2,1)}, bf16[576,768]{1,0:T(8,128)(2,1)}, bf16[4,576,768]{2,1,0:T(8,128)(2,1)}) custom-call(bf16[576,768]{1,0:T(8,128)(2,1)} %get-tuple-element.59.rows_ref, bf16[576,768]{1,0:T(8,128)(2,1)} %get-tuple-element.60.g_ref, f32[8,768]{1,0:T(8,128)} %router_in.1, ...), custom_call_target="tpu_custom_call" | custom-call | tf_op jit(solution)/shard_map/expert_stage/pallas_call | solution.py:1584
  205.3 0.0 copy-start.3
  205.3 0.0 copy-start.4
  205.4 0.0 copy-start.5
  205.4 0.0 copy-start.1
  205.4 87.2 %attention_backward.1 = (f32[192,768]{1,0:T(8,128)}, f32[16,768]{1,0:T(8,128)}, f32[768,768]{1,0:T(8,128)}, bf16[4,576,768]{2,1,0:T(8,128)(2,1)}, bf16[640,768]{1,0:T(8,128)(2,1)}) custom-call(bf16[768,768]{1,0:T(8,128)(2,1)} %get-tuple-element.52.w_ref, f32[4,8,576]{2,1,0:T(8,128)} %get-tuple-element.57.lse_ref, s32[1,768]{1,0:T(1,128)} %get-tuple-element.58.src_ref, ...), custom_call_target="tpu_custom_call" | custom-call | tf_op jit(solution)/shard_map/attention_backward/pallas_call | solution.py:1341
  292.6 0.0 copy-start
  292.6 0.1 collective-permute-start.1
  292.7 0.1 collective-permute-start
  292.8 1.5 multiply_subtract_fusion.4
  294.3 0.6 fusion.17
  294.9 1.4 multiply_subtract_fusion.3
  296.4 0.0 copy-done.3
  296.4 0.0 copy-done.4
  296.4 0.0 copy-done.5
  296.4 2.6 fusion.14
  299.0 0.0 copy-done.1
  299.0 0.0 copy-done
  299.0 10.6 %fusion.10 = (bf16[1,768,768]{2,1,0:T(8,128)(2,1)}, f32[1,768,768]{2,1,0:T(8,128)}, f32[1,768,768]{2,1,0:T(8,128)}, f32[1,768,768]{2,1,0:T(8,128)}, bf16[1,768,7...) fusion(f32[1,768,768]{2,1,0:T(8,128)S(1)} %copy-done.1, ...), kind=kLoop, calls=%fused_computation.24 | loop fusion | flops 18874368 | bytes 35389440 | tf_op jit(solution)/shard_map/convert_element_type | solution.py:1689
  309.6 5.3 %collective-permute-done.1.refs_2_ = bf16[640,768]{1,0:T(8,128)(2,1)S(1)} collective-permute-done((bf16[640,768]{1,0:T(8,128)(2,1)}, bf16[640,768]{1,0:T(8,128)(2,1)S(1)}, u32[]{:S(2)}, u32[]{:S(2)}) %collective-permute-start.1) | collective-permute-done | bytes 983072 | tf_op jit(solution)/shard_map/ppermute | solution.py:1652
  314.9 0.0 collective-permute-start.2
  314.9 0.0 copy-done.2
  314.9 3.7 %bitcast_convert_fusion = f32[2304,768]{1,0:T(8,128)} fusion(bf16[4,576,768]{2,1,0:T(8,128)(2,1)S(1)} %copy-done.2), kind=kLoop, calls=%fused_computation | loop fusion | flops 1769472 | bytes 10616832 | tf_op jit(solution)/shard_map/convert_element_type | solution.py:1649
  318.7 0.0 collective-permute-done.refs_1_
  318.7 0.0 collective-permute-done.2.refs_3_
  318.7 0.9 copy-done.7
  319.6 1.0 copy-done.8
  320.6 13.7 %combine_forward.1 = bf16[4,576,768]{2,1,0:T(8,128)(2,1)} custom-call(s32[4,576,2]{2,1,0:T(8,128)} %get-tuple-element.51.col_ref, bf16[4,576,768]{2,1,0:T(8,128)(2,1)} %get-tuple-element.56.x1_in.x1_ref, bf16[640,768]{1,0:T(8,128)(2,1)} %get-tuple-element.75.refs_0_, bf16[640,768]{1,0:T(8,128)(2,1)} %copy-done.7, bf16[640,768]{1,0:T(8,128)(2,1)} %copy-done.6, ...), custom_call_target="tpu_custom_call" | custom-call | flops 9059696640 | bytes 11010048 | tf_op jit(solution)/shard_map/combine_forward/pallas_call | solution.py:1394
  (5 shorter events, 0.0 us)
Async XLA Ops:
  205.3 91.0 %copy-start.3 = (f32[24,8,768]{2,1,0:T(8,128)S(1)}, f32[24,8,768]{2,1,0:T(8,128)}, u32[]{:S(2)}) copy-start(f32[24,8,768]{2,1,0:T(8,128)} %param.25) | copy-start | bytes 1769476
  205.3 91.0 %copy-start.4 = (f32[24,8,768]{2,1,0:T(8,128)S(1)}, f32[24,8,768]{2,1,0:T(8,128)}, u32[]{:S(2)}) copy-start(f32[24,8,768]{2,1,0:T(8,128)} %param.26) | copy-start | bytes 1769476
  205.4 91.0 %copy-start.5 = (f32[24,8,768]{2,1,0:T(8,128)S(1)}, f32[24,8,768]{2,1,0:T(8,128)}, u32[]{:S(2)}) copy-start(f32[24,8,768]{2,1,0:T(8,128)} %param.27) | copy-start | bytes 1769476
  205.4 93.6 %copy-start.1 = (f32[1,768,768]{2,1,0:T(8,128)S(1)}, f32[1,768,768]{2,1,0:T(8,128)}, u32[]{:S(2)}) copy-start(f32[1,768,768]{2,1,0:T(8,128)} %param.31) | copy-start | bytes 7077892
  292.6 6.4 %copy-start = (f32[1,768,768]{2,1,0:T(8,128)S(1)}, f32[1,768,768]{2,1,0:T(8,128)}, u32[]{:S(2)}) copy-start(f32[1,768,768]{2,1,0:T(8,128)} %param.28) | copy-start | bytes 7077892
  292.6 22.3 %collective-permute-start.1 = (bf16[640,768]{1,0:T(8,128)(2,1)}, bf16[640,768]{1,0:T(8,128)(2,1)S(1)}, u32[]{:S(2)}, u32[]{:S(2)}) collective-permute-start(bf16[640,768]{1,0:T(8,128)(2,1)} %get-tuple-element.75.refs_0_), channel_id=1, source_target_pairs={{0,2},{1,3},{2,0},{3,1},{4,6},{5,7},{6,4},{7,5},{8,10},{9,11},{10,... | collective-permute-start | bytes 2949128 | tf_op jit(solution)/shard_map/ppermute | solution.py:1652
  292.7 26.0 %collective-permute-start = (bf16[640,768]{1,0:T(8,128)(2,1)}, bf16[640,768]{1,0:T(8,128)(2,1)S(1)}, u32[]{:S(2)}, u32[]{:S(2)}) collective-permute-start(bf16[640,768]{1,0:T(8,128)(2,1)} %get-tuple-element.75.refs_0_), channel_id=1, source_target_pairs={{0,1},{1,0},{2,3},{3,2},{4,5},{5,4},{6,7},{7,6},{8,9},{9,8},{10,11... | collective-permute-start | bytes 2949128 | tf_op jit(solution)/shard_map/ppermute | solution.py:1652
  299.0 15.9 %copy-start.2 = (bf16[4,576,768]{2,1,0:T(8,128)(2,1)S(1)}, bf16[4,576,768]{2,1,0:T(8,128)(2,1)}, u32[]{:S(2)}) copy-start(bf16[4,576,768]{2,1,0:T(8,128)(2,1)} %get-tuple-element.76) | copy-start | bytes 10616836
  314.9 3.8 %copy-start.6 = (bf16[640,768]{1,0:T(8,128)(2,1)}, bf16[640,768]{1,0:T(8,128)(2,1)S(1)}, u32[]{:S(2)}) copy-start(bf16[640,768]{1,0:T(8,128)(2,1)S(1)} %collective-permute-done.1.refs_2_) | copy-start | bytes 2949124
  314.9 3.8 %collective-permute-start.2 = (bf16[640,768]{1,0:T(8,128)(2,1)S(1)}, bf16[640,768]{1,0:T(8,128)(2,1)S(1)}, u32[]{:S(2)}, u32[]{:S(2)}) collective-permute-start(bf16[640,768]{1,0:T(8,128)(2,1)S(1)} %collective-permute-done.1.refs_2_), channel_id=1, source_target_pairs={{0,1},{1,0},{2,3},{3,2},{4,5},{5,4},{6,7},{7,6},{8,9},{9,8},{10,11... | collective-permute-start | bytes 2949128 | tf_op jit(solution)/shard_map/ppermute | solution.py:1652
  318.7 1.0 copy-start.7
  319.6 1.0 copy-start.8
